TPU v7x, 512 devices: a whole 4x4x16 slice. The times are simulated.
512 devices in a mesh: dp: 32 (over z, y_lo), seq: 16 (over y_hi, x, core).
Axes of the slice: x: 4, y: 4 (y_hi: 2, y_lo: 2; y = y_hi * 2 + y_lo), z: 16, core: 2. Of those that a mesh axis runs over, the one named last changes fastest.
Arguments:
- normed_layer_input: bfloat16 [32, 2560, 4096], P('dp', 'seq'), may hold values from -6 to 6
- queries: bfloat16 [32, 2560, 2048], P('dp', 'seq'), may hold values from -8 to 8
- keys: bfloat16 [32, 2560, 2048], P('dp', 'seq'), may hold values from -8 to 8
- values: bfloat16 [32, 2560, 2048], P('dp', 'seq'), may hold values from -6 to 6
- output_gradient: bfloat16 [32, 2560, 2048], P('dp', 'seq'), may hold values from -0.59765625 to 0.59765625
- adapter_down_weight: bfloat16 [4096, 96], replicated, may hold values from -0.09375 to 0.09375
- adapter_up_weight: bfloat16 [32, 6144], replicated, may hold values from -1 to 1
- head_order: int32 [16], replicated, may hold values from 0 to 15, each once
Outputs:
- lora_down_grad: bfloat16 [4096, 96], P(('dp', 'seq'))
- lora_up_grad: bfloat16 [32, 6144], P(None, ('dp', 'seq'))
Inputs may be any that keep to these rules, and one draw needn't show every extreme that they name: `head_order`: every head number appears exactly once.
All inputs are finite; a program needn't handle non-finite values.
Results may differ from a plain program's by a relative error of at most 0.017.
Values may be sent and summed in bfloat16 or wider, within the bound.
No kernel may reach another device: no remote copies, remote signals or barrier semaphores. Data moves between devices by JAX's collectives and lax.ppermute only.
A program may use at most 64 MiB of HBM per device.

v0:
```python
import jax
import jax.numpy as jnp
from jax import lax
from jax.sharding import PartitionSpec as P

HEAD_SIZE = 128


ADAPTER_SCALE = 0.25


def from_behind(value, axis, steps):
    count = lax.axis_size(axis)
    pairs = [(source, (source + steps) % count) for source in range(count)]
    return lax.ppermute(value, axis, pairs)


def attend(query, key_in, value, cotangent):
    scale = HEAD_SIZE ** (-0.5)
    size = query.shape[0]
    causal = jnp.arange(size)[:, None] >= jnp.arange(size)[None, :]
    scores = jnp.einsum("qhd,khd->hqk", query, key_in, preferred_element_type=jnp.float32) * scale
    scores = jnp.where(causal, scores, -jnp.inf)
    probs = jax.nn.softmax(scores, axis=-1)
    weights = probs.astype(jnp.bfloat16)
    output = jnp.einsum("hqk,khd->qhd", weights, value, preferred_element_type=jnp.float32)
    delta = jnp.sum(cotangent.astype(jnp.float32) * output, axis=-1)
    dvalue = jnp.einsum(
        "hqk,qhd->khd", weights, cotangent, preferred_element_type=jnp.float32
    ).astype(jnp.bfloat16)
    dprob = jnp.einsum("qhd,khd->hqk", cotangent, value, preferred_element_type=jnp.float32)
    dscore = (probs * (dprob - delta.T[:, :, None])).astype(jnp.bfloat16)
    dquery = (
        jnp.einsum("hqk,khd->qhd", dscore, key_in, preferred_element_type=jnp.float32) * scale
    ).astype(jnp.bfloat16)
    dkey = (
        jnp.einsum("hqk,qhd->khd", dscore, query, preferred_element_type=jnp.float32) * scale
    ).astype(jnp.bfloat16)
    return (dquery, dkey, dvalue)


def contract_last(left, right):
    return lax.dot_general(
        left, right, (((1,), (1,)), ((), ())), preferred_element_type=jnp.float32
    )


def contract_first(left, right):
    return lax.dot_general(
        left, right, (((0,), (0,)), ((), ())), preferred_element_type=jnp.float32
    )


def per_device(
    normed_layer_input,
    queries,
    keys,
    values,
    output_gradient,
    adapter_down_weight,
    adapter_up_weight,
    head_order,
):
    input_arrays = normed_layer_input[0]
    row_count = input_arrays.shape[0]
    half_rows = row_count // 2
    output_width = queries.shape[2]
    head_count = output_width // HEAD_SIZE
    half_heads = head_count // 2
    adapter_rank = adapter_down_weight.shape[1] // 3
    reduced_rank_term = jnp.dot(
        input_arrays, adapter_down_weight, preferred_element_type=jnp.float32
    ).astype(jnp.bfloat16)
    selector = (head_order[:, None] == jnp.arange(head_count, dtype=jnp.int32)[None, :]).astype(
        jnp.bfloat16
    )

    def permute(array):
        return jnp.einsum(
            "ph,shd->spd", selector, array, preferred_element_type=jnp.float32
        ).astype(jnp.bfloat16)

    def restore(array):
        return jnp.einsum(
            "ph,spd->shd", selector, array, preferred_element_type=jnp.float32
        ).astype(jnp.bfloat16)

    ordered = [
        permute(item[0].reshape(row_count, head_count, HEAD_SIZE))
        for item in (queries, keys, values, output_gradient)
    ]
    shift_parts = [item[:, :half_heads] for item in ordered]
    plain_parts = [item[:, half_heads:] for item in ordered]
    plain_grads = attend(*plain_parts)

    def assemble(plain_piece, shift_piece):
        joined = jnp.concatenate([shift_piece, plain_piece], axis=1)
        return restore(joined).reshape(shift_piece.shape[0], output_width)

    forward_rows = from_behind(
        (
            shift_parts[0][:half_rows],
            shift_parts[1][:half_rows],
            shift_parts[2][:half_rows],
            shift_parts[3][:half_rows],
        ),
        "seq",
        -1,
    )
    grouped = [
        jnp.concatenate([own[half_rows:], other], axis=0)
        for own, other in zip(shift_parts, forward_rows)
    ]
    shift_grads = attend(*grouped)
    returned = from_behind(
        (shift_grads[0][half_rows:], shift_grads[1][half_rows:], shift_grads[2][half_rows:]),
        "seq",
        1,
    )
    stacked_weight = jnp.concatenate(
        [
            assemble(plain_piece, jnp.concatenate([back_piece, group_piece[:half_rows]], axis=0))
            for plain_piece, back_piece, group_piece in zip(plain_grads, returned, shift_grads)
        ],
        axis=1,
    )
    projection_kind = jnp.concatenate(
        [
            contract_last(
                stacked_weight[
                    :, projection_index * output_width : (projection_index + 1) * output_width
                ],
                adapter_up_weight[
                    :, projection_index * output_width : (projection_index + 1) * output_width
                ],
            )
            for projection_index in range(3)
        ],
        axis=1,
    ).astype(jnp.bfloat16)
    up_local = jnp.concatenate(
        [
            contract_first(
                stacked_weight[
                    :, projection_index * output_width : (projection_index + 1) * output_width
                ],
                reduced_rank_term[
                    :, projection_index * adapter_rank : (projection_index + 1) * adapter_rank
                ],
            )
            for projection_index in range(3)
        ],
        axis=0,
    )
    down_local = contract_first(input_arrays, projection_kind)
    down_projection_sum, up_weight_rows = (
        lax.psum_scatter(down_local, ("dp", "seq"), scatter_dimension=0, tiled=True),
        lax.psum_scatter(up_local, ("dp", "seq"), scatter_dimension=0, tiled=True),
    )
    return (
        (ADAPTER_SCALE * down_projection_sum).astype(jnp.bfloat16),
        (ADAPTER_SCALE * up_weight_rows.T).astype(jnp.bfloat16),
    )


def solution(mesh):
    in_specs = (
        P("dp", "seq", None),
        P("dp", "seq", None),
        P("dp", "seq", None),
        P("dp", "seq", None),
        P("dp", "seq", None),
        P(),
        P(),
        P(),
    )
    out_specs = (P(("dp", "seq"), None), P(None, ("dp", "seq")))
    return jax.shard_map(
        per_device, mesh=mesh, in_specs=in_specs, out_specs=out_specs, check_vma=False
    )
```

profile of v0, /device:TPU:4, one launch (start us, length us, event | category | flops | bytes accessed | tf_op | source)
XLA Modules:
  0.0 559.8 jit_solution(116615509929649786)
XLA Ops:
  7.2 0.0 all-reduce.5.cloned.1.call-start
  7.2 1.3 copy.88
  8.6 0.4 fusion.16
  9.0 0.7 fusion.126
  9.7 1.9 collective-permute-start.1
  11.6 0.1 copy.87
  11.8 0.4 fusion.15
  12.2 0.8 fusion.127
  13.0 2.5 collective-permute-start
  15.5 0.1 copy.90
  15.7 0.4 fusion.18
  16.0 0.8 fusion.124
  16.8 1.9 collective-permute-start.3
  18.7 0.1 copy.89
  18.9 0.4 fusion.17
  19.3 0.7 fusion.125
  19.9 7.9 %collective-permute-start.2 = (bf16[80,8,128]{2,1,0:T(8,128)(2,1)}, bf16[80,8,128]{2,1,0:T(8,128)(2,1)}, u32[]{:S(2)}, u32[]{:S(2)}) collective-permute-start(bf16[80,8,128]{2,1,0:T(8,128)(2,1)} %get-tuple-element.11), channel_id=1, source_target_pairs={{0,15},{1,0},{2,1},{3,2},{4,3},{5,4},{6,5},{7,6},{8,7},{9,8},{10,9... | collective-permute-start | bytes 491528 | tf_op jit(solution)/shard_map/ppermute | solution.py:15
  28.0 1.6 fusion.131
  29.7 1.4 fusion.53
  31.1 0.3 fusion.24
  31.4 0.4 fusion.54
  31.9 1.1 fusion.41
  33.0 0.9 copy.61
  33.9 1.7 fusion.10
  35.7 1.0 fusion.25
  36.7 0.1 copy-done.1
  36.8 0.5 fusion.29
  37.3 0.5 fusion.27
  37.8 0.9 pad_maximum_fusion.5
  38.8 1.1 pad_maximum_fusion.4
  39.8 1.6 fusion.136
  41.5 1.4 fusion.52
  42.9 1.0 pad_maximum_fusion.6
  43.9 0.3 fusion.23
  44.3 0.9 pad_maximum_fusion.7
  45.2 0.4 fusion.65
  45.6 2.0 fusion.42
  47.7 0.9 copy.50
  48.6 1.7 fusion.11
  50.4 0.3 fusion.26
  50.7 0.5 fusion.28
  51.2 2.1 collective-permute-start.6
  53.3 1.9 collective-permute-start.5
  55.2 1.9 collective-permute-start.4
  57.2 2.7 collective-permute-done.5
  60.0 0.3 convolution_convert_fusion.1
  60.3 0.1 pad_maximum_fusion.3
  60.4 0.3 convolution_convert_fusion
  60.7 0.6 copy-done.14
  61.3 0.3 convolution_convert_fusion.9
  61.6 0.3 fusion.32
  62.0 0.3 fusion.35
  62.3 0.3 convolution_convert_fusion.10
  62.7 0.1 pad_maximum_fusion.1
  62.7 0.3 convolution_convert_fusion.2
  63.1 0.3 convolution_convert_fusion.11
  63.4 0.3 fusion.38
  63.6 0.9 pad_maximum_fusion
  64.6 1.6 convolution_bitcast_fusion
  66.2 483.7 %all-reduce.5.cloned.1.call-done = (f32[4096,96]{0,1:T(8,128)}, f32[6144,32]{0,1:T(8,128)}) async-done(((f32[4096,96]{0,1:T(8,128)}, f32[6144,32]{0,1:T(8,128)}), (f32[4096,96]{0,1:T(8,128)}, f32[6144,32]{0,1:T(8,128)})) %all-reduce.5.cloned.1.call-update) | async-done | bytes 2359312
  549.9 0.9 fusion.83
  550.8 0.7 copy.68
  551.5 0.8 fusion.93
  552.3 0.7 copy.69
  (44 shorter events, 0.3 us)
Async XLA Ops:
  7.2 29.6 %copy-start = (bf16[1,160,4096]{2,1,0:T(8,128)(2,1)S(1)}, bf16[1,160,4096]{2,1,0:T(8,128)(2,1)}, u32[]{:S(2)}) copy-start(bf16[1,160,4096]{2,1,0:T(8,128)(2,1)} %param.8) | copy-start | bytes 3932164
  7.2 1.4 copy-start.13
  7.2 542.7 %all-reduce.5.cloned.1.call-start = ((), (), s32[]{:S(2)}) async-start(), calls=%async_computation | async-start | bytes 4718592
  8.6 3.1 copy-start.5
  9.7 28.1 %collective-permute-start.1 = (bf16[80,8,128]{2,1,0:T(8,128)(2,1)}, bf16[80,8,128]{2,1,0:T(8,128)(2,1)}, u32[]{:S(2)}, u32[]{:S(2)}) collective-permute-start(bf16[80,8,128]{2,1,0:T(8,128)(2,1)} %get-tuple-element.13), channel_id=1, source_target_pairs={{0,15},{1,0},{2,1},{3,2},{4,3},{5,4},{6,5},{7,6},{8,7},{9,8},{10,9... | collective-permute-start | bytes 491528 | tf_op jit(solution)/shard_map/ppermute | solution.py:15
  11.8 3.7 copy-start.6
  13.0 25.8 %collective-permute-start = (bf16[80,8,128]{2,1,0:T(8,128)(2,1)}, bf16[80,8,128]{2,1,0:T(8,128)(2,1)}, u32[]{:S(2)}, u32[]{:S(2)}) collective-permute-start(bf16[80,8,128]{2,1,0:T(8,128)(2,1)} %get-tuple-element.15), channel_id=1, source_target_pairs={{0,15},{1,0},{2,1},{3,2},{4,3},{5,4},{6,5},{7,6},{8,7},{9,8},{10,9... | collective-permute-start | bytes 491528 | tf_op jit(solution)/shard_map/ppermute | solution.py:15
  15.6 3.1 copy-start.7
  16.8 27.4 %collective-permute-start.3 = (bf16[80,8,128]{2,1,0:T(8,128)(2,1)}, bf16[80,8,128]{2,1,0:T(8,128)(2,1)}, u32[]{:S(2)}, u32[]{:S(2)}) collective-permute-start(bf16[80,8,128]{2,1,0:T(8,128)(2,1)} %get-tuple-element.9), channel_id=1, source_target_pairs={{0,15},{1,0},{2,1},{3,2},{4,3},{5,4},{6,5},{7,6},{8,7},{9,8},{10,9... | collective-permute-start | bytes 491528 | tf_op jit(solution)/shard_map/ppermute | solution.py:15
  19.9 23.0 %collective-permute-start.2 = (bf16[80,8,128]{2,1,0:T(8,128)(2,1)}, bf16[80,8,128]{2,1,0:T(8,128)(2,1)}, u32[]{:S(2)}, u32[]{:S(2)}) collective-permute-start(bf16[80,8,128]{2,1,0:T(8,128)(2,1)} %get-tuple-element.11), channel_id=1, source_target_pairs={{0,15},{1,0},{2,1},{3,2},{4,3},{5,4},{6,5},{7,6},{8,7},{9,8},{10,9... | collective-permute-start | bytes 491528 | tf_op jit(solution)/shard_map/ppermute | solution.py:15
  27.9 1.8 copy-start.11
  33.9 1.7 copy-start.12
  35.7 1.1 copy-start.1
  36.8 1.0 copy-start.3
  37.3 1.5 copy-start.4
  38.7 2.7 copy-start.9
  42.9 1.3 copy-start.2
  48.6 1.7 copy-start.10
  51.1 8.8 %copy-start.8 = (bf16[160,8,128]{2,0,1:T(8,128)(2,1)S(1)}, bf16[160,8,128]{2,0,1:T(8,128)(2,1)}, u32[]{:S(2)}) copy-start(bf16[160,8,128]{2,0,1:T(8,128)(2,1)} %fusion.25) | copy-start | bytes 983044
  51.2 9.1 %collective-permute-start.6 = (bf16[80,8,128]{2,0,1:T(8,128)(2,1)S(1)}, bf16[80,8,128]{2,0,1:T(8,128)(2,1)S(1)}, u32[]{:S(2)}, u32[]{:S(2)}) collective-permute-start(bf16[80,8,128]{2,0,1:T(8,128)(2,1)S(1)} %get-tuple-element.20), channel_id=1, source_target_pairs={{0,1},{1,2},{2,3},{3,4},{4,5},{5,6},{6,7},{7,8},{8,9},{9,10},{10,1... | collective-permute-start | bytes 491528 | tf_op jit(solution)/shard_map/ppermute | solution.py:15
  53.3 6.6 %collective-permute-start.5 = (bf16[80,8,128]{2,0,1:T(8,128)(2,1)S(1)}, bf16[80,8,128]{2,0,1:T(8,128)(2,1)S(1)}, u32[]{:S(2)}, u32[]{:S(2)}) collective-permute-start(bf16[80,8,128]{2,0,1:T(8,128)(2,1)S(1)} %get-tuple-element.18), channel_id=1, source_target_pairs={{0,1},{1,2},{2,3},{3,4},{4,5},{5,6},{6,7},{7,8},{8,9},{9,10},{10,1... | collective-permute-start | bytes 491528 | tf_op jit(solution)/shard_map/ppermute | solution.py:15
  55.2 7.4 %collective-permute-start.4 = (bf16[80,8,128]{2,0,1:T(8,128)(2,1)S(1)}, bf16[80,8,128]{2,0,1:T(8,128)(2,1)S(1)}, u32[]{:S(2)}, u32[]{:S(2)}) collective-permute-start(bf16[80,8,128]{2,0,1:T(8,128)(2,1)S(1)} %get-tuple-element.16), channel_id=1, source_target_pairs={{0,1},{1,2},{2,3},{3,4},{4,5},{5,6},{6,7},{7,8},{8,9},{9,10},{10,1... | collective-permute-start | bytes 491528 | tf_op jit(solution)/shard_map/ppermute | solution.py:15
  60.3 1.0 copy-start.14
Sparse Core Ops, SparseCore 0:
  66.4 483.5 all-reduce.4
where the time goes:
time: 561 us; the launch traced here: 560 us
  waiting for transfers between devices  486 us (87%)
  starting transfers between devices  20.2 us (4%)
  matrix products  17.1 us (3%)
  between operations  14.6 us (3%)
  other arithmetic  12.7 us (2%)
  local copies, waits for them, and re-layouts  8.79 us (2%)
    unnamed x2, waiting for transfers between devices  484 us
    ppermute x7, starting transfers between devices, from_behind(): return lax.ppermute(value, axis, pairs)  20.2 us
  transfers between devices with their start and end apart: 8, of which 2 were waited for; matrix products, arithmetic and copies ran while one was open for 4% of the time, Pallas kernels for 0%

commit v1 on v0

v1 whole, which is shorter than its diff:
```python
import jax
import jax.numpy as jnp
from jax import lax
from jax.experimental import pallas as pl
from jax.experimental.pallas import tpu as pltpu
from jax.sharding import Mesh
from jax.sharding import PartitionSpec as P

HEAD = 128
ROWS = 160
HALF = 80
HEADS = 16
SHIFTED = 8
WIDTH = HEADS * HEAD
MODEL = 4096
RANK = 32
SCALE = HEAD ** -0.5
ADAPTER_SCALE = 0.25
Z, G, C = 16, 16, 2
PART = Z * 8 + 16

BF16, F32 = jnp.bfloat16, jnp.float32
VMEM = pl.BlockSpec(memory_space=pltpu.VMEM)
SMEM = pl.BlockSpec(memory_space=pltpu.SMEM)


def call(body, name, out_shape, in_specs, flops, size, limit=32, **rest):
    return pl.pallas_call(
        body,
        name=name,
        out_shape=out_shape,
        in_specs=in_specs,
        out_specs=jax.tree.map(lambda _: VMEM, out_shape),
        compiler_params=pltpu.CompilerParams(vmem_limit_bytes=limit * 1024 * 1024),
        cost_estimate=pl.CostEstimate(flops=flops, bytes_accessed=size, transcendentals=0),
        **rest,
    )


def dot(left, right):
    return jnp.dot(left, right, preferred_element_type=F32)


def dot_last(left, right):
    return lax.dot_general(left, right, (((1,), (1,)), ((), ())), preferred_element_type=F32)


def dot_first(left, right):
    return lax.dot_general(left, right, (((0,), (0,)), ((), ())), preferred_element_type=F32)


def attend(query, key, value, cotangent, allowed):
    scores = jnp.where(allowed, dot_last(key, query), -jnp.inf)
    top = jnp.max(scores, axis=0, keepdims=True)
    powers = jnp.exp((scores - top) * SCALE)
    probs = powers / jnp.sum(powers, axis=0, keepdims=True)
    weights = probs.astype(BF16)
    dprob = dot_last(value, cotangent)
    delta = jnp.sum(weights.astype(F32) * dprob, axis=0, keepdims=True)
    dscore = (probs * (dprob - delta)).astype(BF16)
    dquery = (dot_first(dscore, key) * SCALE).astype(BF16)
    dkey = (dot(dscore, query) * SCALE).astype(BF16)
    dvalue = dot(weights, cotangent).astype(BF16)
    return dquery, dkey, dvalue


def causal(keys, queries, ahead):
    row = lax.broadcasted_iota(jnp.int32, (keys, queries), 0)
    column = lax.broadcasted_iota(jnp.int32, (keys, queries), 1)
    return row <= column + ahead


def lanes_of(order_ref, slot, block=0):
    return pl.ds(pl.multiple_of(order_ref[slot] * HEAD + block * WIDTH, HEAD), HEAD)


def first_kernel(order_ref, normed_ref, down_ref, key_ref, value_ref, send_ref, low_ref):
    low = dot(normed_ref[...], down_ref[...]).astype(BF16)
    low = jnp.concatenate([low, jnp.zeros((ROWS, HEAD - 3 * RANK), BF16)], axis=1)
    low_ref[...] = low
    send_ref[:, 2 * SHIFTED * HEAD :] = low[HALF:]
    for slot in range(SHIFTED):
        lanes = lanes_of(order_ref, slot)
        send_ref[:, slot * HEAD : (slot + 1) * HEAD] = key_ref[HALF:, lanes]
        send_ref[:, (SHIFTED + slot) * HEAD : (SHIFTED + slot + 1) * HEAD] = value_ref[HALF:, lanes]


def own_kernel(order_ref, query_ref, key_ref, value_ref, cot_ref, out_ref):
    whole = causal(ROWS, ROWS, 0)
    half = causal(HALF, HALF, 0)
    nothing = jnp.zeros((HALF, HEAD), BF16)
    for slot in range(SHIFTED, HEADS):
        lanes = lanes_of(order_ref, slot)
        grads = attend(query_ref[:, lanes], key_ref[:, lanes], value_ref[:, lanes], cot_ref[:, lanes], whole)
        for block in range(3):
            out_ref[:ROWS, lanes_of(order_ref, slot, block)] = grads[block]
            out_ref[ROWS:, lanes_of(order_ref, slot, block)] = nothing
    for slot in range(SHIFTED):
        lanes = lanes_of(order_ref, slot)
        grads = attend(
            query_ref[HALF:, lanes], key_ref[HALF:, lanes], value_ref[HALF:, lanes], cot_ref[HALF:, lanes], half
        )
        for block in range(3):
            out_ref[HALF:ROWS, lanes_of(order_ref, slot, block)] = grads[block]


def joint_kernel(
    order_ref, query_ref, key_ref, value_ref, cot_ref, come_ref, up_ref, have_ref, out_ref, proj_ref, back_ref
):
    out_ref[...] = have_ref[...]
    allowed = causal(ROWS, HALF, HALF)
    nothing = jnp.zeros((HALF, HEAD), BF16)
    for slot in range(SHIFTED):
        lanes = lanes_of(order_ref, slot)
        far_key = come_ref[:, slot * HEAD : (slot + 1) * HEAD]
        far_value = come_ref[:, (SHIFTED + slot) * HEAD : (SHIFTED + slot + 1) * HEAD]
        key = jnp.concatenate([far_key, key_ref[:HALF, lanes]], axis=0)
        value = jnp.concatenate([far_value, value_ref[:HALF, lanes]], axis=0)
        dquery, dkey, dvalue = attend(query_ref[:HALF, lanes], key, value, cot_ref[:HALF, lanes], allowed)
        out_ref[:HALF, lanes] = dquery
        out_ref[ROWS:, lanes] = nothing
        for block, grad in ((1, dkey), (2, dvalue)):
            out_ref[:HALF, lanes_of(order_ref, slot, block)] = grad[HALF:]
            out_ref[ROWS:, lanes_of(order_ref, slot, block)] = grad[:HALF]
    total = jnp.zeros((ROWS + HALF, HEAD), F32)
    for block in range(3):
        columns = slice(block * WIDTH, (block + 1) * WIDTH)
        parts = [up_ref[:, columns] if place == block else jnp.zeros((RANK, WIDTH), BF16) for place in range(4)]
        total = total + dot_last(out_ref[:, columns], jnp.concatenate(parts, axis=0))
    proj_ref[...] = total[:ROWS]
    back_ref[...] = total[ROWS:]


def up_kernel(grads_ref, low_ref, come_ref, out_ref, sums_ref):
    low = jnp.concatenate([low_ref[...], come_ref[...]], axis=0).astype(F32)
    lane = lax.broadcasted_iota(jnp.int32, low.shape, 1) // RANK
    span = WIDTH // 4
    for chunk in range(12):
        block, quarter = chunk // 4, chunk // 3
        right = jnp.zeros_like(low)
        for place in sorted({quarter, 3}):
            turned = pltpu.roll(low, (place - block) % 4 * RANK, 1) if place != block else low
            right = jnp.where(lane == place, turned, right)
        sums_ref[chunk * span : (chunk + 1) * span, :] = dot_first(
            grads_ref[:, chunk * span : (chunk + 1) * span], right.astype(BF16)
        )
    place = lax.broadcasted_iota(jnp.int32, (8, HEAD), 1) // RANK
    upper = lax.broadcasted_iota(jnp.int32, (8, HEAD), 0) < 4

    def tile(z, g, third):
        start = ((z * G + g) * 3 + third) * 8
        return sums_ref[start : start + 8, :]

    for g in range(G):
        for z in range(0, Z, 2):
            for c in range(C):
                pair = jnp.concatenate([tile(z, g, 2 * c), tile(z + 1, g, 2 * c)], axis=0)
                out_ref[c, g, z * 8 : z * 8 + 16, :] = pair.astype(BF16)
        middle = []
        for low_z in range(4):
            merged = tile(low_z, g, 1)
            for quarter in range(1, 4):
                merged = jnp.where(place == quarter, tile(4 * quarter + low_z, g, 1), merged)
            middle.append(merged)
        swapped = [pltpu.roll(item, 4, 0) for item in middle]
        for c in range(C):
            rows = []
            for even in (0, 2):
                if c == 0:
                    rows.append(jnp.where(upper, middle[even], swapped[even + 1]))
                else:
                    rows.append(jnp.where(upper, swapped[even], middle[even + 1]))
            out_ref[c, g, Z * 8 :, :] = jnp.concatenate(rows, axis=0).astype(BF16)


def down_kernel(core_ref, normed_ref, proj_ref, back_ref, up_ref, mine_ref, other_ref):
    own = core_ref[0]
    total = proj_ref[...]
    total = jnp.concatenate([total[:HALF], total[HALF:] + back_ref[...]], axis=0).astype(BF16)
    lane = lax.broadcasted_iota(jnp.int32, (16, HEAD), 1)
    for z in range(0, Z, 2):
        part = dot_first(normed_ref[:, z * 256 : (z + 2) * 256], total)
        part = part.reshape(2, G, C, 8, HEAD)
        for g in range(G):
            pieces = []
            for c in range(C):
                down = jnp.concatenate([part[0, g, c], part[1, g, c]], axis=0)
                up = up_ref[c, g, z * 8 : z * 8 + 16, :]
                pieces.append(jnp.where(lane < 3 * RANK, down, up.astype(F32)).astype(BF16))
            start = g * PART + z * 8
            mine_ref[start : start + 16, :] = jnp.where(own == 0, pieces[0], pieces[1])
            other_ref[start : start + 16, :] = jnp.where(own == 0, pieces[1], pieces[0])
    for g in range(G):
        start = g * PART + Z * 8
        pieces = [up_ref[c, g, Z * 8 :, :] for c in range(C)]
        mine_ref[start : start + 16, :] = jnp.where(own == 0, pieces[0], pieces[1])
        other_ref[start : start + 16, :] = jnp.where(own == 0, pieces[1], pieces[0])


def middle_kernel(come_ref, out_ref):
    total = come_ref[0].astype(F32)
    for item in range(1, G):
        total = total + come_ref[item].astype(F32)
    for z in range(Z):
        start = Z * 8 + z % 4 // 2 * 8
        tiles = jnp.concatenate([total[z * 8 : z * 8 + 8], total[start : start + 8]], axis=0)
        out_ref[z] = tiles.astype(BF16)


def last_kernel(place_ref, come_ref, down_ref, up_ref):
    z, c = place_ref[0], place_ref[1]
    total = come_ref[0].astype(F32)
    for item in range(1, Z):
        total = total + come_ref[item].astype(F32)
    total = total * ADAPTER_SCALE
    upper, lower = total[:8], total[8:]
    down_ref[...] = upper[:, : 3 * RANK].astype(BF16)
    lower = pltpu.roll(lower, lax.rem((3 - z // 4) * RANK, HEAD), 1)
    moved = lax.rem(z, 2) != c
    lower = jnp.where(moved, pltpu.roll(lower, 4, 0), lower)
    both = jnp.concatenate([upper, lower], axis=0)
    both = jnp.where(c == 1, pltpu.roll(both, 4, 0), both)
    square = jnp.concatenate([both, jnp.zeros((HEAD - 16, HEAD), F32)], axis=0)
    up_ref[...] = square.T[3 * RANK :, :12].astype(BF16)


def shape(dims, kind=BF16):
    return jax.ShapeDtypeStruct(dims, kind)


def first_call(order, normed, down, keys, values):
    return call(
        first_kernel,
        "send_parts",
        (shape((HALF, (2 * SHIFTED + 1) * HEAD)), shape((ROWS, HEAD))),
        [SMEM, VMEM, VMEM, VMEM, VMEM],
        130_000_000,
        4_000_000,
    )(order, normed, down, keys, values)


def own_call(order, queries, keys, values, cotangent):
    return call(
        own_kernel,
        "own_attention",
        shape((ROWS + HALF, 3 * WIDTH)),
        [SMEM, VMEM, VMEM, VMEM, VMEM],
        2_000_000_000,
        6_000_000,
    )(order, queries, keys, values, cotangent)


def joint_call(order, queries, keys, values, cotangent, come, up, have):
    return call(
        joint_kernel,
        "joint_attention",
        (shape((ROWS + HALF, 3 * WIDTH)), shape((ROWS, HEAD), F32), shape((HALF, HEAD), F32)),
        [SMEM] + [VMEM] * 7,
        1_000_000_000,
        6_000_000,
    )(order, queries, keys, values, cotangent, come, up, have)


def up_call(grads, low, far_low):
    return call(
        up_kernel,
        "up_gradient",
        shape((C, G, PART, HEAD)),
        [VMEM] * 3,
        1_000_000_000,
        6_000_000,
        scratch_shapes=[pltpu.VMEM((3 * WIDTH, HEAD), F32)],
    )(grads, low, far_low)


def down_call(core, normed, proj, back, up):
    return call(
        down_kernel,
        "down_gradient",
        (shape((G * PART, HEAD)), shape((G * PART, HEAD))),
        [SMEM] + [VMEM] * 4,
        500_000_000,
        4_000_000,
    )(core, normed, proj, back, up)


def middle_call(come):
    return call(middle_kernel, "middle_sum", shape((Z, 16, HEAD)), [VMEM], 1_000_000, 600_000)(come)


def last_call(place, come):
    return call(
        last_kernel, "last_sum", (shape((8, 3 * RANK)), shape((RANK, 12))), [SMEM, VMEM], 100_000, 70_000
    )(place, come)


def per_device(normed, queries, keys, values, cotangent, down, up, order):
    normed, queries, keys, values, cotangent = (
        item[0] for item in (normed, queries, keys, values, cotangent)
    )
    z, core = lax.axis_index("z"), lax.axis_index("c")
    ring = ("yh", "x", "c")
    count = 16
    send, low = first_call(order, normed, down, keys, values)
    come = lax.ppermute(send, ring, [(item, (item + 1) % count) for item in range(count)])
    have = own_call(order, queries, keys, values, cotangent)
    grads, proj, back = joint_call(order, queries, keys, values, cotangent, come, up, have)
    back = lax.ppermute(back, ring, [(item, (item - 1) % count) for item in range(count)])
    up_part = up_call(grads, low, come[:, 2 * SHIFTED * HEAD :])
    mine, other = down_call(core.reshape(1), normed, proj, back, up_part)
    other = lax.ppermute(other, "c", [(0, 1), (1, 0)])
    chip = (mine.astype(F32) + other.astype(F32)).astype(BF16)
    plane = lax.all_to_all(chip.reshape(G, PART, HEAD), ("yl", "yh", "x"), 0, 0)
    line = lax.all_to_all(middle_call(plane), "z", 0, 0)
    return last_call(jnp.stack([z, core]), line)


def solution(mesh):
    fine = Mesh(mesh.devices.reshape(Z, 2, 2, 4, C), ("z", "yl", "yh", "x", "c"))
    dp, seq = ("z", "yl"), ("yh", "x", "c")
    tokens = P(dp, seq, None)
    in_specs = (tokens,) * 5 + (P(),) * 3
    out_specs = (P(dp + seq, None), P(None, dp + seq))
    return jax.shard_map(per_device, mesh=fine, in_specs=in_specs, out_specs=out_specs, check_vma=False)
```

time: 561 us -> 84.2 us (0.15)
  the two profiles are of different devices: /device:TPU:4 before, /device:TPU:2 now
where the time goes in v1:
time: 84.2 us; the launch traced here: 83.6 us
  blocking collectives  26.2 us (31%)
  starting transfers between devices  19.6 us (23%)
  waiting for transfers between devices  14.8 us (18%)
  Pallas kernels  14.1 us (17%)
  local copies, waits for them, and re-layouts  7.8 us (9%)
    all_to_all x1, blocking collectives, per_device(): plane = lax.all_to_all(chip.reshape(G, PART, HEAD), ('yl', 'yh', 'x'), 0, 0)  26.2 us
    all_to_all x1, waiting for transfers between devices, per_device(): line = lax.all_to_all(middle_call(plane), 'z', 0, 0)  12.8 us
    all_to_all x1, starting transfers between devices, per_device(): line = lax.all_to_all(middle_call(plane), 'z', 0, 0)  10.5 us
    unnamed x19, local copies, waits for them, and re-layouts  7.12 us
    pallas_call x1, Pallas kernels, own_call(): call(own_kernel, 'own_attention', shape((ROWS + HALF, 3 * WIDTH)), [SMEM,...  5.38 us
    pallas_call x1, Pallas kernels, joint_call(): call(joint_kernel, 'joint_attention', (shape((ROWS + HALF, 3 * WIDTH)), s...  3.8 us
    ppermute x1, starting transfers between devices, per_device(): lax.ppermute(back, ring, [(item, (item - 1) % count) for item in range(co...  3.64 us
    ppermute x1, starting transfers between devices, per_device(): other = lax.ppermute(other, 'c', [(0, 1), (1, 0)])  3.52 us
  transfers between devices with their start and end apart: 4, of which 3 were waited for; matrix products, arithmetic and copies ran while one was open for 0% of the time, Pallas kernels for 8%

profile of v1, /device:TPU:2, one launch (start us, length us, event | category | flops | bytes accessed | tf_op | source)
XLA Modules:
  0.0 83.6 jit_solution(16905244006901914396)
XLA Ops:
  0.6 0.0 copy-start
  0.6 0.0 copy-start.8
  0.6 1.7 %copy.10.down_ref = bf16[4096,96]{1,0:T(8,128)(2,1)S(1)} copy(bf16[4096,96]{0,1:T(8,128)(2,1)} %param.13) | data formatting | bytes 1572864 | tf_op args[5]
  2.3 0.0 copy-done
  2.3 0.0 copy-done.8
  2.4 0.0 copy-start.1
  2.4 1.1 %copy-done.1 = bf16[1,160,2048]{2,1,0:T(8,128)(2,1)S(1)} copy-done((bf16[1,160,2048]{2,1,0:T(8,128)(2,1)S(1)}, bf16[1,160,2048]{2,1,0:T(8,128)(2,1)}, u32[]{:S(2)}) %copy-start.1) | copy-done | bytes 655384
  3.4 0.0 copy-start.3
  3.4 1.1 %copy-done.3 = bf16[1,160,2048]{2,1,0:T(8,128)(2,1)S(1)} copy-done((bf16[1,160,2048]{2,1,0:T(8,128)(2,1)S(1)}, bf16[1,160,2048]{2,1,0:T(8,128)(2,1)}, u32[]{:S(2)}) %copy-start.3) | copy-done | bytes 655384
  4.5 0.0 copy-start.2
  4.5 1.1 %send_parts.1 = (bf16[80,2176]{1,0:T(8,128)(2,1)S(1)}, bf16[160,128]{1,0:T(8,128)(2,1)S(1)}) custom-call(s32[16]{0:T(128)S(1)} %copy-done.8, bf16[160,4096]{1,0:T(8,128)(2,1)S(1)} %bitcast.8, bf16[4096,96]{1,0:T(8,128)(2,1)S(1)} %copy.10.down_ref, bf16[160,2048]{1,0:T(8,128)(2,1)S(1)} %bitcast.10, bf16[160,2048]{1,0:T(8,128)(2,1)S(1)} %bitcast.13), custom_call_target="tpu_custom_call" | custom-call | flops 130000000 | bytes 4000000 | tf_op jit(solution)/shard_map/send_parts/pallas_call | solution.py:232
  5.6 1.9 %collective-permute-start = (bf16[80,2176]{1,0:T(8,128)(2,1)S(1)}, bf16[80,2176]{1,0:T(8,128)(2,1)S(1)}, u32[]{:S(2)}, u32[]{:S(2)}) collective-permute-start(bf16[80,2176]{1,0:T(8,128)(2,1)S(1)} %get-tuple-element.9), channel_id=1, source_target_pairs={{0,1},{1,2},{2,3},{3,4},{4,5},{5,6},{6,7},{7,8},{8,9},{9,10},{10,1... | collective-permute-start | bytes 1044488 | tf_op jit(solution)/shard_map/ppermute | solution.py:305
  7.5 0.0 copy-done.2
  7.5 0.0 copy-start.4
  7.6 1.1 %copy-done.4 = bf16[1,160,2048]{2,1,0:T(8,128)(2,1)S(1)} copy-done((bf16[1,160,2048]{2,1,0:T(8,128)(2,1)S(1)}, bf16[1,160,2048]{2,1,0:T(8,128)(2,1)}, u32[]{:S(2)}) %copy-start.4) | copy-done | bytes 655384
  8.6 0.0 copy-start.5
  8.6 1.1 %copy-done.5 = bf16[1,160,2048]{2,1,0:T(8,128)(2,1)S(1)} copy-done((bf16[1,160,2048]{2,1,0:T(8,128)(2,1)S(1)}, bf16[1,160,2048]{2,1,0:T(8,128)(2,1)}, u32[]{:S(2)}) %copy-start.5) | copy-done | bytes 655384
  9.7 0.0 copy-start.6
  9.7 1.1 %copy-done.6 = bf16[1,160,2048]{2,1,0:T(8,128)(2,1)S(1)} copy-done((bf16[1,160,2048]{2,1,0:T(8,128)(2,1)S(1)}, bf16[1,160,2048]{2,1,0:T(8,128)(2,1)}, u32[]{:S(2)}) %copy-start.6) | copy-done | bytes 655384
  10.8 0.0 copy-start.7
  10.8 5.4 %own_attention.1.have_ref = bf16[240,6144]{1,0:T(8,128)(2,1)S(1)} custom-call(s32[16]{0:T(128)S(1)} %copy-done.8, bf16[160,2048]{1,0:T(8,128)(2,1)S(1)} %bitcast.16, bf16[160,2048]{1,0:T(8,128)(2,1)S(1)} %bitcast.11, bf16[160,2048]{1,0:T(8,128)(2,1)S(1)} %bitcast.14, bf16[160,2048]{1,0:T(8,128)(2,1)S(1)} %bitcast.18), custom_call_target="tpu_custom_call" | custom-call | flops 2000000000 | bytes 6000000 | tf_op jit(solution)/shard_map/own_attention/pallas_call | solution.py:243
  16.2 0.0 collective-permute-done.come_ref
  16.2 0.0 copy-done.7
  16.2 3.8 %joint_attention.1 = (bf16[240,6144]{1,0:T(8,128)(2,1)S(1)}, f32[160,128]{1,0:T(8,128)S(1)}, f32[80,128]{1,0:T(8,128)S(1)}) custom-call(s32[16]{0:T(128)S(1)} %copy-done.8, bf16[160,2048]{1,0:T(8,128)(2,1)S(1)} %bitcast.17, bf16[160,2048]{1,0:T(8,128)(2,1)S(1)} %bitcast.12, bf16[160,2048]{1,0:T(8,128)(2,1)S(1)} %bitcast.15, bf16[160,2048]{1,0:T(8,128)(2,1)S(1)} %bitcast.19, ...), custom_call_target="tpu_custom_call" | custom-call | flops 1000000000 | bytes 6000000 | tf_op jit(solution)/shard_map/joint_attention/pallas_call | solution.py:254
  20.0 3.6 %collective-permute-start.1 = (f32[80,128]{1,0:T(8,128)S(1)}, f32[80,128]{1,0:T(8,128)S(1)}, u32[]{:S(2)}, u32[]{:S(2)}) collective-permute-start(f32[80,128]{1,0:T(8,128)S(1)} %get-tuple-element.11), channel_id=1, source_target_pairs={{0,15},{1,0},{2,1},{3,2},{4,3},{5,4},{6,5},{7,6},{8,7},{9,8},{10,9... | collective-permute-start | bytes 122888 | tf_op jit(solution)/shard_map/ppermute | solution.py:308
  23.7 1.2 %up_gradient.1.up_ref = bf16[2,16,144,128]{3,2,1,0:T(8,128)(2,1)S(1)} custom-call(bf16[240,6144]{1,0:T(8,128)(2,1)S(1)} %get-tuple-element.12.grads_ref, bf16[160,128]{1,0:T(8,128)(2,1)S(1)} %get-tuple-element.13.low_ref, bf16[80,128]{1,0:T(8,128)(2,1)S(1)} %slice.4.come_ref), custom_call_target="tpu_custom_call" | custom-call | flops 1000000000 | bytes 6000000 | tf_op jit(solution)/shard_map/up_gradient/pallas_call | solution.py:265
  24.9 0.4 collective-permute-done.1.back_ref
  25.3 0.8 down_gradient.1
  26.2 3.5 %collective-permute-start.2 = (bf16[2304,128]{1,0:T(8,128)(2,1)S(1)}, bf16[2304,128]{1,0:T(8,128)(2,1)S(1)}, u32[]{:S(2)}, u32[]{:S(2)}) collective-permute-start(bf16[2304,128]{1,0:T(8,128)(2,1)S(1)} %get-tuple-element.15), channel_id=1, source_target_pairs={{0,1},{1,0},{2,3},{3,2},{4,5},{5,4},{6,7},{7,6},{8,9},{9,8},{10,11... | collective-permute-start | bytes 1769480 | tf_op jit(solution)/shard_map/ppermute | solution.py:311
  29.7 1.6 %collective-permute-done.2 = bf16[2304,128]{1,0:T(8,128)(2,1)S(1)} collective-permute-done((bf16[2304,128]{1,0:T(8,128)(2,1)S(1)}, bf16[2304,128]{1,0:T(8,128)(2,1)S(1)}, u32[]{:S(2)}, u32[]{:S(2)}) %collective-permute-start.2) | collective-permute-done | bytes 589856 | tf_op jit(solution)/shard_map/ppermute | solution.py:311
  31.3 0.2 add_convert_fusion
  31.5 26.2 %all_to_all.10.come_ref = bf16[16,144,128]{2,1,0:T(8,128)(2,1)S(1)} all-to-all(bf16[16,144,128]{2,1,0:T(8,128)(2,1)S(1)} %bitcast.20), channel_id=1, replica_groups=mesh['z'=16,'yl'=2,'yh'=2,'x'=4,'c'=2] {'yl','yh','x'}, dimensions={0} | all-to-all | bytes 1179648 | tf_op jit(solution)/shard_map/all_to_all | solution.py:313
  57.7 0.7 middle_sum.1
  58.4 10.5 %all-to-all-start.1 = ((bf16[16,16,128]{2,1,0:T(8,128)(2,1)}), bf16[16,16,128]{2,1,0:T(8,128)(2,1)S(1)}, u32[]{:S(2)}, u32[]{:S(2)}) async-start(bf16[16,16,128]{2,1,0:T(8,128)(2,1)} %middle_sum.1), calls=%async_computation.1 | async-start | bytes 131072 | tf_op jit(solution)/shard_map/all_to_all | solution.py:314
  68.9 0.1 pad_add_fusion.place_ref
  69.0 12.8 %all-to-all-done.1.come_ref = bf16[16,16,128]{2,1,0:T(8,128)(2,1)S(1)} async-done(((bf16[16,16,128]{2,1,0:T(8,128)(2,1)}), bf16[16,16,128]{2,1,0:T(8,128)(2,1)S(1)}, u32[]{:S(2)}, u32[]{:S(2)}) %all-to-all-start.1) | async-done | bytes 65568 | tf_op jit(solution)/shard_map/all_to_all | solution.py:314
  81.8 1.1 %last_sum.1 = (bf16[8,96]{1,0:T(8,128)(2,1)}, bf16[32,12]{1,0:T(8,128)(2,1)S(1)}) custom-call(s32[2]{0:T(128)S(1)} %pad_add_fusion.place_ref, bf16[16,16,128]{2,1,0:T(8,128)(2,1)S(1)} %all-to-all-done.1.come_ref), custom_call_target="tpu_custom_call" | custom-call | flops 100000 | bytes 70000 | tf_op jit(solution)/shard_map/last_sum/pallas_call | solution.py:292
  82.9 0.7 copy.11
  (1 shorter events, 0.0 us)
Async XLA Ops:
  0.6 1.7 %copy-start = (bf16[1,160,4096]{2,1,0:T(8,128)(2,1)S(1)}, bf16[1,160,4096]{2,1,0:T(8,128)(2,1)}, u32[]{:S(2)}) copy-start(bf16[1,160,4096]{2,1,0:T(8,128)(2,1)} %param.8) | copy-start | bytes 3932164
  0.6 1.7 %copy-start.8 = (s32[16]{0:T(128)S(1)}, s32[16]{0:T(128)}, u32[]{:S(2)}) copy-start(s32[16]{0:T(128)} %order_ref.5) | copy-start | bytes 196
  2.4 1.1 %copy-start.1 = (bf16[1,160,2048]{2,1,0:T(8,128)(2,1)S(1)}, bf16[1,160,2048]{2,1,0:T(8,128)(2,1)}, u32[]{:S(2)}) copy-start(bf16[1,160,2048]{2,1,0:T(8,128)(2,1)} %param.10) | copy-start | bytes 1966084
  3.4 1.1 %copy-start.3 = (bf16[1,160,2048]{2,1,0:T(8,128)(2,1)S(1)}, bf16[1,160,2048]{2,1,0:T(8,128)(2,1)}, u32[]{:S(2)}) copy-start(bf16[1,160,2048]{2,1,0:T(8,128)(2,1)} %param.11) | copy-start | bytes 1966084
  4.5 3.0 %copy-start.2 = (bf16[1,160,2048]{2,1,0:T(8,128)(2,1)S(1)}, bf16[1,160,2048]{2,1,0:T(8,128)(2,1)}, u32[]{:S(2)}) copy-start(bf16[1,160,2048]{2,1,0:T(8,128)(2,1)} %param.10) | copy-start | bytes 1966084
  5.6 10.6 %collective-permute-start = (bf16[80,2176]{1,0:T(8,128)(2,1)S(1)}, bf16[80,2176]{1,0:T(8,128)(2,1)S(1)}, u32[]{:S(2)}, u32[]{:S(2)}) collective-permute-start(bf16[80,2176]{1,0:T(8,128)(2,1)S(1)} %get-tuple-element.9), channel_id=1, source_target_pairs={{0,1},{1,2},{2,3},{3,4},{4,5},{5,6},{6,7},{7,8},{8,9},{9,10},{10,1... | collective-permute-start | bytes 1044488 | tf_op jit(solution)/shard_map/ppermute | solution.py:305
  7.5 1.1 %copy-start.4 = (bf16[1,160,2048]{2,1,0:T(8,128)(2,1)S(1)}, bf16[1,160,2048]{2,1,0:T(8,128)(2,1)}, u32[]{:S(2)}) copy-start(bf16[1,160,2048]{2,1,0:T(8,128)(2,1)} %param.11) | copy-start | bytes 1966084
  8.6 1.1 %copy-start.5 = (bf16[1,160,2048]{2,1,0:T(8,128)(2,1)S(1)}, bf16[1,160,2048]{2,1,0:T(8,128)(2,1)}, u32[]{:S(2)}) copy-start(bf16[1,160,2048]{2,1,0:T(8,128)(2,1)} %param.9) | copy-start | bytes 1966084
  9.7 1.1 %copy-start.6 = (bf16[1,160,2048]{2,1,0:T(8,128)(2,1)S(1)}, bf16[1,160,2048]{2,1,0:T(8,128)(2,1)}, u32[]{:S(2)}) copy-start(bf16[1,160,2048]{2,1,0:T(8,128)(2,1)} %param.12) | copy-start | bytes 1966084
  10.8 5.4 %copy-start.7 = (bf16[32,6144]{1,0:T(8,128)(2,1)S(1)}, bf16[32,6144]{1,0:T(8,128)(2,1)}, u32[]{:S(2)}) copy-start(bf16[32,6144]{1,0:T(8,128)(2,1)} %up_ref.1) | copy-start | bytes 1179652
  20.0 5.3 %collective-permute-start.1 = (f32[80,128]{1,0:T(8,128)S(1)}, f32[80,128]{1,0:T(8,128)S(1)}, u32[]{:S(2)}, u32[]{:S(2)}) collective-permute-start(f32[80,128]{1,0:T(8,128)S(1)} %get-tuple-element.11), channel_id=1, source_target_pairs={{0,15},{1,0},{2,1},{3,2},{4,3},{5,4},{6,5},{7,6},{8,7},{9,8},{10,9... | collective-permute-start | bytes 122888 | tf_op jit(solution)/shard_map/ppermute | solution.py:308
  26.2 5.1 %collective-permute-start.2 = (bf16[2304,128]{1,0:T(8,128)(2,1)S(1)}, bf16[2304,128]{1,0:T(8,128)(2,1)S(1)}, u32[]{:S(2)}, u32[]{:S(2)}) collective-permute-start(bf16[2304,128]{1,0:T(8,128)(2,1)S(1)} %get-tuple-element.15), channel_id=1, source_target_pairs={{0,1},{1,0},{2,3},{3,2},{4,5},{5,4},{6,7},{7,6},{8,9},{9,8},{10,11... | collective-permute-start | bytes 1769480 | tf_op jit(solution)/shard_map/ppermute | solution.py:311
  58.4 23.4 %all-to-all-start.1 = ((bf16[16,16,128]{2,1,0:T(8,128)(2,1)}), bf16[16,16,128]{2,1,0:T(8,128)(2,1)S(1)}, u32[]{:S(2)}, u32[]{:S(2)}) async-start(bf16[16,16,128]{2,1,0:T(8,128)(2,1)} %middle_sum.1), calls=%async_computation.1 | async-start | bytes 131072 | tf_op jit(solution)/shard_map/all_to_all | solution.py:314

commit v2 on v1

--- a/solution.py
+++ b/solution.py
@@ -16,12 +16,16 @@
 RANK = 32
 SCALE = HEAD ** -0.5
 ADAPTER_SCALE = 0.25
+NEAR, FAR = ("yl", "yh", "x"), ("z",)
 Z, G, C = 16, 16, 2
-PART = Z * 8 + 16
+BAND = Z // 4
+WIDE = 4
+PART = Z * 8 + BAND * 4
 
 BF16, F32 = jnp.bfloat16, jnp.float32
 VMEM = pl.BlockSpec(memory_space=pltpu.VMEM)
 SMEM = pl.BlockSpec(memory_space=pltpu.SMEM)
+HBM = pl.BlockSpec(memory_space=pltpu.HBM)
 
 
 def call(body, name, out_shape, in_specs, flops, size, limit=32, **rest):
@@ -74,15 +78,33 @@
     return pl.ds(pl.multiple_of(order_ref[slot] * HEAD + block * WIDTH, HEAD), HEAD)
 
 
-def first_kernel(order_ref, normed_ref, down_ref, key_ref, value_ref, send_ref, low_ref):
-    low = dot(normed_ref[...], down_ref[...]).astype(BF16)
+def first_kernel(
+    order_ref, key_ref, value_ref, normed_ref, down_ref, send_ref, low_ref, normed_own, down_own, sems, wide_sems
+):
+    copies, wide_copies = [], []
+    span = MODEL // WIDE
+    for part in range(WIDE):
+        lanes = slice(part * span, (part + 1) * span)
+        for item, (source, target) in enumerate(((normed_ref, normed_own), (down_ref, down_own))):
+            copy = pltpu.make_async_copy(source.at[:, lanes], target.at[:, lanes], wide_sems.at[item, part])
+            copy.start()
+            wide_copies.append(copy)
+    for place in range(2 * SHIFTED):
+        copy = pltpu.make_async_copy(
+            (key_ref if place < SHIFTED else value_ref).at[HALF:, lanes_of(order_ref, place % SHIFTED)],
+            send_ref.at[:, place * HEAD : (place + 1) * HEAD],
+            sems.at[place],
+        )
+        copy.start()
+        copies.append(copy)
+    for copy in wide_copies:
+        copy.wait()
+    low = dot_last(normed_own[...], down_own[...]).astype(BF16)
     low = jnp.concatenate([low, jnp.zeros((ROWS, HEAD - 3 * RANK), BF16)], axis=1)
     low_ref[...] = low
     send_ref[:, 2 * SHIFTED * HEAD :] = low[HALF:]
-    for slot in range(SHIFTED):
-        lanes = lanes_of(order_ref, slot)
-        send_ref[:, slot * HEAD : (slot + 1) * HEAD] = key_ref[HALF:, lanes]
-        send_ref[:, (SHIFTED + slot) * HEAD : (SHIFTED + slot + 1) * HEAD] = value_ref[HALF:, lanes]
+    for copy in copies:
+        copy.wait()
 
 
 def own_kernel(order_ref, query_ref, key_ref, value_ref, cot_ref, out_ref):
@@ -107,7 +129,7 @@
 def joint_kernel(
     order_ref, query_ref, key_ref, value_ref, cot_ref, come_ref, up_ref, have_ref, out_ref, proj_ref, back_ref
 ):
-    out_ref[...] = have_ref[...]
+    del have_ref
     allowed = causal(ROWS, HALF, HALF)
     nothing = jnp.zeros((HALF, HEAD), BF16)
     for slot in range(SHIFTED):
@@ -132,7 +154,7 @@
 
 
 def up_kernel(grads_ref, low_ref, come_ref, out_ref, sums_ref):
-    low = jnp.concatenate([low_ref[...], come_ref[...]], axis=0).astype(F32)
+    low = jnp.concatenate([low_ref[...], come_ref[:, 2 * SHIFTED * HEAD :]], axis=0).astype(F32)
     lane = lax.broadcasted_iota(jnp.int32, low.shape, 1) // RANK
     span = WIDTH // 4
     for chunk in range(12):
@@ -157,15 +179,15 @@
                 pair = jnp.concatenate([tile(z, g, 2 * c), tile(z + 1, g, 2 * c)], axis=0)
                 out_ref[c, g, z * 8 : z * 8 + 16, :] = pair.astype(BF16)
         middle = []
-        for low_z in range(4):
+        for low_z in range(BAND):
             merged = tile(low_z, g, 1)
             for quarter in range(1, 4):
-                merged = jnp.where(place == quarter, tile(4 * quarter + low_z, g, 1), merged)
+                merged = jnp.where(place == quarter, tile(BAND * quarter + low_z, g, 1), merged)
             middle.append(merged)
         swapped = [pltpu.roll(item, 4, 0) for item in middle]
         for c in range(C):
             rows = []
-            for even in (0, 2):
+            for even in range(0, BAND, 2):
                 if c == 0:
                     rows.append(jnp.where(upper, middle[even], swapped[even + 1]))
                 else:
@@ -179,7 +201,7 @@
     total = jnp.concatenate([total[:HALF], total[HALF:] + back_ref[...]], axis=0).astype(BF16)
     lane = lax.broadcasted_iota(jnp.int32, (16, HEAD), 1)
     for z in range(0, Z, 2):
-        part = dot_first(normed_ref[:, z * 256 : (z + 2) * 256], total)
+        part = dot_first(normed_ref[:, z * G * 16 : (z + 2) * G * 16], total)
         part = part.reshape(2, G, C, 8, HEAD)
         for g in range(G):
             pieces = []
@@ -191,10 +213,10 @@
             mine_ref[start : start + 16, :] = jnp.where(own == 0, pieces[0], pieces[1])
             other_ref[start : start + 16, :] = jnp.where(own == 0, pieces[1], pieces[0])
     for g in range(G):
-        start = g * PART + Z * 8
+        span = slice(g * PART + Z * 8, (g + 1) * PART)
         pieces = [up_ref[c, g, Z * 8 :, :] for c in range(C)]
-        mine_ref[start : start + 16, :] = jnp.where(own == 0, pieces[0], pieces[1])
-        other_ref[start : start + 16, :] = jnp.where(own == 0, pieces[1], pieces[0])
+        mine_ref[span, :] = jnp.where(own == 0, pieces[0], pieces[1])
+        other_ref[span, :] = jnp.where(own == 0, pieces[1], pieces[0])
 
 
 def middle_kernel(come_ref, out_ref):
@@ -202,7 +224,7 @@
     for item in range(1, G):
         total = total + come_ref[item].astype(F32)
     for z in range(Z):
-        start = Z * 8 + z % 4 // 2 * 8
+        start = Z * 8 + z % BAND // 2 * 8
         tiles = jnp.concatenate([total[z * 8 : z * 8 + 8], total[start : start + 8]], axis=0)
         out_ref[z] = tiles.astype(BF16)
 
@@ -215,28 +237,34 @@
     total = total * ADAPTER_SCALE
     upper, lower = total[:8], total[8:]
     down_ref[...] = upper[:, : 3 * RANK].astype(BF16)
-    lower = pltpu.roll(lower, lax.rem((3 - z // 4) * RANK, HEAD), 1)
+    lower = pltpu.roll(lower, (3 - z // BAND) * RANK, 1)
     moved = lax.rem(z, 2) != c
     lower = jnp.where(moved, pltpu.roll(lower, 4, 0), lower)
     both = jnp.concatenate([upper, lower], axis=0)
     both = jnp.where(c == 1, pltpu.roll(both, 4, 0), both)
-    square = jnp.concatenate([both, jnp.zeros((HEAD - 16, HEAD), F32)], axis=0)
-    up_ref[...] = square.T[3 * RANK :, :12].astype(BF16)
+    up_ref[...] = both[:12, 3 * RANK :].astype(BF16)
 
 
 def shape(dims, kind=BF16):
     return jax.ShapeDtypeStruct(dims, kind)
 
 
-def first_call(order, normed, down, keys, values):
+def first_call(order, keys, values, normed, down):
     return call(
         first_kernel,
         "send_parts",
         (shape((HALF, (2 * SHIFTED + 1) * HEAD)), shape((ROWS, HEAD))),
-        [SMEM, VMEM, VMEM, VMEM, VMEM],
+        [SMEM, HBM, HBM, HBM, HBM],
         130_000_000,
-        4_000_000,
-    )(order, normed, down, keys, values)
+        3_000_000,
+        limit=63,
+        scratch_shapes=[
+            pltpu.VMEM(normed.shape, BF16),
+            pltpu.VMEM(down.shape, BF16),
+            pltpu.SemaphoreType.DMA((2 * SHIFTED,)),
+            pltpu.SemaphoreType.DMA((2, WIDE)),
+        ],
+    )(order, keys, values, normed, down)
 
 
 def own_call(order, queries, keys, values, cotangent):
@@ -258,10 +286,11 @@
         [SMEM] + [VMEM] * 7,
         1_000_000_000,
         6_000_000,
+        input_output_aliases={7: 0},
     )(order, queries, keys, values, cotangent, come, up, have)
 
 
-def up_call(grads, low, far_low):
+def up_call(grads, low, come):
     return call(
         up_kernel,
         "up_gradient",
@@ -270,7 +299,7 @@
         1_000_000_000,
         6_000_000,
         scratch_shapes=[pltpu.VMEM((3 * WIDTH, HEAD), F32)],
-    )(grads, low, far_low)
+    )(grads, low, come)
 
 
 def down_call(core, normed, proj, back, up):
@@ -290,7 +319,7 @@
 
 def last_call(place, come):
     return call(
-        last_kernel, "last_sum", (shape((8, 3 * RANK)), shape((RANK, 12))), [SMEM, VMEM], 100_000, 70_000
+        last_kernel, "last_sum", (shape((8, 3 * RANK)), shape((12, RANK))), [SMEM, VMEM], 100_000, 70_000
     )(place, come)
 
 
@@ -298,25 +327,28 @@
     normed, queries, keys, values, cotangent = (
         item[0] for item in (normed, queries, keys, values, cotangent)
     )
-    z, core = lax.axis_index("z"), lax.axis_index("c")
+    far, core = lax.axis_index(FAR), lax.axis_index("c")
     ring = ("yh", "x", "c")
     count = 16
-    send, low = first_call(order, normed, down, keys, values)
-    come = lax.ppermute(send, ring, [(item, (item + 1) % count) for item in range(count)])
+    ahead = [(item, (item + 1) % count) for item in range(count)]
+    behind = [(item, (item - 1) % count) for item in range(count)]
+    send, low = first_call(order, keys, values, normed, down.T)
+    come = lax.ppermute(send, ring, ahead)
     have = own_call(order, queries, keys, values, cotangent)
     grads, proj, back = joint_call(order, queries, keys, values, cotangent, come, up, have)
-    back = lax.ppermute(back, ring, [(item, (item - 1) % count) for item in range(count)])
-    up_part = up_call(grads, low, come[:, 2 * SHIFTED * HEAD :])
+    back = lax.ppermute(back, ring, behind)
+    up_part = up_call(grads, low, come)
     mine, other = down_call(core.reshape(1), normed, proj, back, up_part)
     other = lax.ppermute(other, "c", [(0, 1), (1, 0)])
     chip = (mine.astype(F32) + other.astype(F32)).astype(BF16)
-    plane = lax.all_to_all(chip.reshape(G, PART, HEAD), ("yl", "yh", "x"), 0, 0)
-    line = lax.all_to_all(middle_call(plane), "z", 0, 0)
-    return last_call(jnp.stack([z, core]), line)
+    plane = lax.all_to_all(chip.reshape(G, PART, HEAD), NEAR, 0, 0)
+    line = lax.all_to_all(middle_call(plane), FAR, 0, 0)
+    down_grad, up_grad = last_call(jnp.stack([far, core]), line)
+    return down_grad, up_grad.T
 
 
 def solution(mesh):
-    fine = Mesh(mesh.devices.reshape(Z, 2, 2, 4, C), ("z", "yl", "yh", "x", "c"))
+    fine = Mesh(mesh.devices.reshape(16, 2, 2, 4, 2), ("z", "yl", "yh", "x", "c"))
     dp, seq = ("z", "yl"), ("yh", "x", "c")
     tokens = P(dp, seq, None)
     in_specs = (tokens,) * 5 + (P(),) * 3

time: 84.2 us -> 82.6 us (0.981)
  local copies, waits for them, and re-layouts: 7.8 us -> 3.28 us
  Pallas kernels: 14.1 us -> 17.1 us
    unnamed x19 -> x16, local copies, waits for them, and re-layouts: 7.12 us -> 3.28 us
    pallas_call x1, Pallas kernels: 1.06 us -> 4.02 us  [first_call(): call(first_kernel, 'send_parts', (shape((HALF, (2 * SHIFTED + 1) * HEAD))...]
where the time goes in v2:
time: 82.6 us; the launch traced here: 82.1 us
  blocking collectives  26.2 us (32%)
  starting transfers between devices  19.6 us (24%)
  Pallas kernels  17.1 us (21%)
  waiting for transfers between devices  14.9 us (18%)
  local copies, waits for them, and re-layouts  3.28 us (4%)
    all_to_all x1, blocking collectives, per_device(): plane = lax.all_to_all(chip.reshape(G, PART, HEAD), NEAR, 0, 0)  26.2 us
    all_to_all x1, waiting for transfers between devices, per_device(): line = lax.all_to_all(middle_call(plane), FAR, 0, 0)  12.8 us
    all_to_all x1, starting transfers between devices, per_device(): line = lax.all_to_all(middle_call(plane), FAR, 0, 0)  10.5 us
    pallas_call x1, Pallas kernels, own_call(): call(own_kernel, 'own_attention', shape((ROWS + HALF, 3 * WIDTH)), [SMEM,...  5.38 us
    pallas_call x1, Pallas kernels, first_call(): call(first_kernel, 'send_parts', (shape((HALF, (2 * SHIFTED + 1) * HEAD))...  4.02 us
    pallas_call x1, Pallas kernels, joint_call(): call(joint_kernel, 'joint_attention', (shape((ROWS + HALF, 3 * WIDTH)), s...  3.74 us
    ppermute x1, starting transfers between devices, per_device(): back = lax.ppermute(back, ring, behind)  3.64 us
    ppermute x1, starting transfers between devices, per_device(): other = lax.ppermute(other, 'c', [(0, 1), (1, 0)])  3.51 us
  transfers between devices with their start and end apart: 4, of which 3 were waited for; matrix products, arithmetic and copies ran while one was open for 0% of the time, Pallas kernels for 8%

profile of v2, /device:TPU:2, one launch (start us, length us, event | category | flops | bytes accessed | tf_op | source)
XLA Modules:
  0.0 82.1 jit_solution(12671223136336584568)
XLA Ops:
  0.6 0.0 copy-start.1
  0.6 0.0 copy-start.7
  0.7 4.0 %send_parts.1 = (bf16[80,2176]{1,0:T(8,128)(2,1)}, bf16[160,128]{1,0:T(8,128)(2,1)}) custom-call(s32[16]{0:T(128)} %order_ref.5, bf16[160,2048]{1,0:T(8,128)(2,1)} %bitcast.12, bf16[160,2048]{1,0:T(8,128)(2,1)} %bitcast.15, bf16[160,4096]{1,0:T(8,128)(2,1)} %bitcast.10, bf16[96,4096]{1,0:T(8,128)(2,1)} %bitcast.23), custom_call_target="tpu_custom_call" | custom-call | flops 130000000 | bytes 3000000 | tf_op jit(solution)/shard_map/send_parts/pallas_call | solution.py:253
  4.7 1.9 %collective-permute-start = (bf16[80,2176]{1,0:T(8,128)(2,1)}, bf16[80,2176]{1,0:T(8,128)(2,1)S(1)}, u32[]{:S(2)}, u32[]{:S(2)}) collective-permute-start(bf16[80,2176]{1,0:T(8,128)(2,1)} %get-tuple-element.11), channel_id=1, source_target_pairs={{0,1},{1,2},{2,3},{3,4},{4,5},{5,6},{6,7},{7,8},{8,9},{9,10},{10,1... | collective-permute-start | bytes 1044488 | tf_op jit(solution)/shard_map/ppermute | solution.py:336
  6.6 0.0 copy-done.1
  6.6 0.0 copy-done.7
  6.6 0.0 copy-start.2
  6.6 1.1 %copy-done.2 = bf16[1,160,2048]{2,1,0:T(8,128)(2,1)S(1)} copy-done((bf16[1,160,2048]{2,1,0:T(8,128)(2,1)S(1)}, bf16[1,160,2048]{2,1,0:T(8,128)(2,1)}, u32[]{:S(2)}) %copy-start.2) | copy-done | bytes 655384
  7.7 0.0 copy-start.3
  7.7 1.1 %copy-done.3 = bf16[1,160,2048]{2,1,0:T(8,128)(2,1)S(1)} copy-done((bf16[1,160,2048]{2,1,0:T(8,128)(2,1)S(1)}, bf16[1,160,2048]{2,1,0:T(8,128)(2,1)}, u32[]{:S(2)}) %copy-start.3) | copy-done | bytes 655384
  8.8 0.0 copy-start.4
  8.8 1.1 %copy-done.4 = bf16[1,160,2048]{2,1,0:T(8,128)(2,1)S(1)} copy-done((bf16[1,160,2048]{2,1,0:T(8,128)(2,1)S(1)}, bf16[1,160,2048]{2,1,0:T(8,128)(2,1)}, u32[]{:S(2)}) %copy-start.4) | copy-done | bytes 655384
  9.9 0.0 copy-start.5
  9.9 5.4 %own_attention.1.have_ref = bf16[240,6144]{1,0:T(8,128)(2,1)S(1)} custom-call(s32[16]{0:T(128)S(1)} %copy-done.7, bf16[160,2048]{1,0:T(8,128)(2,1)S(1)} %bitcast.18, bf16[160,2048]{1,0:T(8,128)(2,1)S(1)} %bitcast.13, bf16[160,2048]{1,0:T(8,128)(2,1)S(1)} %bitcast.16, bf16[160,2048]{1,0:T(8,128)(2,1)S(1)} %bitcast.20), custom_call_target="tpu_custom_call" | custom-call | flops 2000000000 | bytes 6000000 | tf_op jit(solution)/shard_map/own_attention/pallas_call | solution.py:271
  15.3 0.0 copy-start.6
  15.3 0.0 collective-permute-done.come_ref
  15.3 0.0 copy-done.5
  15.3 3.7 %joint_attention.1 = (bf16[240,6144]{1,0:T(8,128)(2,1)S(1)}, f32[160,128]{1,0:T(8,128)S(1)}, f32[80,128]{1,0:T(8,128)S(1)}) custom-call(s32[16]{0:T(128)S(1)} %copy-done.7, bf16[160,2048]{1,0:T(8,128)(2,1)S(1)} %bitcast.19, bf16[160,2048]{1,0:T(8,128)(2,1)S(1)} %bitcast.14, bf16[160,2048]{1,0:T(8,128)(2,1)S(1)} %bitcast.17, ...), custom_call_target="tpu_custom_call", output_to_operand_aliasing={{0}: (7, {})} | custom-call | flops 1000000000 | bytes 6000000 | tf_op jit(solution)/shard_map/joint_attention/pallas_call | solution.py:282
  19.1 3.6 %collective-permute-start.1 = (f32[80,128]{1,0:T(8,128)S(1)}, f32[80,128]{1,0:T(8,128)S(1)}, u32[]{:S(2)}, u32[]{:S(2)}) collective-permute-start(f32[80,128]{1,0:T(8,128)S(1)} %get-tuple-element.13), channel_id=1, source_target_pairs={{0,15},{1,0},{2,1},{3,2},{4,3},{5,4},{6,5},{7,6},{8,7},{9,8},{10,9... | collective-permute-start | bytes 122888 | tf_op jit(solution)/shard_map/ppermute | solution.py:339
  22.7 0.0 copy-done.6
  22.7 0.0 copy-start
  22.7 1.2 %up_gradient.1.up_ref = bf16[2,16,144,128]{3,2,1,0:T(8,128)(2,1)S(1)} custom-call(bf16[240,6144]{1,0:T(8,128)(2,1)S(1)} %get-tuple-element.14.grads_ref, bf16[160,128]{1,0:T(8,128)(2,1)S(1)} %copy-done.6, bf16[80,2176]{1,0:T(8,128)(2,1)S(1)} %collective-permute-done.come_ref), custom_call_target="tpu_custom_call" | custom-call | flops 1000000000 | bytes 6000000 | tf_op jit(solution)/shard_map/up_gradient/pallas_call | solution.py:294
  23.9 0.4 collective-permute-done.1.back_ref
  24.4 0.0 copy-done
  24.4 0.8 down_gradient.1
  25.2 3.5 %collective-permute-start.2 = (bf16[2304,128]{1,0:T(8,128)(2,1)S(1)}, bf16[2304,128]{1,0:T(8,128)(2,1)S(1)}, u32[]{:S(2)}, u32[]{:S(2)}) collective-permute-start(bf16[2304,128]{1,0:T(8,128)(2,1)S(1)} %get-tuple-element.17), channel_id=1, source_target_pairs={{0,1},{1,0},{2,3},{3,2},{4,5},{5,4},{6,7},{7,6},{8,9},{9,8},{10,11... | collective-permute-start | bytes 1769480 | tf_op jit(solution)/shard_map/ppermute | solution.py:342
  28.7 1.6 %collective-permute-done.2 = bf16[2304,128]{1,0:T(8,128)(2,1)S(1)} collective-permute-done((bf16[2304,128]{1,0:T(8,128)(2,1)S(1)}, bf16[2304,128]{1,0:T(8,128)(2,1)S(1)}, u32[]{:S(2)}, u32[]{:S(2)}) %collective-permute-start.2) | collective-permute-done | bytes 589856 | tf_op jit(solution)/shard_map/ppermute | solution.py:342
  30.3 0.2 add_convert_fusion
  30.5 26.2 %all_to_all.10.come_ref = bf16[16,144,128]{2,1,0:T(8,128)(2,1)S(1)} all-to-all(bf16[16,144,128]{2,1,0:T(8,128)(2,1)S(1)} %bitcast.22), channel_id=1, replica_groups=mesh['z'=16,'yl'=2,'yh'=2,'x'=4,'c'=2] {'yl','yh','x'}, dimensions={0} | all-to-all | bytes 1179648 | tf_op jit(solution)/shard_map/all_to_all | solution.py:344
  56.7 0.7 middle_sum.1
  57.4 10.5 %all-to-all-start.1 = ((bf16[16,16,128]{2,1,0:T(8,128)(2,1)}), bf16[16,16,128]{2,1,0:T(8,128)(2,1)S(1)}, u32[]{:S(2)}, u32[]{:S(2)}) async-start(bf16[16,16,128]{2,1,0:T(8,128)(2,1)} %middle_sum.1), calls=%async_computation.1 | async-start | bytes 131072 | tf_op jit(solution)/shard_map/all_to_all | solution.py:345
  68.0 0.1 pad_add_fusion.place_ref
  68.0 12.8 %all-to-all-done.1.come_ref = bf16[16,16,128]{2,1,0:T(8,128)(2,1)S(1)} async-done(((bf16[16,16,128]{2,1,0:T(8,128)(2,1)}), bf16[16,16,128]{2,1,0:T(8,128)(2,1)S(1)}, u32[]{:S(2)}, u32[]{:S(2)}) %all-to-all-start.1) | async-done | bytes 65568 | tf_op jit(solution)/shard_map/all_to_all | solution.py:345
  80.8 1.3 %last_sum.1 = (bf16[8,96]{1,0:T(8,128)(2,1)}, bf16[12,32]{1,0:T(8,128)(2,1)}) custom-call(s32[2]{0:T(128)S(1)} %pad_add_fusion.place_ref, bf16[16,16,128]{2,1,0:T(8,128)(2,1)S(1)} %all-to-all-done.1.come_ref), custom_call_target="tpu_custom_call" | custom-call | flops 100000 | bytes 70000 | tf_op jit(solution)/shard_map/last_sum/pallas_call | solution.py:321
Async XLA Ops:
  0.6 6.0 %copy-start.1 = (bf16[1,160,2048]{2,1,0:T(8,128)(2,1)S(1)}, bf16[1,160,2048]{2,1,0:T(8,128)(2,1)}, u32[]{:S(2)}) copy-start(bf16[1,160,2048]{2,1,0:T(8,128)(2,1)} %param.10) | copy-start | bytes 1966084
  0.6 6.0 %copy-start.7 = (s32[16]{0:T(128)S(1)}, s32[16]{0:T(128)}, u32[]{:S(2)}) copy-start(s32[16]{0:T(128)} %order_ref.5) | copy-start | bytes 196
  4.7 10.6 %collective-permute-start = (bf16[80,2176]{1,0:T(8,128)(2,1)}, bf16[80,2176]{1,0:T(8,128)(2,1)S(1)}, u32[]{:S(2)}, u32[]{:S(2)}) collective-permute-start(bf16[80,2176]{1,0:T(8,128)(2,1)} %get-tuple-element.11), channel_id=1, source_target_pairs={{0,1},{1,2},{2,3},{3,4},{4,5},{5,6},{6,7},{7,8},{8,9},{9,10},{10,1... | collective-permute-start | bytes 1044488 | tf_op jit(solution)/shard_map/ppermute | solution.py:336
  6.6 1.1 %copy-start.2 = (bf16[1,160,2048]{2,1,0:T(8,128)(2,1)S(1)}, bf16[1,160,2048]{2,1,0:T(8,128)(2,1)}, u32[]{:S(2)}) copy-start(bf16[1,160,2048]{2,1,0:T(8,128)(2,1)} %param.11) | copy-start | bytes 1966084
  7.7 1.1 %copy-start.3 = (bf16[1,160,2048]{2,1,0:T(8,128)(2,1)S(1)}, bf16[1,160,2048]{2,1,0:T(8,128)(2,1)}, u32[]{:S(2)}) copy-start(bf16[1,160,2048]{2,1,0:T(8,128)(2,1)} %param.9) | copy-start | bytes 1966084
  8.8 1.1 %copy-start.4 = (bf16[1,160,2048]{2,1,0:T(8,128)(2,1)S(1)}, bf16[1,160,2048]{2,1,0:T(8,128)(2,1)}, u32[]{:S(2)}) copy-start(bf16[1,160,2048]{2,1,0:T(8,128)(2,1)} %param.12) | copy-start | bytes 1966084
  9.9 5.4 %copy-start.5 = (bf16[32,6144]{1,0:T(8,128)(2,1)S(1)}, bf16[32,6144]{1,0:T(8,128)(2,1)}, u32[]{:S(2)}) copy-start(bf16[32,6144]{1,0:T(8,128)(2,1)} %up_ref.1) | copy-start | bytes 1179652
  15.3 7.4 %copy-start.6 = (bf16[160,128]{1,0:T(8,128)(2,1)S(1)}, bf16[160,128]{1,0:T(8,128)(2,1)}, u32[]{:S(2)}) copy-start(bf16[160,128]{1,0:T(8,128)(2,1)} %get-tuple-element.15.low_ref) | copy-start | bytes 122884
  19.1 5.3 %collective-permute-start.1 = (f32[80,128]{1,0:T(8,128)S(1)}, f32[80,128]{1,0:T(8,128)S(1)}, u32[]{:S(2)}, u32[]{:S(2)}) collective-permute-start(f32[80,128]{1,0:T(8,128)S(1)} %get-tuple-element.13), channel_id=1, source_target_pairs={{0,15},{1,0},{2,1},{3,2},{4,3},{5,4},{6,5},{7,6},{8,7},{9,8},{10,9... | collective-permute-start | bytes 122888 | tf_op jit(solution)/shard_map/ppermute | solution.py:339
  22.7 1.6 %copy-start = (bf16[1,160,4096]{2,1,0:T(8,128)(2,1)S(1)}, bf16[1,160,4096]{2,1,0:T(8,128)(2,1)}, u32[]{:S(2)}) copy-start(bf16[1,160,4096]{2,1,0:T(8,128)(2,1)} %param.8) | copy-start | bytes 3932164
  25.2 5.1 %collective-permute-start.2 = (bf16[2304,128]{1,0:T(8,128)(2,1)S(1)}, bf16[2304,128]{1,0:T(8,128)(2,1)S(1)}, u32[]{:S(2)}, u32[]{:S(2)}) collective-permute-start(bf16[2304,128]{1,0:T(8,128)(2,1)S(1)} %get-tuple-element.17), channel_id=1, source_target_pairs={{0,1},{1,0},{2,3},{3,2},{4,5},{5,4},{6,7},{7,6},{8,9},{9,8},{10,11... | collective-permute-start | bytes 1769480 | tf_op jit(solution)/shard_map/ppermute | solution.py:342
  57.4 23.4 %all-to-all-start.1 = ((bf16[16,16,128]{2,1,0:T(8,128)(2,1)}), bf16[16,16,128]{2,1,0:T(8,128)(2,1)S(1)}, u32[]{:S(2)}, u32[]{:S(2)}) async-start(bf16[16,16,128]{2,1,0:T(8,128)(2,1)} %middle_sum.1), calls=%async_computation.1 | async-start | bytes 131072 | tf_op jit(solution)/shard_map/all_to_all | solution.py:345

commit v3 on v2

v3 whole, which is shorter than its diff:
```python
import jax
import jax.numpy as jnp
from jax import lax
from jax.experimental import pallas as pl
from jax.experimental.pallas import tpu as pltpu
from jax.sharding import Mesh
from jax.sharding import PartitionSpec as P

HEAD = 128
ROWS = 160
HALF = 80
HEADS = 16
SHIFTED = 8
WIDTH = HEADS * HEAD
MODEL = 4096
RANK = 32
SCALE = HEAD ** -0.5
ADAPTER_SCALE = 0.25
NEAR, FAR = ("yl", "yh", "x"), ("z",)
Z, G, C = 16, 16, 2
BAND = Z // 4
WIDE = 2
BATCH = 8
PART = Z * 8 + BAND * 4

BF16, F32 = jnp.bfloat16, jnp.float32
VMEM = pl.BlockSpec(memory_space=pltpu.VMEM)
SMEM = pl.BlockSpec(memory_space=pltpu.SMEM)
HBM = pl.BlockSpec(memory_space=pltpu.HBM)


def call(body, name, out_shape, in_specs, flops, size, limit=32, out_specs=None, **rest):
    return pl.pallas_call(
        body,
        name=name,
        out_shape=out_shape,
        in_specs=in_specs,
        out_specs=out_specs or jax.tree.map(lambda _: VMEM, out_shape),
        compiler_params=pltpu.CompilerParams(vmem_limit_bytes=limit * 1024 * 1024),
        cost_estimate=pl.CostEstimate(flops=flops, bytes_accessed=size, transcendentals=0),
        **rest,
    )


def dot(left, right):
    return jnp.dot(left, right, preferred_element_type=F32)


def dot_last(left, right):
    return lax.dot_general(left, right, (((1,), (1,)), ((), ())), preferred_element_type=F32)


def dot_first(left, right):
    return lax.dot_general(left, right, (((0,), (0,)), ((), ())), preferred_element_type=F32)


def attend(parts, allowed):
    queries, keys, values, cotangents = zip(*parts)
    scores = [jnp.where(allowed, dot_last(key, query), -jnp.inf) for query, key in zip(queries, keys)]
    dprobs = [dot_last(value, cotangent) for value, cotangent in zip(values, cotangents)]
    tops = [jnp.max(item, axis=0, keepdims=True) for item in scores]
    powers = [jnp.exp((item - top) * SCALE) for item, top in zip(scores, tops)]
    probs = [item * (1.0 / jnp.sum(item, axis=0, keepdims=True)) for item in powers]
    weights = [item.astype(BF16) for item in probs]
    dvalues = [dot(weight, cotangent).astype(BF16) for weight, cotangent in zip(weights, cotangents)]
    deltas = [
        jnp.sum(weight.astype(F32) * dprob, axis=0, keepdims=True) for weight, dprob in zip(weights, dprobs)
    ]
    dscores = [
        (prob * (dprob - delta)).astype(BF16) for prob, dprob, delta in zip(probs, dprobs, deltas)
    ]
    dkeys = [(dot(dscore, query) * SCALE).astype(BF16) for dscore, query in zip(dscores, queries)]
    dqueries = [(dot_first(dscore, key) * SCALE).astype(BF16) for dscore, key in zip(dscores, keys)]
    return list(zip(dqueries, dkeys, dvalues))


def causal(keys, queries, ahead):
    row = lax.broadcasted_iota(jnp.int32, (keys, queries), 0)
    column = lax.broadcasted_iota(jnp.int32, (keys, queries), 1)
    return row <= column + ahead


def lanes_of(info_ref, slot, block=0):
    return pl.ds(pl.multiple_of(info_ref[2 + slot] * HEAD + block * WIDTH, HEAD), HEAD)


def spread(ref, place):
    parts = [ref if item == place else jnp.zeros_like(ref) for item in range(4)]
    return jnp.concatenate(parts, axis=0)


def prepare(
    info_ref, key_ref, value_ref, normed_ref, down_ref, send_ref, low_ref, pair_own, normed_own, down_own, *sems
):
    pair_copies, wide_copies = [], []
    for item, source in enumerate((key_ref, value_ref)):
        copy = pltpu.make_async_copy(source.at[HALF:], pair_own.at[item], sems[0].at[item])
        copy.start()
        pair_copies.append(copy)
    span = MODEL // WIDE
    for part in range(WIDE):
        lanes = slice(part * span, (part + 1) * span)
        for item, (source, target) in enumerate(((normed_ref, normed_own), (down_ref, down_own))):
            copy = pltpu.make_async_copy(source.at[:, lanes], target.at[:, lanes], sems[1].at[item, part])
            copy.start()
            wide_copies.append(copy)
    for item in range(2):
        pair_copies[item].wait()
        for slot in range(SHIFTED):
            place = item * SHIFTED + slot
            send_ref[:, place * HEAD : (place + 1) * HEAD] = pair_own[item, :, lanes_of(info_ref, slot)]
    low = jnp.zeros((ROWS, 3 * RANK), F32)
    for part in range(WIDE):
        lanes = slice(part * span, (part + 1) * span)
        for copy in wide_copies[2 * part : 2 * part + 2]:
            copy.wait()
        low = low + dot_last(normed_own[:, lanes], down_own[:, lanes])
    low = jnp.concatenate([low.astype(BF16), jnp.zeros((ROWS, HEAD - 3 * RANK), BF16)], axis=1)
    low_ref[...] = low
    send_ref[:, 2 * SHIFTED * HEAD :] = low[HALF:]


def outer_kernel(info_ref, *refs):
    @pl.when(info_ref[0] == 1)
    def _():
        prepare(info_ref, *refs)


def inner_kernel(info_ref, have_ref, *refs):
    @pl.when(info_ref[0] == 0)
    def _():
        prepare(info_ref, *refs)

    @pl.when(info_ref[0] == 1)
    def _():
        refs[5][...] = have_ref[...]


def own_work(info_ref, query_ref, key_ref, value_ref, cot_ref, up_ref, out_ref, proj_ref):
    refs = (query_ref, key_ref, value_ref, cot_ref)
    whole = causal(ROWS, ROWS, 0)
    half = causal(HALF, HALF, 0)
    nothing = jnp.zeros((HALF, HEAD), BF16)
    for start in range(SHIFTED, HEADS, BATCH):
        slots = range(start, start + BATCH)
        grads = attend([[ref[:, lanes_of(info_ref, slot)] for ref in refs] for slot in slots], whole)
        for slot, parts in zip(slots, grads):
            for block in range(3):
                out_ref[:, lanes_of(info_ref, slot, block)] = parts[block]
    for start in range(0, SHIFTED, BATCH):
        slots = range(start, start + BATCH)
        grads = attend([[ref[HALF:, lanes_of(info_ref, slot)] for ref in refs] for slot in slots], half)
        for slot, parts in zip(slots, grads):
            for block in range(3):
                out_ref[:HALF, lanes_of(info_ref, slot, block)] = nothing
                out_ref[HALF:, lanes_of(info_ref, slot, block)] = parts[block]
    total = jnp.zeros((ROWS, HEAD), F32)
    for block in range(3):
        columns = slice(block * WIDTH, (block + 1) * WIDTH)
        total = total + dot_last(out_ref[:, columns], spread(up_ref[:, columns], block))
    proj_ref[...] = total


def joint_work(
    info_ref, query_ref, key_ref, value_ref, cot_ref, come_ref, up_ref, have_ref, late_ref, proj_ref, back_ref, far_ref
):
    far_ref[...] = come_ref[:, 2 * SHIFTED * HEAD :]
    allowed = causal(ROWS, HALF, HALF)
    nothing = jnp.zeros((HALF, HEAD), BF16)
    width = SHIFTED * HEAD
    for start in range(0, SHIFTED, BATCH):
        slots = range(start, start + BATCH)
        parts = []
        for slot in slots:
            lanes = lanes_of(info_ref, slot)
            key, value = (
                jnp.concatenate([come_ref[:, place * HEAD : (place + 1) * HEAD], ref[:HALF, lanes]], axis=0)
                for place, ref in ((slot, key_ref), (SHIFTED + slot, value_ref))
            )
            parts.append([query_ref[:HALF, lanes], key, value, cot_ref[:HALF, lanes]])
        for slot, (dquery, dkey, dvalue) in zip(slots, attend(parts, allowed)):
            lanes = slice(slot * HEAD, (slot + 1) * HEAD)
            late_ref[:HALF, lanes] = dquery
            late_ref[HALF:, lanes] = nothing
            for block, grad in ((1, dkey), (2, dvalue)):
                lanes = slice(block * width + slot * HEAD, block * width + (slot + 1) * HEAD)
                late_ref[:HALF, lanes] = grad[HALF:]
                late_ref[HALF:, lanes] = grad[:HALF]
    total = jnp.zeros((ROWS, HEAD), F32)
    for block in range(3):
        up = jnp.concatenate([up_ref[:, lanes_of(info_ref, slot, block)] for slot in range(SHIFTED)], axis=1)
        total = total + dot_last(late_ref[:, block * width : (block + 1) * width], spread(up, block))
    proj_ref[...] = jnp.concatenate([have_ref[:HALF] + total[:HALF], have_ref[HALF:]], axis=0)
    back_ref[...] = total[HALF:]


def own_kernel(info_ref, *refs):
    @pl.when(info_ref[0] == 0)
    def _():
        own_work(info_ref, *refs)


def joint_kernel(info_ref, *refs):
    @pl.when(info_ref[0] == 0)
    def _():
        joint_work(info_ref, *refs)


def later_kernel(
    info_ref, query_ref, key_ref, value_ref, cot_ref, come_ref, up_ref, ready_ref, grads_ref, *refs
):
    del ready_ref
    refs, have_ref = refs[:-1], refs[-1]
    inputs = (info_ref, query_ref, key_ref, value_ref, cot_ref)

    @pl.when(info_ref[0] == 1)
    def _():
        own_work(*inputs, up_ref, grads_ref, have_ref)
        joint_work(*inputs, come_ref, up_ref, have_ref, *refs)


def accumulate(info_ref, grads_ref, late_ref, far_ref, low_ref, sums_ref):
    span = WIDTH // 4
    low = low_ref[...]
    far_low = jnp.concatenate([low[:HALF], far_ref[...]], axis=0)
    for block in range(3):
        right, far_right = (
            jnp.concatenate([item[:, block * RANK : (block + 1) * RANK]] * 4, axis=1) for item in (low, far_low)
        )
        for chunk in range(4 * block, 4 * block + 4):
            columns = slice(chunk * span, (chunk + 1) * span)
            sums_ref[columns, :] = dot_first(grads_ref[:, columns], right)
        for slot in range(SHIFTED):
            start = (block * SHIFTED + slot) * HEAD
            sums_ref[lanes_of(info_ref, slot, block), :] += dot_first(late_ref[:, start : start + HEAD], far_right)


def up_kernel(info_ref, *refs):
    parts, (low_ref, out_ref, sums_ref) = (refs[:3], refs[3:6]), refs[6:]
    for core in range(C):

        @pl.when(info_ref[0] == core)
        def _():
            accumulate(info_ref, *parts[core], low_ref, sums_ref)

    place = lax.broadcasted_iota(jnp.int32, (8, HEAD), 1) // RANK
    upper = lax.broadcasted_iota(jnp.int32, (8, HEAD), 0) < 4

    def tile(z, g, third):
        start = ((z * G + g) * 3 + third) * 8
        return sums_ref[start : start + 8, :]

    for g in range(G):
        for z in range(0, Z, 2):
            for c in range(C):
                pair = jnp.concatenate([tile(z, g, 2 * c), tile(z + 1, g, 2 * c)], axis=0)
                out_ref[c, g, z * 8 : z * 8 + 16, :] = pair.astype(BF16)
        middle = []
        for low_z in range(BAND):
            merged = tile(low_z, g, 1)
            for quarter in range(1, 4):
                merged = jnp.where(place == quarter, tile(BAND * quarter + low_z, g, 1), merged)
            middle.append(merged)
        swapped = [pltpu.roll(item, 4, 0) for item in middle]
        for c in range(C):
            rows = []
            for even in range(0, BAND, 2):
                if c == 0:
                    rows.append(jnp.where(upper, middle[even], swapped[even + 1]))
                else:
                    rows.append(jnp.where(upper, swapped[even], middle[even + 1]))
            out_ref[c, g, Z * 8 :, :] = jnp.concatenate(rows, axis=0).astype(BF16)


def down_kernel(info_ref, normed_ref, first_ref, later_ref, outer_ref, inner_ref, up_ref, mine_ref, other_ref):
    own = info_ref[0]
    total = jnp.where(own == 0, first_ref[...], later_ref[...])
    back = jnp.where(own == 0, inner_ref[...], outer_ref[...])
    total = jnp.concatenate([total[:HALF], total[HALF:] + back], axis=0).astype(BF16)
    lane = lax.broadcasted_iota(jnp.int32, (16, HEAD), 1)
    for z in range(0, Z, 2):
        part = dot_first(normed_ref[:, z * G * 16 : (z + 2) * G * 16], total)
        part = part.reshape(2, G, C, 8, HEAD)
        for g in range(G):
            pieces = []
            for c in range(C):
                down = jnp.concatenate([part[0, g, c], part[1, g, c]], axis=0)
                up = up_ref[c, g, z * 8 : z * 8 + 16, :]
                pieces.append(jnp.where(lane < 3 * RANK, down, up.astype(F32)).astype(BF16))
            start = g * PART + z * 8
            mine_ref[start : start + 16, :] = jnp.where(own == 0, pieces[0], pieces[1])
            other_ref[start : start + 16, :] = jnp.where(own == 0, pieces[1], pieces[0])
    for g in range(G):
        span = slice(g * PART + Z * 8, (g + 1) * PART)
        pieces = [up_ref[c, g, Z * 8 :, :] for c in range(C)]
        mine_ref[span, :] = jnp.where(own == 0, pieces[0], pieces[1])
        other_ref[span, :] = jnp.where(own == 0, pieces[1], pieces[0])


def middle_kernel(come_ref, out_ref):
    total = come_ref[0].astype(F32)
    for item in range(1, G):
        total = total + come_ref[item].astype(F32)
    for z in range(Z):
        start = Z * 8 + z % BAND // 2 * 8
        tiles = jnp.concatenate([total[z * 8 : z * 8 + 8], total[start : start + 8]], axis=0)
        out_ref[z] = tiles.astype(BF16)


def last_kernel(info_ref, come_ref, down_ref, up_ref):
    c, z = info_ref[0], info_ref[1]
    total = come_ref[0].astype(F32)
    for item in range(1, Z):
        total = total + come_ref[item].astype(F32)
    total = total * ADAPTER_SCALE
    upper, lower = total[:8], total[8:]
    down_ref[...] = upper[:, : 3 * RANK].astype(BF16)
    lower = pltpu.roll(lower, (3 - z // BAND) * RANK, 1)
    moved = lax.rem(z, 2) != c
    lower = jnp.where(moved, pltpu.roll(lower, 4, 0), lower)
    both = jnp.concatenate([upper, lower], axis=0)
    both = jnp.where(c == 1, pltpu.roll(both, 4, 0), both)
    up_ref[...] = both[:12, 3 * RANK :].astype(BF16)


def shape(dims, kind=BF16):
    return jax.ShapeDtypeStruct(dims, kind)


def prepare_call(body, name, info, extra, keys, values, normed, down):
    return call(
        body,
        name,
        (shape((HALF, (2 * SHIFTED + 1) * HEAD)), shape((ROWS, HEAD))),
        [SMEM] + [VMEM] * len(extra) + [HBM] * 4,
        130_000_000,
        3_000_000,
        limit=53,
        scratch_shapes=[
            pltpu.VMEM((2, HALF, WIDTH), BF16),
            pltpu.VMEM(normed.shape, BF16),
            pltpu.VMEM(down.shape, BF16),
            pltpu.SemaphoreType.DMA((2,)),
            pltpu.SemaphoreType.DMA((2, WIDE)),
        ],
    )(info, *extra, keys, values, normed, down)


OWN = (shape((ROWS, 3 * WIDTH)), shape((ROWS, HEAD), F32))
JOINT = (shape((ROWS, 3 * SHIFTED * HEAD)), shape((ROWS, HEAD), F32), shape((HALF, HEAD), F32), shape((HALF, HEAD)))


def own_call(info, *inputs):
    return call(own_kernel, "own_attention", OWN, [SMEM] + [VMEM] * 5, 2_000_000_000, 6_000_000)(info, *inputs)


def joint_call(info, *inputs):
    return call(joint_kernel, "joint_attention", JOINT, [SMEM] + [VMEM] * 7, 1_000_000_000, 4_000_000)(info, *inputs)


def later_call(info, *inputs):
    return call(
        later_kernel,
        "later_attention",
        (OWN[0], *JOINT),
        [SMEM] + [VMEM] * 7,
        3_000_000_000,
        8_000_000,
        scratch_shapes=[pltpu.VMEM((ROWS, HEAD), F32)],
    )(info, *inputs)


def up_call(info, *inputs):
    return call(
        up_kernel,
        "up_gradient",
        shape((C, G, PART, HEAD)),
        [SMEM] + [VMEM] * 7,
        1_000_000_000,
        6_000_000,
        scratch_shapes=[pltpu.VMEM((3 * WIDTH, HEAD), F32)],
    )(info, *inputs)


def down_call(info, *inputs):
    return call(
        down_kernel,
        "down_gradient",
        (shape((G * PART, HEAD)), shape((G * PART, HEAD))),
        [SMEM] + [VMEM] * 6,
        500_000_000,
        4_000_000,
    )(info, *inputs)


def middle_call(come):
    return call(middle_kernel, "middle_sum", shape((Z, 16, HEAD)), [VMEM], 1_000_000, 600_000)(come)


def last_call(info, come):
    return call(
        last_kernel, "last_sum", (shape((8, 3 * RANK)), shape((12, RANK))), [SMEM, VMEM], 100_000, 70_000
    )(info, come)


def per_device(normed, queries, keys, values, cotangent, down, up, order):
    normed, queries, keys, values, cotangent = (
        item[0] for item in (normed, queries, keys, values, cotangent)
    )
    ring = ("yh", "x", "c")
    count = 16
    ahead = [(item, (item + 1) % count) for item in range(count)]
    behind = [(item, (item - 1) % count) for item in range(count)]
    info = jnp.concatenate([jnp.stack([lax.axis_index("c"), lax.axis_index(FAR)]), order])
    sources = (keys, values, normed, down.T)
    inputs = (queries, keys, values, cotangent)
    send, low = prepare_call(outer_kernel, "outer_parts", info, (), *sources)
    outer = lax.ppermute(send, ring, ahead[1::2])
    send, low = prepare_call(inner_kernel, "inner_parts", info, (low,), *sources)
    inner = lax.ppermute(send, ring, ahead[::2])
    grads, have = own_call(info, *inputs, up)
    late, proj, back, far = joint_call(info, *inputs, outer, up, have)
    outer_back = lax.ppermute(back, ring, behind[::2])
    later = later_call(info, *inputs, inner, up, far)
    inner_back = lax.ppermute(later[3], ring, behind[1::2])
    up_part = up_call(info, grads, late, far, later[0], later[1], later[4], low)
    mine, other = down_call(info, normed, proj, later[2], outer_back, inner_back, up_part)
    other = lax.ppermute(other, "c", [(0, 1), (1, 0)])
    chip = (mine.astype(F32) + other.astype(F32)).astype(BF16)
    plane = lax.all_to_all(chip.reshape(G, PART, HEAD), NEAR, 0, 0)
    line = lax.all_to_all(middle_call(plane), FAR, 0, 0)
    down_grad, up_grad = last_call(info, line)
    return down_grad, up_grad.T


def solution(mesh):
    fine = Mesh(mesh.devices.reshape(16, 2, 2, 4, 2), ("z", "yl", "yh", "x", "c"))
    dp, seq = ("z", "yl"), ("yh", "x", "c")
    tokens = P(dp, seq, None)
    in_specs = (tokens,) * 5 + (P(),) * 3
    out_specs = (P(dp + seq, None), P(None, dp + seq))
    return jax.shard_map(per_device, mesh=fine, in_specs=in_specs, out_specs=out_specs, check_vma=False)
```

time: 82.6 us -> 74 us (0.90)
  blocking collectives: 26.2 us -> 46.4 us
  waiting for transfers between devices: 14.9 us -> 1.62 us
  starting transfers between devices: 19.6 us -> 8.72 us
  local copies, waits for them, and re-layouts: 3.28 us -> 0.04 us
  Pallas kernels: 17.1 us -> 15.2 us
    all_to_all x0 -> x1, blocking collectives: none -> 23.8 us  [per_device(): line = lax.all_to_all(middle_call(plane), FAR, 0, 0)]
    all_to_all x1 -> x0, waiting for transfers between devices: 12.8 us -> none  [per_device(): line = lax.all_to_all(middle_call(plane), FAR, 0, 0)]
    all_to_all x1 -> x0, starting transfers between devices: 10.5 us -> none  [per_device(): line = lax.all_to_all(middle_call(plane), FAR, 0, 0)]
    all_to_all x1, blocking collectives: 26.2 us -> 22.6 us  [per_device(): plane = lax.all_to_all(chip.reshape(G, PART, HEAD), NEAR, 0, 0)]
    unnamed x16 -> x12, local copies, waits for them, and re-layouts: 3.28 us -> 0.04 us
    pallas_call x4 -> x6, Pallas kernels: 14.3 us -> 12.4 us  [the longest x1 4.1 us: own_call(): call(own_kernel, 'own_attention', OWN, [SMEM] + [VMEM] * 5, 2000000000, 6...]
    ppermute x2 -> x4, starting transfers between devices: 5.56 us -> 5.69 us  [the longest x1 1.82 us: per_device(): inner = lax.ppermute(send, ring, ahead[::2])]
  transfers between devices with their start and end apart: 4 -> 5, of which waited for: 3 -> 1; matrix products, arithmetic and copies ran while one was open for 0% -> 0% of each run, Pallas kernels for 8% -> 16%
where the time goes in v3:
time: 74 us; the launch traced here: 73.7 us
  blocking collectives  46.4 us (63%)
  Pallas kernels  15.2 us (21%)
  starting transfers between devices  8.72 us (12%)
  waiting for transfers between devices  1.62 us (2%)
  other arithmetic  0.89 us (1%)
  between operations  0.86 us (1%)
    all_to_all x1, blocking collectives, per_device(): line = lax.all_to_all(middle_call(plane), FAR, 0, 0)  23.8 us
    all_to_all x1, blocking collectives, per_device(): plane = lax.all_to_all(chip.reshape(G, PART, HEAD), NEAR, 0, 0)  22.6 us
    pallas_call x1, Pallas kernels, own_call(): call(own_kernel, 'own_attention', OWN, [SMEM] + [VMEM] * 5, 2000000000, 6...  4.1 us
    pallas_call x2, Pallas kernels, prepare_call(): call(body, name, (shape((HALF, (2 * SHIFTED + 1) * HEAD)), shape((ROWS, H...  3.7 us
    ppermute x1, starting transfers between devices, per_device(): other = lax.ppermute(other, 'c', [(0, 1), (1, 0)])  3.02 us
    pallas_call x1, Pallas kernels, up_call(): call(up_kernel, 'up_gradient', shape((C, G, PART, HEAD)), [SMEM] + [VMEM]...  2.27 us
    ppermute x1, starting transfers between devices, per_device(): inner = lax.ppermute(send, ring, ahead[::2])  1.82 us
    pallas_call x1, Pallas kernels, joint_call(): call(joint_kernel, 'joint_attention', JOINT, [SMEM] + [VMEM] * 7, 1000000...  1.78 us
  transfers between devices with their start and end apart: 5, of which 1 were waited for; matrix products, arithmetic and copies ran while one was open for 0% of the time, Pallas kernels for 16%

profile of v3, /device:TPU:2, one launch (start us, length us, event | category | flops | bytes accessed | tf_op | source)
XLA Modules:
  0.0 73.7 jit_solution(10919475526251284180)
XLA Ops:
  0.6 0.7 pad_add_fusion.info_ref
  1.4 0.6 outer_parts.1
  2.0 1.3 %collective-permute-start = (bf16[80,2176]{1,0:T(8,128)(2,1)S(1)}, bf16[80,2176]{1,0:T(8,128)(2,1)S(1)}, u32[]{:S(2)}, u32[]{:S(2)}) collective-permute-start(bf16[80,2176]{1,0:T(8,128)(2,1)S(1)} %get-tuple-element.21), channel_id=1, source_target_pairs={{1,2},{3,4},{5,6},{7,8},{9,10},{11,12},{13,14},{15,0},{17,18},{19,... | collective-permute-start | bytes 1044488 | tf_op jit(solution)/shard_map/ppermute | solution.py:418
  3.3 0.0 copy-start.1
  3.3 0.0 copy-start.2
  3.3 0.0 copy-start.3
  3.3 0.0 copy-start.4
  3.3 0.0 copy-start.5
  3.3 3.1 %inner_parts.1 = (bf16[80,2176]{1,0:T(8,128)(2,1)S(1)}, bf16[160,128]{1,0:T(8,128)(2,1)S(1)}) custom-call(s32[18]{0:T(128)S(1)} %pad_add_fusion.info_ref, bf16[160,128]{1,0:T(8,128)(2,1)S(1)} %get-tuple-element.24.have_ref, bf16[160,2048]{1,0:T(8,128)(2,1)} %bitcast.14, bf16[160,2048]{1,0:T(8,128)(2,1)} %bitcast.19, bf16[160,4096]{1,0:T(8,128)(2,1)} %bitcast.11, ...), custom_call_target="tpu_custom_call" | custom-call | flops 130000000 | bytes 3000000 | tf_op jit(solution)/shard_map/inner_parts/pallas_call | solution.py:331
  6.4 1.8 %collective-permute-start.1 = (bf16[80,2176]{1,0:T(8,128)(2,1)S(1)}, bf16[80,2176]{1,0:T(8,128)(2,1)S(1)}, u32[]{:S(2)}, u32[]{:S(2)}) collective-permute-start(bf16[80,2176]{1,0:T(8,128)(2,1)S(1)} %get-tuple-element.25), channel_id=1, source_target_pairs={{0,1},{2,3},{4,5},{6,7},{8,9},{10,11},{12,13},{14,15},{16,17},{18,... | collective-permute-start | bytes 1044488 | tf_op jit(solution)/shard_map/ppermute | solution.py:420
  8.3 0.0 copy-done.1
  8.3 0.0 copy-done.2
  8.3 0.0 copy-done.3
  8.3 0.0 copy-done.4
  8.3 0.0 copy-done.5
  8.3 4.1 %own_attention.1 = (bf16[160,6144]{1,0:T(8,128)(2,1)S(1)}, f32[160,128]{1,0:T(8,128)S(1)}) custom-call(s32[18]{0:T(128)S(1)} %pad_add_fusion.info_ref, bf16[160,2048]{1,0:T(8,128)(2,1)S(1)} %bitcast.23, bf16[160,2048]{1,0:T(8,128)(2,1)S(1)} %bitcast.15, bf16[160,2048]{1,0:T(8,128)(2,1)S(1)} %bitcast.20, bf16[160,2048]{1,0:T(8,128)(2,1)S(1)} %bitcast.26, ...), custom_call_target="tpu_custom_call" | custom-call | flops 2000000000 | bytes 6000000 | tf_op jit(solution)/shard_map/own_attention/pallas_call | solution.py:354
  12.4 0.0 collective-permute-done.refs_4_
  12.4 1.8 %joint_attention.1 = (bf16[160,3072]{1,0:T(8,128)(2,1)S(1)}, f32[160,128]{1,0:T(8,128)S(1)}, f32[80,128]{1,0:T(8,128)S(1)}, bf16[80,128]{1,0:T(8,128)(2,1)S(1)}) custom-call(s32[18]{0:T(128)S(1)} %pad_add_fusion.info_ref, bf16[160,2048]{1,0:T(8,128)(2,1)S(1)} %bitcast.24, bf16[160,2048]{1,0:T(8,128)(2,1)S(1)} %bitcast.16, bf16[160,2048]{1,0:T(8,128)(2,1)S(1)} %bitcast.21, ...), custom_call_target="tpu_custom_call" | custom-call | flops 1000000000 | bytes 4000000 | tf_op jit(solution)/shard_map/joint_attention/pallas_call | solution.py:358
  14.2 1.3 %collective-permute-start.2 = (f32[80,128]{1,0:T(8,128)S(1)}, f32[80,128]{1,0:T(8,128)S(1)}, u32[]{:S(2)}, u32[]{:S(2)}) collective-permute-start(f32[80,128]{1,0:T(8,128)S(1)} %get-tuple-element.28), channel_id=1, source_target_pairs={{0,15},{2,1},{4,3},{6,5},{8,7},{10,9},{12,11},{14,13},{16,31},{18,... | collective-permute-start | bytes 122888 | tf_op jit(solution)/shard_map/ppermute | solution.py:423
  15.5 0.0 collective-permute-done.1.come_ref
  15.5 0.6 later_attention.1
  16.1 1.3 %collective-permute-start.3 = (f32[80,128]{1,0:T(8,128)S(1)}, f32[80,128]{1,0:T(8,128)S(1)}, u32[]{:S(2)}, u32[]{:S(2)}) collective-permute-start(f32[80,128]{1,0:T(8,128)S(1)} %get-tuple-element.29), channel_id=1, source_target_pairs={{1,0},{3,2},{5,4},{7,6},{9,8},{11,10},{13,12},{15,14},{17,16},{19,... | collective-permute-start | bytes 122888 | tf_op jit(solution)/shard_map/ppermute | solution.py:425
  17.4 0.0 copy-start
  17.4 2.3 %up_gradient.1.up_ref = bf16[2,16,144,128]{3,2,1,0:T(8,128)(2,1)S(1)} custom-call(s32[18]{0:T(128)S(1)} %pad_add_fusion.info_ref, bf16[160,6144]{1,0:T(8,128)(2,1)S(1)} %get-tuple-element.30.refs_0_, bf16[160,3072]{1,0:T(8,128)(2,1)S(1)} %get-tuple-element.31.refs_1_, bf16[80,128]{1,0:T(8,128)(2,1)S(1)} %get-tuple-element.26.ready_ref.refs_2_, ...), custom_call_target="tpu_custom_call" | custom-call | flops 1000000000 | bytes 6000000 | tf_op jit(solution)/shard_map/up_gradient/pallas_call | solution.py:374
  19.7 0.0 collective-permute-done.2.outer_ref
  19.7 0.0 collective-permute-done.3.inner_ref
  19.7 0.0 copy-done
  19.7 1.4 %down_gradient.1 = (bf16[2304,128]{1,0:T(8,128)(2,1)S(1)}, bf16[2304,128]{1,0:T(8,128)(2,1)S(1)}) custom-call(s32[18]{0:T(128)S(1)} %pad_add_fusion.info_ref, bf16[160,4096]{1,0:T(8,128)(2,1)S(1)} %bitcast.12, f32[160,128]{1,0:T(8,128)S(1)} %get-tuple-element.23.first_ref, f32[160,128]{1,0:T(8,128)S(1)} %get-tuple-element.27.later_ref, ...), custom_call_target="tpu_custom_call" | custom-call | flops 500000000 | bytes 4000000 | tf_op jit(solution)/shard_map/down_gradient/pallas_call | solution.py:386
  21.1 3.0 %collective-permute-start.4 = (bf16[2304,128]{1,0:T(8,128)(2,1)S(1)}, bf16[2304,128]{1,0:T(8,128)(2,1)S(1)}, u32[]{:S(2)}, u32[]{:S(2)}) collective-permute-start(bf16[2304,128]{1,0:T(8,128)(2,1)S(1)} %get-tuple-element.37), channel_id=1, source_target_pairs={{0,1},{1,0},{2,3},{3,2},{4,5},{5,4},{6,7},{7,6},{8,9},{9,8},{10,11... | collective-permute-start | bytes 1769480 | tf_op jit(solution)/shard_map/ppermute | solution.py:428
  24.1 1.6 %collective-permute-done.4 = bf16[2304,128]{1,0:T(8,128)(2,1)S(1)} collective-permute-done((bf16[2304,128]{1,0:T(8,128)(2,1)S(1)}, bf16[2304,128]{1,0:T(8,128)(2,1)S(1)}, u32[]{:S(2)}, u32[]{:S(2)}) %collective-permute-start.4) | collective-permute-done | bytes 589856 | tf_op jit(solution)/shard_map/ppermute | solution.py:428
  25.7 0.2 add_convert_fusion
  25.9 22.6 %all_to_all.10.come_ref = bf16[16,144,128]{2,1,0:T(8,128)(2,1)S(1)} all-to-all(bf16[16,144,128]{2,1,0:T(8,128)(2,1)S(1)} %bitcast.31), channel_id=1, replica_groups=mesh['z'=16,'yl'=2,'yh'=2,'x'=4,'c'=2] {'yl','yh','x'}, dimensions={0} | all-to-all | bytes 1179648 | tf_op jit(solution)/shard_map/all_to_all | solution.py:430
  48.5 0.1 middle_sum.1
  48.6 23.8 %all_to_all.11.come_ref = bf16[16,16,128]{2,1,0:T(8,128)(2,1)S(1)} all-to-all(bf16[16,16,128]{2,1,0:T(8,128)(2,1)S(1)} %middle_sum.1), channel_id=1, replica_groups=mesh['z'=16,'yl'=2,'yh'=2,'x'=4,'c'=2] {'z'}, dimensions={0} | all-to-all | bytes 131072 | tf_op jit(solution)/shard_map/all_to_all | solution.py:431
  72.4 1.3 %last_sum.1 = (bf16[8,96]{1,0:T(8,128)(2,1)}, bf16[12,32]{1,0:T(8,128)(2,1)}) custom-call(s32[18]{0:T(128)S(1)} %pad_add_fusion.info_ref, bf16[16,16,128]{2,1,0:T(8,128)(2,1)S(1)} %all_to_all.11.come_ref), custom_call_target="tpu_custom_call" | custom-call | flops 100000 | bytes 70000 | tf_op jit(solution)/shard_map/last_sum/pallas_call | solution.py:401
Async XLA Ops:
  2.0 10.4 %collective-permute-start = (bf16[80,2176]{1,0:T(8,128)(2,1)S(1)}, bf16[80,2176]{1,0:T(8,128)(2,1)S(1)}, u32[]{:S(2)}, u32[]{:S(2)}) collective-permute-start(bf16[80,2176]{1,0:T(8,128)(2,1)S(1)} %get-tuple-element.21), channel_id=1, source_target_pairs={{1,2},{3,4},{5,6},{7,8},{9,10},{11,12},{13,14},{15,0},{17,18},{19,... | collective-permute-start | bytes 1044488 | tf_op jit(solution)/shard_map/ppermute | solution.py:418
  3.3 5.0 %copy-start.1 = (bf16[1,160,2048]{2,1,0:T(8,128)(2,1)S(1)}, bf16[1,160,2048]{2,1,0:T(8,128)(2,1)}, u32[]{:S(2)}) copy-start(bf16[1,160,2048]{2,1,0:T(8,128)(2,1)} %param.10) | copy-start | bytes 1966084
  3.3 5.0 %copy-start.2 = (bf16[1,160,2048]{2,1,0:T(8,128)(2,1)S(1)}, bf16[1,160,2048]{2,1,0:T(8,128)(2,1)}, u32[]{:S(2)}) copy-start(bf16[1,160,2048]{2,1,0:T(8,128)(2,1)} %param.11) | copy-start | bytes 1966084
  3.3 5.0 %copy-start.3 = (bf16[1,160,2048]{2,1,0:T(8,128)(2,1)S(1)}, bf16[1,160,2048]{2,1,0:T(8,128)(2,1)}, u32[]{:S(2)}) copy-start(bf16[1,160,2048]{2,1,0:T(8,128)(2,1)} %param.9) | copy-start | bytes 1966084
  3.3 5.0 %copy-start.4 = (bf16[1,160,2048]{2,1,0:T(8,128)(2,1)S(1)}, bf16[1,160,2048]{2,1,0:T(8,128)(2,1)}, u32[]{:S(2)}) copy-start(bf16[1,160,2048]{2,1,0:T(8,128)(2,1)} %param.12) | copy-start | bytes 1966084
  3.3 5.0 %copy-start.5 = (bf16[32,6144]{1,0:T(8,128)(2,1)S(1)}, bf16[32,6144]{1,0:T(8,128)(2,1)}, u32[]{:S(2)}) copy-start(bf16[32,6144]{1,0:T(8,128)(2,1)} %up_ref.1) | copy-start | bytes 1179652
  6.4 9.1 %collective-permute-start.1 = (bf16[80,2176]{1,0:T(8,128)(2,1)S(1)}, bf16[80,2176]{1,0:T(8,128)(2,1)S(1)}, u32[]{:S(2)}, u32[]{:S(2)}) collective-permute-start(bf16[80,2176]{1,0:T(8,128)(2,1)S(1)} %get-tuple-element.25), channel_id=1, source_target_pairs={{0,1},{2,3},{4,5},{6,7},{8,9},{10,11},{12,13},{14,15},{16,17},{18,... | collective-permute-start | bytes 1044488 | tf_op jit(solution)/shard_map/ppermute | solution.py:420
  14.2 5.5 %collective-permute-start.2 = (f32[80,128]{1,0:T(8,128)S(1)}, f32[80,128]{1,0:T(8,128)S(1)}, u32[]{:S(2)}, u32[]{:S(2)}) collective-permute-start(f32[80,128]{1,0:T(8,128)S(1)} %get-tuple-element.28), channel_id=1, source_target_pairs={{0,15},{2,1},{4,3},{6,5},{8,7},{10,9},{12,11},{14,13},{16,31},{18,... | collective-permute-start | bytes 122888 | tf_op jit(solution)/shard_map/ppermute | solution.py:423
  16.1 3.6 %collective-permute-start.3 = (f32[80,128]{1,0:T(8,128)S(1)}, f32[80,128]{1,0:T(8,128)S(1)}, u32[]{:S(2)}, u32[]{:S(2)}) collective-permute-start(f32[80,128]{1,0:T(8,128)S(1)} %get-tuple-element.29), channel_id=1, source_target_pairs={{1,0},{3,2},{5,4},{7,6},{9,8},{11,10},{13,12},{15,14},{17,16},{19,... | collective-permute-start | bytes 122888 | tf_op jit(solution)/shard_map/ppermute | solution.py:425
  17.4 2.3 %copy-start = (bf16[1,160,4096]{2,1,0:T(8,128)(2,1)S(1)}, bf16[1,160,4096]{2,1,0:T(8,128)(2,1)}, u32[]{:S(2)}) copy-start(bf16[1,160,4096]{2,1,0:T(8,128)(2,1)} %param.8) | copy-start | bytes 3932164
  21.1 4.6 %collective-permute-start.4 = (bf16[2304,128]{1,0:T(8,128)(2,1)S(1)}, bf16[2304,128]{1,0:T(8,128)(2,1)S(1)}, u32[]{:S(2)}, u32[]{:S(2)}) collective-permute-start(bf16[2304,128]{1,0:T(8,128)(2,1)S(1)} %get-tuple-element.37), channel_id=1, source_target_pairs={{0,1},{1,0},{2,3},{3,2},{4,5},{5,4},{6,7},{7,6},{8,9},{9,8},{10,11... | collective-permute-start | bytes 1769480 | tf_op jit(solution)/shard_map/ppermute | solution.py:428

commit v4 on v3

v4 whole, which is shorter than its diff:
```python
import jax
import jax.numpy as jnp
from jax import lax
from jax.experimental import pallas as pl
from jax.experimental.pallas import tpu as pltpu
from jax.sharding import Mesh
from jax.sharding import PartitionSpec as P

HEAD = 128
ROWS = 160
HALF = 80
HEADS = 16
SHIFTED = 8
WIDTH = HEADS * HEAD
MODEL = 4096
RANK = 32
SCALE = HEAD ** -0.5
ADAPTER_SCALE = 0.25
NEAR, FAR = ("yl", "yh", "x"), ("z",)
Z, G, C = 16, 16, 2
BAND = Z // 4
WIDE = 2
NARROW = SHIFTED * HEAD
PART = Z * 8 + BAND * 4

BF16, F32 = jnp.bfloat16, jnp.float32
VMEM = pl.BlockSpec(memory_space=pltpu.VMEM)
HBM = pl.BlockSpec(memory_space=pltpu.HBM)
ANY = pl.BlockSpec(memory_space=pl.ANY)
ORDER = (pltpu.SMEM((HEADS,), jnp.int32), pltpu.SemaphoreType.DMA)


def call(body, name, out_shape, in_specs, flops, size, limit=32, out_specs=None, **rest):
    return pl.pallas_call(
        body,
        name=name,
        out_shape=out_shape,
        in_specs=in_specs,
        out_specs=out_specs or jax.tree.map(lambda _: VMEM, out_shape),
        compiler_params=pltpu.CompilerParams(vmem_limit_bytes=limit * 1024 * 1024),
        cost_estimate=pl.CostEstimate(flops=flops, bytes_accessed=size, transcendentals=0),
        **rest,
    )


def dot(left, right):
    return jnp.dot(left, right, preferred_element_type=F32)


def dot_last(left, right):
    return lax.dot_general(left, right, (((1,), (1,)), ((), ())), preferred_element_type=F32)


def dot_first(left, right):
    return lax.dot_general(left, right, (((0,), (0,)), ((), ())), preferred_element_type=F32)


def attend(parts, allowed):
    queries, keys, values, cotangents = zip(*parts)
    scores = [jnp.where(allowed, dot_last(key, query), -jnp.inf) for query, key in zip(queries, keys)]
    dprobs = [dot_last(value, cotangent) for value, cotangent in zip(values, cotangents)]
    tops = [jnp.max(item, axis=0, keepdims=True) for item in scores]
    powers = [jnp.exp((item - top) * SCALE) for item, top in zip(scores, tops)]
    probs = [item * (1.0 / jnp.sum(item, axis=0, keepdims=True)) for item in powers]
    weights = [item.astype(BF16) for item in probs]
    dvalues = [dot(weight, cotangent).astype(BF16) for weight, cotangent in zip(weights, cotangents)]
    deltas = [
        jnp.sum(weight.astype(F32) * dprob, axis=0, keepdims=True) for weight, dprob in zip(weights, dprobs)
    ]
    dscores = [
        (prob * (dprob - delta)).astype(BF16) for prob, dprob, delta in zip(probs, dprobs, deltas)
    ]
    dkeys = [(dot(dscore, query) * SCALE).astype(BF16) for dscore, query in zip(dscores, queries)]
    dqueries = [(dot_first(dscore, key) * SCALE).astype(BF16) for dscore, key in zip(dscores, keys)]
    return list(zip(dqueries, dkeys, dvalues))


def causal(keys, queries, ahead):
    row = lax.broadcasted_iota(jnp.int32, (keys, queries), 0)
    column = lax.broadcasted_iota(jnp.int32, (keys, queries), 1)
    return row <= column + ahead


def lanes_of(order_ref, slot, block=0):
    return pl.ds(pl.multiple_of(order_ref[slot] * HEAD + block * WIDTH, HEAD), HEAD)


def narrow_lanes(slot, block=0):
    return slice(block * NARROW + slot * HEAD, block * NARROW + (slot + 1) * HEAD)


def fetch(source_ref, order_ref, sem):
    copy = pltpu.make_async_copy(source_ref, order_ref, sem)
    copy.start()
    return copy


def prepare(
    source_ref,
    key_ref,
    value_ref,
    normed_ref,
    down_ref,
    send_ref,
    low_ref,
    pair_own,
    normed_own,
    down_own,
    pair_sems,
    wide_sems,
    order_ref,
    order_sem,
):
    order_copy = fetch(source_ref, order_ref, order_sem)
    pair_copies, wide_copies = [], []
    for item, source in enumerate((key_ref, value_ref)):
        copy = pltpu.make_async_copy(source.at[HALF:], pair_own.at[item], pair_sems.at[item])
        copy.start()
        pair_copies.append(copy)
    span = MODEL // WIDE
    for part in range(WIDE):
        lanes = slice(part * span, (part + 1) * span)
        for item, (source, target) in enumerate(((normed_ref, normed_own), (down_ref, down_own))):
            copy = pltpu.make_async_copy(source.at[:, lanes], target.at[:, lanes], wide_sems.at[item, part])
            copy.start()
            wide_copies.append(copy)
    order_copy.wait()
    for item in range(2):
        pair_copies[item].wait()
        for slot in range(SHIFTED):
            place = item * SHIFTED + slot
            send_ref[:, place * HEAD : (place + 1) * HEAD] = pair_own[item, :, lanes_of(order_ref, slot)]
    low = jnp.zeros((ROWS, 3 * RANK), F32)
    for part in range(WIDE):
        lanes = slice(part * span, (part + 1) * span)
        for copy in wide_copies[2 * part : 2 * part + 2]:
            copy.wait()
        low = low + dot_last(normed_own[:, lanes], down_own[:, lanes])
    low = jnp.concatenate([low.astype(BF16), jnp.zeros((ROWS, HEAD - 3 * RANK), BF16)], axis=1)
    low_ref[...] = low
    send_ref[:, 2 * SHIFTED * HEAD :] = low[HALF:]


def outer_kernel(*refs):
    @pl.when(lax.axis_index("c") == 1)
    def _():
        prepare(*refs)


def inner_kernel(have_ref, *refs):
    core = lax.axis_index("c")

    @pl.when(core == 0)
    def _():
        prepare(*refs)

    @pl.when(core == 1)
    def _():
        refs[6][...] = have_ref[...]


def project(order_ref, grads_ref, up_ref, slots):
    total = jnp.zeros((grads_ref.shape[0], HEAD), F32)
    for block in range(3):
        up = jnp.concatenate([up_ref[:, lanes_of(order_ref, slot, block)] for slot in slots], axis=1)
        parts = [up if place == block else jnp.zeros_like(up) for place in range(4)]
        columns = slice(block * NARROW, (block + 1) * NARROW)
        total = total + dot_last(grads_ref[:, columns], jnp.concatenate(parts, axis=0))
    return total


def half_work(order_ref, refs, up_ref, half_ref, half_proj_ref):
    slots = range(SHIFTED)
    parts = [[ref[HALF:, lanes_of(order_ref, slot)] for ref in refs] for slot in slots]
    for slot, grads in zip(slots, attend(parts, causal(HALF, HALF, 0))):
        for block in range(3):
            half_ref[:, narrow_lanes(slot, block)] = grads[block]
    half_proj_ref[...] = project(order_ref, half_ref, up_ref, slots)


def plain_work(order_ref, refs, up_ref, plain_ref, plain_proj_ref):
    slots = range(SHIFTED, HEADS)
    parts = [[ref[:, lanes_of(order_ref, slot)] for ref in refs] for slot in slots]
    for slot, grads in zip(slots, attend(parts, causal(ROWS, ROWS, 0))):
        for block in range(3):
            plain_ref[:, narrow_lanes(slot - SHIFTED, block)] = grads[block]
    plain_proj_ref[...] = project(order_ref, plain_ref, up_ref, slots)


def joint_work(
    order_ref, refs, come_ref, up_ref, plain_proj_ref, half_proj_ref, late_ref, proj_ref, back_ref, far_ref
):
    query_ref, key_ref, value_ref, cot_ref = refs
    far_ref[...] = come_ref[:, 2 * SHIFTED * HEAD :]
    nothing = jnp.zeros((HALF, HEAD), BF16)
    slots = range(SHIFTED)
    parts = []
    for slot in slots:
        lanes = lanes_of(order_ref, slot)
        key, value = (
            jnp.concatenate([come_ref[:, place * HEAD : (place + 1) * HEAD], ref[:HALF, lanes]], axis=0)
            for place, ref in ((slot, key_ref), (SHIFTED + slot, value_ref))
        )
        parts.append([query_ref[:HALF, lanes], key, value, cot_ref[:HALF, lanes]])
    for slot, (dquery, dkey, dvalue) in zip(slots, attend(parts, causal(ROWS, HALF, HALF))):
        late_ref[:HALF, narrow_lanes(slot)] = dquery
        late_ref[HALF:, narrow_lanes(slot)] = nothing
        for block, grad in ((1, dkey), (2, dvalue)):
            late_ref[:HALF, narrow_lanes(slot, block)] = grad[HALF:]
            late_ref[HALF:, narrow_lanes(slot, block)] = grad[:HALF]
    total = project(order_ref, late_ref, up_ref, slots)
    plain = plain_proj_ref[...]
    proj_ref[...] = jnp.concatenate([plain[:HALF] + total[:HALF], plain[HALF:] + half_proj_ref[...]], axis=0)
    back_ref[...] = total[HALF:]


def own_kernel(*refs):
    source_ref, inputs, up_ref = refs[0], refs[1:5], refs[5]
    half_refs, plain_refs, (order_ref, order_sem) = refs[6:8], refs[8:10], refs[10:]
    fetch(source_ref, order_ref, order_sem).wait()

    @pl.when(lax.axis_index("c") == 0)
    def _():
        plain_work(order_ref, inputs, up_ref, *plain_refs)

    half_work(order_ref, inputs, up_ref, *half_refs)


def joint_kernel(*refs):
    source_ref, inputs, rest, (order_ref, order_sem) = refs[0], refs[1:5], refs[5:-2], refs[-2:]

    @pl.when(lax.axis_index("c") == 0)
    def _():
        fetch(source_ref, order_ref, order_sem).wait()
        joint_work(order_ref, inputs, *rest)


def later_kernel(*refs):
    source_ref, inputs, come_ref, up_ref, half_proj_ref = refs[0], refs[1:5], refs[5], refs[6], refs[7]
    plain_ref, outs, (plain_proj_ref, order_ref, order_sem) = refs[9], refs[10:14], refs[14:]

    @pl.when(lax.axis_index("c") == 1)
    def _():
        fetch(source_ref, order_ref, order_sem).wait()
        plain_work(order_ref, inputs, up_ref, plain_ref, plain_proj_ref)
        joint_work(order_ref, inputs, come_ref, up_ref, plain_proj_ref, half_proj_ref, *outs)


def accumulate(order_ref, order_copy, plain_ref, late_ref, far_ref, half_ref, low_ref, sums_ref):
    low = low_ref[...]
    late_low = jnp.concatenate([low[:HALF], far_ref[...], low[HALF:]], axis=0)
    rights = [
        [jnp.concatenate([item[:, block * RANK : (block + 1) * RANK]] * 4, axis=1) for block in range(3)]
        for item in (low, late_low)
    ]
    order_copy.wait()
    for block in range(3):
        for slot in range(SHIFTED):
            lanes = narrow_lanes(slot, block)
            sums_ref[lanes_of(order_ref, SHIFTED + slot, block), :] = dot_first(plain_ref[:, lanes], rights[0][block])
            left = jnp.concatenate([late_ref[:, lanes], half_ref[:, lanes]], axis=0)
            sums_ref[lanes_of(order_ref, slot, block), :] = dot_first(left, rights[1][block])


def up_kernel(*refs):
    source_ref, parts, half_ref, low_ref = refs[0], (refs[1:4], refs[4:7]), refs[7], refs[8]
    out_ref, sums_ref, order_ref, order_sem = refs[9:]
    order_copy = fetch(source_ref, order_ref, order_sem)
    for core in range(C):

        @pl.when(lax.axis_index("c") == core)
        def _():
            accumulate(order_ref, order_copy, *parts[core], half_ref, low_ref, sums_ref)

    place = lax.broadcasted_iota(jnp.int32, (8, HEAD), 1) // RANK
    upper = lax.broadcasted_iota(jnp.int32, (8, HEAD), 0) < 4

    def tile(z, g, third):
        start = ((z * G + g) * 3 + third) * 8
        return sums_ref[start : start + 8, :]

    for g in range(G):
        for z in range(0, Z, 2):
            for c in range(C):
                pair = jnp.concatenate([tile(z, g, 2 * c), tile(z + 1, g, 2 * c)], axis=0)
                out_ref[c, g, z * 8 : z * 8 + 16, :] = pair.astype(BF16)
        middle = []
        for low_z in range(BAND):
            merged = tile(low_z, g, 1)
            for quarter in range(1, 4):
                merged = jnp.where(place == quarter, tile(BAND * quarter + low_z, g, 1), merged)
            middle.append(merged)
        swapped = [pltpu.roll(item, 4, 0) for item in middle]
        for c in range(C):
            rows = []
            for even in range(0, BAND, 2):
                if c == 0:
                    rows.append(jnp.where(upper, middle[even], swapped[even + 1]))
                else:
                    rows.append(jnp.where(upper, swapped[even], middle[even + 1]))
            out_ref[c, g, Z * 8 :, :] = jnp.concatenate(rows, axis=0).astype(BF16)


def down_kernel(normed_ref, first_ref, later_ref, outer_ref, inner_ref, up_ref, mine_ref, other_ref):
    own = lax.axis_index("c")
    total = jnp.where(own == 0, first_ref[...], later_ref[...])
    back = jnp.where(own == 0, inner_ref[...], outer_ref[...])
    total = jnp.concatenate([total[:HALF], total[HALF:] + back], axis=0).astype(BF16)
    lane = lax.broadcasted_iota(jnp.int32, (16, HEAD), 1)
    for z in range(0, Z, 2):
        part = dot_first(normed_ref[:, z * G * 16 : (z + 2) * G * 16], total)
        part = part.reshape(2, G, C, 8, HEAD)
        for g in range(G):
            pieces = []
            for c in range(C):
                down = jnp.concatenate([part[0, g, c], part[1, g, c]], axis=0)
                up = up_ref[c, g, z * 8 : z * 8 + 16, :]
                pieces.append(jnp.where(lane < 3 * RANK, down, up.astype(F32)).astype(BF16))
            start = g * PART + z * 8
            mine_ref[start : start + 16, :] = jnp.where(own == 0, pieces[0], pieces[1])
            other_ref[start : start + 16, :] = jnp.where(own == 0, pieces[1], pieces[0])
    for g in range(G):
        span = slice(g * PART + Z * 8, (g + 1) * PART)
        pieces = [up_ref[c, g, Z * 8 :, :] for c in range(C)]
        mine_ref[span, :] = jnp.where(own == 0, pieces[0], pieces[1])
        other_ref[span, :] = jnp.where(own == 0, pieces[1], pieces[0])


def middle_kernel(come_ref, out_ref):
    total = come_ref[0].astype(F32)
    for item in range(1, G):
        total = total + come_ref[item].astype(F32)
    for z in range(Z):
        start = Z * 8 + z % BAND // 2 * 8
        tiles = jnp.concatenate([total[z * 8 : z * 8 + 8], total[start : start + 8]], axis=0)
        out_ref[z] = tiles.astype(BF16)


def last_kernel(come_ref, down_ref, up_ref):
    c, z = lax.axis_index("c"), lax.axis_index(FAR)
    total = come_ref[0].astype(F32)
    for item in range(1, Z):
        total = total + come_ref[item].astype(F32)
    total = total * ADAPTER_SCALE
    upper, lower = total[:8], total[8:]
    down_ref[...] = upper[:, : 3 * RANK].astype(BF16)
    lower = pltpu.roll(lower, (3 - z // BAND) * RANK, 1)
    moved = lax.rem(z, 2) != c
    lower = jnp.where(moved, pltpu.roll(lower, 4, 0), lower)
    both = jnp.concatenate([upper, lower], axis=0)
    both = jnp.where(c == 1, pltpu.roll(both, 4, 0), both)
    up_ref[...] = both[:12, 3 * RANK :].astype(BF16)


def shape(dims, kind=BF16):
    return jax.ShapeDtypeStruct(dims, kind)


def prepare_call(body, name, extra, order, keys, values, normed, down):
    return call(
        body,
        name,
        (shape((HALF, (2 * SHIFTED + 1) * HEAD)), shape((ROWS, HEAD))),
        [VMEM] * len(extra) + [ANY] + [HBM] * 4,
        130_000_000,
        3_000_000,
        limit=53,
        scratch_shapes=[
            pltpu.VMEM((2, HALF, WIDTH), BF16),
            pltpu.VMEM(normed.shape, BF16),
            pltpu.VMEM(down.shape, BF16),
            pltpu.SemaphoreType.DMA((2,)),
            pltpu.SemaphoreType.DMA((2, WIDE)),
            *ORDER,
        ],
    )(*extra, order, keys, values, normed, down)


PLAIN = (shape((ROWS, 3 * NARROW)), shape((ROWS, HEAD), F32))
HALVES = (shape((HALF, 3 * NARROW)), shape((HALF, HEAD), F32))
JOINT = (shape((ROWS, 3 * NARROW)), shape((ROWS, HEAD), F32), shape((HALF, HEAD), F32), shape((HALF, HEAD)))


def work_call(body, name, out_shape, inputs, flops, scratch=()):
    return call(
        body,
        name,
        out_shape,
        [ANY] + [VMEM] * (len(inputs) - 1),
        flops,
        6_000_000,
        scratch_shapes=[*scratch, *ORDER],
    )(*inputs)


def down_call(*inputs):
    return call(
        down_kernel,
        "down_gradient",
        (shape((G * PART, HEAD)), shape((G * PART, HEAD))),
        [VMEM] * 6,
        500_000_000,
        4_000_000,
    )(*inputs)


def middle_call(come):
    return call(middle_kernel, "middle_sum", shape((Z, 16, HEAD)), [VMEM], 1_000_000, 600_000)(come)


def last_call(come):
    return call(last_kernel, "last_sum", (shape((8, 3 * RANK)), shape((12, RANK))), [VMEM], 100_000, 70_000)(come)


def per_device(normed, queries, keys, values, cotangent, down, up, order):
    normed, queries, keys, values, cotangent = (
        item[0] for item in (normed, queries, keys, values, cotangent)
    )
    ring = ("yh", "x", "c")
    count = 16
    ahead = [(item, (item + 1) % count) for item in range(count)]
    behind = [(item, (item - 1) % count) for item in range(count)]
    sources = (order, keys, values, normed, down.T)
    inputs = (order, queries, keys, values, cotangent)
    send, low = prepare_call(outer_kernel, "outer_parts", (), *sources)
    outer = lax.ppermute(send, ring, ahead[1::2])
    send, low = prepare_call(inner_kernel, "inner_parts", (low,), *sources)
    inner = lax.ppermute(send, ring, ahead[::2])
    half, half_proj, plain, plain_proj = work_call(
        own_kernel, "own_attention", HALVES + PLAIN, (*inputs, up), 2_000_000_000
    )
    late, proj, back, far = work_call(
        joint_kernel, "joint_attention", JOINT, (*inputs, outer, up, plain_proj, half_proj), 1_000_000_000
    )
    outer_back = lax.ppermute(back, ring, behind[::2])
    later = work_call(
        later_kernel,
        "later_attention",
        PLAIN[:1] + JOINT,
        (*inputs, inner, up, half_proj, far),
        3_000_000_000,
        [pltpu.VMEM(PLAIN[1].shape, F32)],
    )
    inner_back = lax.ppermute(later[3], ring, behind[1::2])
    up_part = work_call(
        up_kernel,
        "up_gradient",
        shape((C, G, PART, HEAD)),
        (order, plain, late, far, later[0], later[1], later[4], half, low),
        1_000_000_000,
        [pltpu.VMEM((3 * WIDTH, HEAD), F32)],
    )
    mine, other = down_call(normed, proj, later[2], outer_back, inner_back, up_part)
    other = lax.ppermute(other, "c", [(0, 1), (1, 0)])
    chip = (mine.astype(F32) + other.astype(F32)).astype(BF16)
    plane = lax.all_to_all(chip.reshape(G, PART, HEAD), NEAR, 0, 0)
    line = lax.all_to_all(middle_call(plane), FAR, 0, 0)
    down_grad, up_grad = last_call(line)
    return down_grad, up_grad.T


def solution(mesh):
    fine = Mesh(mesh.devices.reshape(16, 2, 2, 4, 2), ("z", "yl", "yh", "x", "c"))
    dp, seq = ("z", "yl"), ("yh", "x", "c")
    tokens = P(dp, seq, None)
    in_specs = (tokens,) * 5 + (P(),) * 3
    out_specs = (P(dp + seq, None), P(None, dp + seq))
    return jax.shard_map(per_device, mesh=fine, in_specs=in_specs, out_specs=out_specs, check_vma=False)
```

time: 74 us -> 71.8 us (0.970)
  Pallas kernels: 15.2 us -> 11.1 us
  blocking collectives: 46.4 us -> 48.2 us
    all_to_all x1, blocking collectives: 22.6 us -> 24.6 us  [per_device(): plane = lax.all_to_all(chip.reshape(G, PART, HEAD), NEAR, 0, 0)]
    pallas_call x4, Pallas kernels: 8.7 us -> 6.94 us  [work_call(): call(body, name, out_shape, [ANY] + [VMEM] * (len(inputs) - 1), flops, 60...]
    pallas_call x2, Pallas kernels: 3.7 us -> 2.49 us  [prepare_call(): call(body, name, (shape((HALF, (2 * SHIFTED + 1) * HEAD)), shape((ROWS, H...]
  transfers between devices with their start and end apart: 5 -> 5, of which waited for: 1 -> 1; matrix products, arithmetic and copies ran while one was open for 0% -> 0% of each run, Pallas kernels for 16% -> 13%
where the time goes in v4:
time: 71.8 us; the launch traced here: 71.5 us
  blocking collectives  48.2 us (67%)
  Pallas kernels  11.1 us (15%)
  starting transfers between devices  8.86 us (12%)
  waiting for transfers between devices  1.64 us (2%)
  between operations  0.85 us (1%)
    all_to_all x1, blocking collectives, per_device(): plane = lax.all_to_all(chip.reshape(G, PART, HEAD), NEAR, 0, 0)  24.6 us
    all_to_all x1, blocking collectives, per_device(): line = lax.all_to_all(middle_call(plane), FAR, 0, 0)  23.6 us
    pallas_call x4, Pallas kernels, work_call(): call(body, name, out_shape, [ANY] + [VMEM] * (len(inputs) - 1), flops, 60...  6.94 us
    ppermute x1, starting transfers between devices, per_device(): other = lax.ppermute(other, 'c', [(0, 1), (1, 0)])  3.03 us
    pallas_call x2, Pallas kernels, prepare_call(): call(body, name, (shape((HALF, (2 * SHIFTED + 1) * HEAD)), shape((ROWS, H...  2.49 us
    ppermute x1, starting transfers between devices, per_device(): inner = lax.ppermute(send, ring, ahead[::2])  1.95 us
    ppermute x1, waiting for transfers between devices, per_device(): other = lax.ppermute(other, 'c', [(0, 1), (1, 0)])  1.61 us
  transfers between devices with their start and end apart: 5, of which 1 were waited for; matrix products, arithmetic and copies ran while one was open for 0% of the time, Pallas kernels for 13%

profile of v4, /device:TPU:2, one launch (start us, length us, event | category | flops | bytes accessed | tf_op | source)
XLA Modules:
  0.0 71.5 jit_solution(10886234881726821062)
XLA Ops:
  0.6 0.0 copy-start.3
  0.6 0.6 copy-done.3
  1.3 0.1 outer_parts.1
  1.4 1.3 %collective-permute-start = (bf16[80,2176]{1,0:T(8,128)(2,1)S(1)}, bf16[80,2176]{1,0:T(8,128)(2,1)S(1)}, u32[]{:S(2)}, u32[]{:S(2)}) collective-permute-start(bf16[80,2176]{1,0:T(8,128)(2,1)S(1)} %get-tuple-element.23), channel_id=1, source_target_pairs={{1,2},{3,4},{5,6},{7,8},{9,10},{11,12},{13,14},{15,0},{17,18},{19,... | collective-permute-start | bytes 1044488 | tf_op jit(solution)/shard_map/ppermute | solution.py:426
  2.7 0.0 copy-start.1
  2.7 0.0 copy-start.2
  2.7 0.0 copy-start.4
  2.7 0.0 copy-start.5
  2.7 0.0 copy-start.6
  2.7 2.4 %inner_parts.1 = (bf16[80,2176]{1,0:T(8,128)(2,1)S(1)}, bf16[160,128]{1,0:T(8,128)(2,1)S(1)}) custom-call(bf16[160,128]{1,0:T(8,128)(2,1)S(1)} %get-tuple-element.27.have_ref, s32[16]{0:T(128)S(1)} %copy-done.3, bf16[160,2048]{1,0:T(8,128)(2,1)} %bitcast.12, bf16[160,2048]{1,0:T(8,128)(2,1)} %bitcast.17, bf16[160,4096]{1,0:T(8,128)(2,1)} %bitcast.9, ...), custom_call_target="tpu_custom_call" | custom-call | flops 130000000 | bytes 3000000 | tf_op jit(solution)/shard_map/inner_parts/pallas_call | solution.py:360
  5.1 2.0 %collective-permute-start.1 = (bf16[80,2176]{1,0:T(8,128)(2,1)S(1)}, bf16[80,2176]{1,0:T(8,128)(2,1)S(1)}, u32[]{:S(2)}, u32[]{:S(2)}) collective-permute-start(bf16[80,2176]{1,0:T(8,128)(2,1)S(1)} %get-tuple-element.28), channel_id=1, source_target_pairs={{0,1},{2,3},{4,5},{6,7},{8,9},{10,11},{12,13},{14,15},{16,17},{18,... | collective-permute-start | bytes 1044488 | tf_op jit(solution)/shard_map/ppermute | solution.py:428
  7.1 0.0 copy-done.1
  7.1 0.0 copy-done.2
  7.1 0.0 copy-done.4
  7.1 0.0 copy-done.5
  7.2 0.0 copy-done.6
  7.2 3.4 %own_attention.1 = (bf16[80,3072]{1,0:T(8,128)(2,1)S(1)}, f32[80,128]{1,0:T(8,128)S(1)}, bf16[160,3072]{1,0:T(8,128)(2,1)S(1)}, f32[160,128]{1,0:T(8,128)S(1)}) custom-call(s32[16]{0:T(128)S(1)} %copy-done.3, bf16[160,2048]{1,0:T(8,128)(2,1)S(1)} %bitcast.21, bf16[160,2048]{1,0:T(8,128)(2,1)S(1)} %bitcast.13, bf16[160,2048]{1,0:T(8,128)(2,1)S(1)} %bitcast.18, ...), custom_call_target="tpu_custom_call" | custom-call | flops 2000000000 | bytes 6000000 | tf_op jit(solution)/shard_map/own_attention/pallas_call | solution.py:385
  10.5 0.0 collective-permute-done.refs_5_
  10.5 1.8 %joint_attention.1 = (bf16[160,3072]{1,0:T(8,128)(2,1)S(1)}, f32[160,128]{1,0:T(8,128)S(1)}, f32[80,128]{1,0:T(8,128)S(1)}, bf16[80,128]{1,0:T(8,128)(2,1)S(1)}) custom-call(s32[16]{0:T(128)S(1)} %copy-done.3, bf16[160,2048]{1,0:T(8,128)(2,1)S(1)} %bitcast.22, bf16[160,2048]{1,0:T(8,128)(2,1)S(1)} %bitcast.14, bf16[160,2048]{1,0:T(8,128)(2,1)S(1)} %bitcast.19, ...), custom_call_target="tpu_custom_call" | custom-call | flops 1000000000 | bytes 6000000 | tf_op jit(solution)/shard_map/joint_attention/pallas_call | solution.py:385
  12.3 1.3 %collective-permute-start.2 = (f32[80,128]{1,0:T(8,128)S(1)}, f32[80,128]{1,0:T(8,128)S(1)}, u32[]{:S(2)}, u32[]{:S(2)}) collective-permute-start(f32[80,128]{1,0:T(8,128)S(1)} %get-tuple-element.31), channel_id=1, source_target_pairs={{0,15},{2,1},{4,3},{6,5},{8,7},{10,9},{12,11},{14,13},{16,31},{18,... | collective-permute-start | bytes 122888 | tf_op jit(solution)/shard_map/ppermute | solution.py:435
  13.6 0.0 collective-permute-done.1.refs_5_
  13.7 1.3 %collective-permute-start.3 = (f32[80,128]{1,0:T(8,128)S(1)}, f32[80,128]{1,0:T(8,128)S(1)}, u32[]{:S(2)}, u32[]{:S(2)}) collective-permute-start(f32[80,128]{1,0:T(8,128)S(1)} %get-tuple-element.32), channel_id=1, source_target_pairs={{1,0},{3,2},{5,4},{7,6},{9,8},{11,10},{13,12},{15,14},{17,16},{19,... | collective-permute-start | bytes 122888 | tf_op jit(solution)/shard_map/ppermute | solution.py:444
  15.0 0.0 copy-start
  15.0 1.8 %up_gradient.1.up_ref = bf16[2,16,144,128]{3,2,1,0:T(8,128)(2,1)S(1)} custom-call(s32[16]{0:T(128)S(1)} %copy-done.3, bf16[160,3072]{1,0:T(8,128)(2,1)S(1)} %get-tuple-element.33.refs_1_, bf16[160,3072]{1,0:T(8,128)(2,1)S(1)} %get-tuple-element.34.refs_2_, bf16[80,128]{1,0:T(8,128)(2,1)S(1)} %get-tuple-element.29.refs_8_.refs_3_, ...), custom_call_target="tpu_custom_call" | custom-call | flops 1000000000 | bytes 6000000 | tf_op jit(solution)/shard_map/up_gradient/pallas_call | solution.py:385
  16.8 0.0 collective-permute-done.2.outer_ref
  16.8 0.0 collective-permute-done.3.inner_ref
  16.8 0.0 copy-done
  16.8 0.8 %down_gradient.1 = (bf16[2304,128]{1,0:T(8,128)(2,1)S(1)}, bf16[2304,128]{1,0:T(8,128)(2,1)S(1)}) custom-call(bf16[160,4096]{1,0:T(8,128)(2,1)S(1)} %bitcast.10, f32[160,128]{1,0:T(8,128)S(1)} %get-tuple-element.26.first_ref, f32[160,128]{1,0:T(8,128)S(1)} %get-tuple-element.30.later_ref, f32[80,128]{1,0:T(8,128)S(1)} %collective-permute-done.2.outer_ref, ...), custom_call_target="tpu_custom_call" | custom-call | flops 500000000 | bytes 4000000 | tf_op jit(solution)/shard_map/down_gradient/pallas_call | solution.py:397
  17.6 3.0 %collective-permute-start.4 = (bf16[2304,128]{1,0:T(8,128)(2,1)S(1)}, bf16[2304,128]{1,0:T(8,128)(2,1)S(1)}, u32[]{:S(2)}, u32[]{:S(2)}) collective-permute-start(bf16[2304,128]{1,0:T(8,128)(2,1)S(1)} %get-tuple-element.41), channel_id=1, source_target_pairs={{0,1},{1,0},{2,3},{3,2},{4,5},{5,4},{6,7},{7,6},{8,9},{9,8},{10,11... | collective-permute-start | bytes 1769480 | tf_op jit(solution)/shard_map/ppermute | solution.py:454
  20.7 1.6 %collective-permute-done.4 = bf16[2304,128]{1,0:T(8,128)(2,1)S(1)} collective-permute-done((bf16[2304,128]{1,0:T(8,128)(2,1)S(1)}, bf16[2304,128]{1,0:T(8,128)(2,1)S(1)}, u32[]{:S(2)}, u32[]{:S(2)}) %collective-permute-start.4) | collective-permute-done | bytes 589856 | tf_op jit(solution)/shard_map/ppermute | solution.py:454
  22.3 0.2 add_convert_fusion
  22.4 24.6 %all_to_all.10.come_ref = bf16[16,144,128]{2,1,0:T(8,128)(2,1)S(1)} all-to-all(bf16[16,144,128]{2,1,0:T(8,128)(2,1)S(1)} %bitcast.29), channel_id=1, replica_groups=mesh['z'=16,'yl'=2,'yh'=2,'x'=4,'c'=2] {'yl','yh','x'}, dimensions={0} | all-to-all | bytes 1179648 | tf_op jit(solution)/shard_map/all_to_all | solution.py:456
  47.1 0.1 middle_sum.1
  47.1 23.6 %all_to_all.11.come_ref = bf16[16,16,128]{2,1,0:T(8,128)(2,1)S(1)} all-to-all(bf16[16,16,128]{2,1,0:T(8,128)(2,1)S(1)} %middle_sum.1), channel_id=1, replica_groups=mesh['z'=16,'yl'=2,'yh'=2,'x'=4,'c'=2] {'z'}, dimensions={0} | all-to-all | bytes 131072 | tf_op jit(solution)/shard_map/all_to_all | solution.py:457
  70.7 0.8 %last_sum.1 = (bf16[8,96]{1,0:T(8,128)(2,1)}, bf16[12,32]{1,0:T(8,128)(2,1)}) custom-call(bf16[16,16,128]{2,1,0:T(8,128)(2,1)S(1)} %all_to_all.11.come_ref), custom_call_target="tpu_custom_call" | custom-call | flops 100000 | bytes 70000 | tf_op jit(solution)/shard_map/last_sum/pallas_call | solution.py:412
  (1 shorter events, 0.0 us)
Async XLA Ops:
  0.6 0.7 copy-start.3
  1.4 9.2 %collective-permute-start = (bf16[80,2176]{1,0:T(8,128)(2,1)S(1)}, bf16[80,2176]{1,0:T(8,128)(2,1)S(1)}, u32[]{:S(2)}, u32[]{:S(2)}) collective-permute-start(bf16[80,2176]{1,0:T(8,128)(2,1)S(1)} %get-tuple-element.23), channel_id=1, source_target_pairs={{1,2},{3,4},{5,6},{7,8},{9,10},{11,12},{13,14},{15,0},{17,18},{19,... | collective-permute-start | bytes 1044488 | tf_op jit(solution)/shard_map/ppermute | solution.py:426
  2.7 4.5 %copy-start.1 = (bf16[1,160,2048]{2,1,0:T(8,128)(2,1)S(1)}, bf16[1,160,2048]{2,1,0:T(8,128)(2,1)}, u32[]{:S(2)}) copy-start(bf16[1,160,2048]{2,1,0:T(8,128)(2,1)} %param.10) | copy-start | bytes 1966084
  2.7 4.5 %copy-start.2 = (bf16[1,160,2048]{2,1,0:T(8,128)(2,1)S(1)}, bf16[1,160,2048]{2,1,0:T(8,128)(2,1)}, u32[]{:S(2)}) copy-start(bf16[1,160,2048]{2,1,0:T(8,128)(2,1)} %param.11) | copy-start | bytes 1966084
  2.7 4.5 %copy-start.4 = (bf16[1,160,2048]{2,1,0:T(8,128)(2,1)S(1)}, bf16[1,160,2048]{2,1,0:T(8,128)(2,1)}, u32[]{:S(2)}) copy-start(bf16[1,160,2048]{2,1,0:T(8,128)(2,1)} %param.9) | copy-start | bytes 1966084
  2.7 4.5 %copy-start.5 = (bf16[1,160,2048]{2,1,0:T(8,128)(2,1)S(1)}, bf16[1,160,2048]{2,1,0:T(8,128)(2,1)}, u32[]{:S(2)}) copy-start(bf16[1,160,2048]{2,1,0:T(8,128)(2,1)} %param.12) | copy-start | bytes 1966084
  2.7 4.4 %copy-start.6 = (bf16[32,6144]{1,0:T(8,128)(2,1)S(1)}, bf16[32,6144]{1,0:T(8,128)(2,1)}, u32[]{:S(2)}) copy-start(bf16[32,6144]{1,0:T(8,128)(2,1)} %refs_6_.3) | copy-start | bytes 1179652
  5.1 8.5 %collective-permute-start.1 = (bf16[80,2176]{1,0:T(8,128)(2,1)S(1)}, bf16[80,2176]{1,0:T(8,128)(2,1)S(1)}, u32[]{:S(2)}, u32[]{:S(2)}) collective-permute-start(bf16[80,2176]{1,0:T(8,128)(2,1)S(1)} %get-tuple-element.28), channel_id=1, source_target_pairs={{0,1},{2,3},{4,5},{6,7},{8,9},{10,11},{12,13},{14,15},{16,17},{18,... | collective-permute-start | bytes 1044488 | tf_op jit(solution)/shard_map/ppermute | solution.py:428
  12.3 4.4 %collective-permute-start.2 = (f32[80,128]{1,0:T(8,128)S(1)}, f32[80,128]{1,0:T(8,128)S(1)}, u32[]{:S(2)}, u32[]{:S(2)}) collective-permute-start(f32[80,128]{1,0:T(8,128)S(1)} %get-tuple-element.31), channel_id=1, source_target_pairs={{0,15},{2,1},{4,3},{6,5},{8,7},{10,9},{12,11},{14,13},{16,31},{18,... | collective-permute-start | bytes 122888 | tf_op jit(solution)/shard_map/ppermute | solution.py:435
  13.7 3.1 %collective-permute-start.3 = (f32[80,128]{1,0:T(8,128)S(1)}, f32[80,128]{1,0:T(8,128)S(1)}, u32[]{:S(2)}, u32[]{:S(2)}) collective-permute-start(f32[80,128]{1,0:T(8,128)S(1)} %get-tuple-element.32), channel_id=1, source_target_pairs={{1,0},{3,2},{5,4},{7,6},{9,8},{11,10},{13,12},{15,14},{17,16},{19,... | collective-permute-start | bytes 122888 | tf_op jit(solution)/shard_map/ppermute | solution.py:444
  15.0 1.8 %copy-start = (bf16[1,160,4096]{2,1,0:T(8,128)(2,1)S(1)}, bf16[1,160,4096]{2,1,0:T(8,128)(2,1)}, u32[]{:S(2)}) copy-start(bf16[1,160,4096]{2,1,0:T(8,128)(2,1)} %param.8) | copy-start | bytes 3932164
  17.6 4.6 %collective-permute-start.4 = (bf16[2304,128]{1,0:T(8,128)(2,1)S(1)}, bf16[2304,128]{1,0:T(8,128)(2,1)S(1)}, u32[]{:S(2)}, u32[]{:S(2)}) collective-permute-start(bf16[2304,128]{1,0:T(8,128)(2,1)S(1)} %get-tuple-element.41), channel_id=1, source_target_pairs={{0,1},{1,0},{2,3},{3,2},{4,5},{5,4},{6,7},{7,6},{8,9},{9,8},{10,11... | collective-permute-start | bytes 1769480 | tf_op jit(solution)/shard_map/ppermute | solution.py:454

commit v5 on v4

--- a/solution.py
+++ b/solution.py
@@ -95,7 +95,30 @@
     return copy
 
 
-def prepare(
+def load_pair(source_ref, key_ref, value_ref, pair_own, pair_sems, order_ref, order_sem):
+    copies = [fetch(source_ref, order_ref, order_sem)]
+    for item, source in enumerate((key_ref, value_ref)):
+        copies.append(fetch(source.at[HALF:], pair_own.at[item], pair_sems.at[item]))
+    return copies
+
+
+def pick_pair(copies, order_ref, pair_own, send_ref):
+    copies[0].wait()
+    for item in range(2):
+        copies[1 + item].wait()
+        for slot in range(SHIFTED):
+            place = item * SHIFTED + slot
+            send_ref[:, place * HEAD : (place + 1) * HEAD] = pair_own[item, :, lanes_of(order_ref, slot)]
+
+
+def outer_kernel(source_ref, key_ref, value_ref, send_ref, pair_own, pair_sems, order_ref, order_sem):
+    @pl.when(lax.axis_index("c") == 1)
+    def _():
+        copies = load_pair(source_ref, key_ref, value_ref, pair_own, pair_sems, order_ref, order_sem)
+        pick_pair(copies, order_ref, pair_own, send_ref)
+
+
+def inner_kernel(
     source_ref,
     key_ref,
     value_ref,
@@ -103,33 +126,35 @@
     down_ref,
     send_ref,
     low_ref,
-    pair_own,
+    far_ref,
     normed_own,
     down_own,
-    pair_sems,
     wide_sems,
-    order_ref,
-    order_sem,
+    pair_own,
+    *rest,
 ):
-    order_copy = fetch(source_ref, order_ref, order_sem)
-    pair_copies, wide_copies = [], []
-    for item, source in enumerate((key_ref, value_ref)):
-        copy = pltpu.make_async_copy(source.at[HALF:], pair_own.at[item], pair_sems.at[item])
-        copy.start()
-        pair_copies.append(copy)
+    pair_sems, order_ref, order_sem = rest
+    core = lax.axis_index("c")
+    pair = (source_ref, key_ref, value_ref, pair_own, pair_sems, order_ref, order_sem)
+
+    @pl.when(core == 0)
+    def _():
+        load_pair(*pair)
+
+    wide_copies = []
     span = MODEL // WIDE
     for part in range(WIDE):
         lanes = slice(part * span, (part + 1) * span)
         for item, (source, target) in enumerate(((normed_ref, normed_own), (down_ref, down_own))):
-            copy = pltpu.make_async_copy(source.at[:, lanes], target.at[:, lanes], wide_sems.at[item, part])
-            copy.start()
-            wide_copies.append(copy)
-    order_copy.wait()
-    for item in range(2):
-        pair_copies[item].wait()
-        for slot in range(SHIFTED):
-            place = item * SHIFTED + slot
-            send_ref[:, place * HEAD : (place + 1) * HEAD] = pair_own[item, :, lanes_of(order_ref, slot)]
+            wide_copies.append(fetch(source.at[:, lanes], target.at[:, lanes], wide_sems.at[item, part]))
+
+    @pl.when(core == 0)
+    def _():
+        copies = [pltpu.make_async_copy(source_ref, order_ref, order_sem)]
+        for item, source in enumerate((key_ref, value_ref)):
+            copies.append(pltpu.make_async_copy(source.at[HALF:], pair_own.at[item], pair_sems.at[item]))
+        pick_pair(copies, order_ref, pair_own, send_ref)
+
     low = jnp.zeros((ROWS, 3 * RANK), F32)
     for part in range(WIDE):
         lanes = slice(part * span, (part + 1) * span)
@@ -138,25 +163,8 @@
         low = low + dot_last(normed_own[:, lanes], down_own[:, lanes])
     low = jnp.concatenate([low.astype(BF16), jnp.zeros((ROWS, HEAD - 3 * RANK), BF16)], axis=1)
     low_ref[...] = low
+    far_ref[...] = low[HALF:]
     send_ref[:, 2 * SHIFTED * HEAD :] = low[HALF:]
-
-
-def outer_kernel(*refs):
-    @pl.when(lax.axis_index("c") == 1)
-    def _():
-        prepare(*refs)
-
-
-def inner_kernel(have_ref, *refs):
-    core = lax.axis_index("c")
-
-    @pl.when(core == 0)
-    def _():
-        prepare(*refs)
-
-    @pl.when(core == 1)
-    def _():
-        refs[6][...] = have_ref[...]
 
 
 def project(order_ref, grads_ref, up_ref, slots):
@@ -188,10 +196,9 @@
 
 
 def joint_work(
-    order_ref, refs, come_ref, up_ref, plain_proj_ref, half_proj_ref, late_ref, proj_ref, back_ref, far_ref
+    order_ref, refs, come_ref, up_ref, plain_proj_ref, half_proj_ref, late_ref, proj_ref, back_ref
 ):
     query_ref, key_ref, value_ref, cot_ref = refs
-    far_ref[...] = come_ref[:, 2 * SHIFTED * HEAD :]
     nothing = jnp.zeros((HALF, HEAD), BF16)
     slots = range(SHIFTED)
     parts = []
@@ -237,7 +244,7 @@
 
 def later_kernel(*refs):
     source_ref, inputs, come_ref, up_ref, half_proj_ref = refs[0], refs[1:5], refs[5], refs[6], refs[7]
-    plain_ref, outs, (plain_proj_ref, order_ref, order_sem) = refs[9], refs[10:14], refs[14:]
+    plain_ref, outs, (plain_proj_ref, order_ref, order_sem) = refs[9], refs[10:13], refs[13:]
 
     @pl.when(lax.axis_index("c") == 1)
     def _():
@@ -248,7 +255,8 @@
 
 def accumulate(order_ref, order_copy, plain_ref, late_ref, far_ref, half_ref, low_ref, sums_ref):
     low = low_ref[...]
-    late_low = jnp.concatenate([low[:HALF], far_ref[...], low[HALF:]], axis=0)
+    far_low = far_ref[:, far_ref.shape[1] - HEAD :]
+    late_low = jnp.concatenate([low[:HALF], far_low, low[HALF:]], axis=0)
     rights = [
         [jnp.concatenate([item[:, block * RANK : (block + 1) * RANK]] * 4, axis=1) for block in range(3)]
         for item in (low, late_low)
@@ -356,29 +364,43 @@
     return jax.ShapeDtypeStruct(dims, kind)
 
 
-def prepare_call(body, name, extra, order, keys, values, normed, down):
+PAIR = (pltpu.VMEM((2, HALF, WIDTH), BF16), pltpu.SemaphoreType.DMA((2,)), *ORDER)
+
+
+def outer_call(order, keys, values):
     return call(
-        body,
-        name,
-        (shape((HALF, (2 * SHIFTED + 1) * HEAD)), shape((ROWS, HEAD))),
-        [VMEM] * len(extra) + [ANY] + [HBM] * 4,
+        outer_kernel,
+        "outer_parts",
+        shape((HALF, 2 * SHIFTED * HEAD)),
+        [ANY, HBM, HBM],
+        1_000_000,
+        1_000_000,
+        limit=53,
+        scratch_shapes=PAIR,
+    )(order, keys, values)
+
+
+def inner_call(order, keys, values, normed, down):
+    return call(
+        inner_kernel,
+        "inner_parts",
+        (shape((HALF, (2 * SHIFTED + 1) * HEAD)), shape((ROWS, HEAD)), shape((HALF, HEAD))),
+        [ANY] + [HBM] * 4,
         130_000_000,
         3_000_000,
         limit=53,
         scratch_shapes=[
-            pltpu.VMEM((2, HALF, WIDTH), BF16),
             pltpu.VMEM(normed.shape, BF16),
             pltpu.VMEM(down.shape, BF16),
-            pltpu.SemaphoreType.DMA((2,)),
             pltpu.SemaphoreType.DMA((2, WIDE)),
-            *ORDER,
+            *PAIR,
         ],
-    )(*extra, order, keys, values, normed, down)
+    )(order, keys, values, normed, down)
 
 
 PLAIN = (shape((ROWS, 3 * NARROW)), shape((ROWS, HEAD), F32))
 HALVES = (shape((HALF, 3 * NARROW)), shape((HALF, HEAD), F32))
-JOINT = (shape((ROWS, 3 * NARROW)), shape((ROWS, HEAD), F32), shape((HALF, HEAD), F32), shape((HALF, HEAD)))
+JOINT = (shape((ROWS, 3 * NARROW)), shape((ROWS, HEAD), F32), shape((HALF, HEAD), F32))
 
 
 def work_call(body, name, out_shape, inputs, flops, scratch=()):
@@ -420,16 +442,15 @@
     count = 16
     ahead = [(item, (item + 1) % count) for item in range(count)]
     behind = [(item, (item - 1) % count) for item in range(count)]
-    sources = (order, keys, values, normed, down.T)
     inputs = (order, queries, keys, values, cotangent)
-    send, low = prepare_call(outer_kernel, "outer_parts", (), *sources)
-    outer = lax.ppermute(send, ring, ahead[1::2])
-    send, low = prepare_call(inner_kernel, "inner_parts", (low,), *sources)
+    outer = lax.ppermute(outer_call(order, keys, values), ring, ahead[1::2])
+    send, low, far = inner_call(order, keys, values, normed, down.T)
     inner = lax.ppermute(send, ring, ahead[::2])
+    outer_low = lax.ppermute(far, ring, ahead[1::2])
     half, half_proj, plain, plain_proj = work_call(
         own_kernel, "own_attention", HALVES + PLAIN, (*inputs, up), 2_000_000_000
     )
-    late, proj, back, far = work_call(
+    late, proj, back = work_call(
         joint_kernel, "joint_attention", JOINT, (*inputs, outer, up, plain_proj, half_proj), 1_000_000_000
     )
     outer_back = lax.ppermute(back, ring, behind[::2])
@@ -437,7 +458,7 @@
         later_kernel,
         "later_attention",
         PLAIN[:1] + JOINT,
-        (*inputs, inner, up, half_proj, far),
+        (*inputs, inner, up, half_proj, back),
         3_000_000_000,
         [pltpu.VMEM(PLAIN[1].shape, F32)],
     )
@@ -446,7 +467,7 @@
         up_kernel,
         "up_gradient",
         shape((C, G, PART, HEAD)),
-        (order, plain, late, far, later[0], later[1], later[4], half, low),
+        (order, plain, late, outer_low, later[0], later[1], inner, half, low),
         1_000_000_000,
         [pltpu.VMEM((3 * WIDTH, HEAD), F32)],
     )

time: 71.8 us -> 74.6 us (1.039)
  starting transfers between devices: 8.86 us -> 12.1 us
  blocking collectives: 48.2 us -> 47.2 us
    ppermute x1, starting transfers between devices: 1.95 us -> 3.86 us  [per_device(): inner = lax.ppermute(send, ring, ahead[::2])]
    all_to_all x1, blocking collectives: 24.6 us -> 22.8 us  [per_device(): plane = lax.all_to_all(chip.reshape(G, PART, HEAD), NEAR, 0, 0)]
    ppermute x1 -> x2, starting transfers between devices: 1.29 us -> 2.58 us  [the longest x1 1.29 us: per_device(): outer = lax.ppermute(outer_call(order, keys, values), ring, ahead[1::2])]
    all_to_all x1, blocking collectives: 23.6 us -> 24.3 us  [per_device(): line = lax.all_to_all(middle_call(plane), FAR, 0, 0)]
  transfers between devices with their start and end apart: 5 -> 6, of which waited for: 1 -> 2; matrix products, arithmetic and copies ran while one was open for 0% -> 0% of each run, Pallas kernels for 13% -> 13%
where the time goes in v5:
time: 74.6 us; the launch traced here: 74.3 us
  blocking collectives  47.2 us (63%)
  starting transfers between devices  12.1 us (16%)
  Pallas kernels  11.2 us (15%)
  waiting for transfers between devices  2.16 us (3%)
  between operations  0.87 us (1%)
    all_to_all x1, blocking collectives, per_device(): line = lax.all_to_all(middle_call(plane), FAR, 0, 0)  24.3 us
    all_to_all x1, blocking collectives, per_device(): plane = lax.all_to_all(chip.reshape(G, PART, HEAD), NEAR, 0, 0)  22.8 us
    pallas_call x4, Pallas kernels, work_call(): call(body, name, out_shape, [ANY] + [VMEM] * (len(inputs) - 1), flops, 60...  6.94 us
    ppermute x1, starting transfers between devices, per_device(): inner = lax.ppermute(send, ring, ahead[::2])  3.86 us
    ppermute x1, starting transfers between devices, per_device(): other = lax.ppermute(other, 'c', [(0, 1), (1, 0)])  3.04 us
    pallas_call x1, Pallas kernels, inner_call(): call(inner_kernel, 'inner_parts', (shape((HALF, (2 * SHIFTED + 1) * HEAD)...  2.53 us
    ppermute x1, waiting for transfers between devices, per_device(): other = lax.ppermute(other, 'c', [(0, 1), (1, 0)])  1.61 us
  transfers between devices with their start and end apart: 6, of which 2 were waited for; matrix products, arithmetic and copies ran while one was open for 0% of the time, Pallas kernels for 13%

profile of v5, /device:TPU:2, one launch (start us, length us, event | category | flops | bytes accessed | tf_op | source)
XLA Modules:
  0.0 74.3 jit_solution(1654500903735303196)
XLA Ops:
  0.6 0.0 copy-start.3
  0.6 0.6 copy-done.3
  1.3 1.3 %collective-permute-start = (bf16[80,2048]{1,0:T(8,128)(2,1)S(1)}, bf16[80,2048]{1,0:T(8,128)(2,1)S(1)}, u32[]{:S(2)}, u32[]{:S(2)}) collective-permute-start(bf16[80,2048]{1,0:T(8,128)(2,1)S(1)} %outer_parts.1), channel_id=1, source_target_pairs={{1,2},{3,4},{5,6},{7,8},{9,10},{11,12},{13,14},{15,0},{17,18},{19,... | collective-permute-start | bytes 983048 | tf_op jit(solution)/shard_map/ppermute | solution.py:446
  2.6 0.0 copy-start.1
  2.6 0.0 copy-start.2
  2.6 0.0 copy-start.4
  2.7 0.0 copy-start.5
  2.7 0.0 copy-start.6
  2.7 2.5 %inner_parts.1 = (bf16[80,2176]{1,0:T(8,128)(2,1)S(1)}, bf16[160,128]{1,0:T(8,128)(2,1)S(1)}, bf16[80,128]{1,0:T(8,128)(2,1)S(1)}) custom-call(s32[16]{0:T(128)S(1)} %copy-done.3, bf16[160,2048]{1,0:T(8,128)(2,1)} %bitcast.11, bf16[160,2048]{1,0:T(8,128)(2,1)} %bitcast.16, bf16[160,4096]{1,0:T(8,128)(2,1)} %bitcast.8, bf16[96,4096]{1,0:T(8,128)(2,1)} %bitcast.27), custom_call_target="tpu_custom_call" | custom-call | flops 130000000 | bytes 3000000 | tf_op jit(solution)/shard_map/inner_parts/pallas_call | solution.py:384
  5.2 3.9 %collective-permute-start.1 = (bf16[80,2176]{1,0:T(8,128)(2,1)S(1)}, bf16[80,2176]{1,0:T(8,128)(2,1)S(1)}, u32[]{:S(2)}, u32[]{:S(2)}) collective-permute-start(bf16[80,2176]{1,0:T(8,128)(2,1)S(1)} %get-tuple-element.23), channel_id=1, source_target_pairs={{0,1},{2,3},{4,5},{6,7},{8,9},{10,11},{12,13},{14,15},{16,17},{18,... | collective-permute-start | bytes 1044488 | tf_op jit(solution)/shard_map/ppermute | solution.py:448
  9.1 1.3 %collective-permute-start.4 = (bf16[80,128]{1,0:T(8,128)(2,1)S(1)}, bf16[80,128]{1,0:T(8,128)(2,1)S(1)}, u32[]{:S(2)}, u32[]{:S(2)}) collective-permute-start(bf16[80,128]{1,0:T(8,128)(2,1)S(1)} %get-tuple-element.29), channel_id=1, source_target_pairs={{1,2},{3,4},{5,6},{7,8},{9,10},{11,12},{13,14},{15,0},{17,18},{19,... | collective-permute-start | bytes 61448 | tf_op jit(solution)/shard_map/ppermute | solution.py:449
  10.4 0.0 copy-done.1
  10.4 0.0 copy-done.2
  10.4 0.0 copy-done.4
  10.4 0.0 copy-done.5
  10.4 0.0 copy-done.6
  10.4 3.3 %own_attention.1 = (bf16[80,3072]{1,0:T(8,128)(2,1)S(1)}, f32[80,128]{1,0:T(8,128)S(1)}, bf16[160,3072]{1,0:T(8,128)(2,1)S(1)}, f32[160,128]{1,0:T(8,128)S(1)}) custom-call(s32[16]{0:T(128)S(1)} %copy-done.3, bf16[160,2048]{1,0:T(8,128)(2,1)S(1)} %bitcast.20, bf16[160,2048]{1,0:T(8,128)(2,1)S(1)} %bitcast.12, bf16[160,2048]{1,0:T(8,128)(2,1)S(1)} %bitcast.17, ...), custom_call_target="tpu_custom_call" | custom-call | flops 2000000000 | bytes 6000000 | tf_op jit(solution)/shard_map/own_attention/pallas_call | solution.py:407
  13.8 0.0 collective-permute-done.refs_5_
  13.8 1.8 %joint_attention.1 = (bf16[160,3072]{1,0:T(8,128)(2,1)S(1)}, f32[160,128]{1,0:T(8,128)S(1)}, f32[80,128]{1,0:T(8,128)S(1)}) custom-call(s32[16]{0:T(128)S(1)} %copy-done.3, bf16[160,2048]{1,0:T(8,128)(2,1)S(1)} %bitcast.21, bf16[160,2048]{1,0:T(8,128)(2,1)S(1)} %bitcast.13, bf16[160,2048]{1,0:T(8,128)(2,1)S(1)} %bitcast.18, bf16[160,2048]{1,0:T(8,128)(2,1)S(1)} %bitcast.24, ...), custom_call_target="tpu_custom_call" | custom-call | flops 1000000000 | bytes 6000000 | tf_op jit(solution)/shard_map/joint_attention/pallas_call | solution.py:407
  15.6 1.3 %collective-permute-start.2 = (f32[80,128]{1,0:T(8,128)S(1)}, f32[80,128]{1,0:T(8,128)S(1)}, u32[]{:S(2)}, u32[]{:S(2)}) collective-permute-start(f32[80,128]{1,0:T(8,128)S(1)} %get-tuple-element.24.refs_8_), channel_id=1, source_target_pairs={{0,15},{2,1},{4,3},{6,5},{8,7},{10,9},{12,11},{14,13},{16,31},{18,... | collective-permute-start | bytes 122888 | tf_op jit(solution)/shard_map/ppermute | solution.py:456
  16.9 0.0 collective-permute-done.1.refs_5_.refs_6_
  17.0 1.3 %collective-permute-start.3 = (f32[80,128]{1,0:T(8,128)S(1)}, f32[80,128]{1,0:T(8,128)S(1)}, u32[]{:S(2)}, u32[]{:S(2)}) collective-permute-start(f32[80,128]{1,0:T(8,128)S(1)} %get-tuple-element.26), channel_id=1, source_target_pairs={{1,0},{3,2},{5,4},{7,6},{9,8},{11,10},{13,12},{15,14},{17,16},{19,... | collective-permute-start | bytes 122888 | tf_op jit(solution)/shard_map/ppermute | solution.py:465
  18.3 0.0 collective-permute-done.4.refs_3_
  18.3 0.0 copy-start
  18.3 1.8 %up_gradient.1.up_ref = bf16[2,16,144,128]{3,2,1,0:T(8,128)(2,1)S(1)} custom-call(s32[16]{0:T(128)S(1)} %copy-done.3, bf16[160,3072]{1,0:T(8,128)(2,1)S(1)} %get-tuple-element.27.refs_1_, bf16[160,3072]{1,0:T(8,128)(2,1)S(1)} %get-tuple-element.28.refs_2_, bf16[80,128]{1,0:T(8,128)(2,1)S(1)} %collective-permute-done.4.refs_3_, ...), custom_call_target="tpu_custom_call" | custom-call | flops 1000000000 | bytes 6000000 | tf_op jit(solution)/shard_map/up_gradient/pallas_call | solution.py:407
  20.0 0.0 collective-permute-done.2.outer_ref
  20.1 0.5 collective-permute-done.3.inner_ref
  20.6 0.0 copy-done
  20.6 0.8 %down_gradient.1 = (bf16[2304,128]{1,0:T(8,128)(2,1)S(1)}, bf16[2304,128]{1,0:T(8,128)(2,1)S(1)}) custom-call(bf16[160,4096]{1,0:T(8,128)(2,1)S(1)} %bitcast.9, f32[160,128]{1,0:T(8,128)S(1)} %get-tuple-element.22.first_ref, f32[160,128]{1,0:T(8,128)S(1)} %get-tuple-element.25.later_ref, f32[80,128]{1,0:T(8,128)S(1)} %collective-permute-done.2.outer_ref, ...), custom_call_target="tpu_custom_call" | custom-call | flops 500000000 | bytes 4000000 | tf_op jit(solution)/shard_map/down_gradient/pallas_call | solution.py:419
  21.4 3.0 %collective-permute-start.5 = (bf16[2304,128]{1,0:T(8,128)(2,1)S(1)}, bf16[2304,128]{1,0:T(8,128)(2,1)S(1)}, u32[]{:S(2)}, u32[]{:S(2)}) collective-permute-start(bf16[2304,128]{1,0:T(8,128)(2,1)S(1)} %get-tuple-element.35), channel_id=1, source_target_pairs={{0,1},{1,0},{2,3},{3,2},{4,5},{5,4},{6,7},{7,6},{8,9},{9,8},{10,11... | collective-permute-start | bytes 1769480 | tf_op jit(solution)/shard_map/ppermute | solution.py:475
  24.5 1.6 %collective-permute-done.5 = bf16[2304,128]{1,0:T(8,128)(2,1)S(1)} collective-permute-done((bf16[2304,128]{1,0:T(8,128)(2,1)S(1)}, bf16[2304,128]{1,0:T(8,128)(2,1)S(1)}, u32[]{:S(2)}, u32[]{:S(2)}) %collective-permute-start.5) | collective-permute-done | bytes 589856 | tf_op jit(solution)/shard_map/ppermute | solution.py:475
  26.1 0.2 add_convert_fusion
  26.2 22.8 %all_to_all.10.come_ref = bf16[16,144,128]{2,1,0:T(8,128)(2,1)S(1)} all-to-all(bf16[16,144,128]{2,1,0:T(8,128)(2,1)S(1)} %bitcast.26), channel_id=1, replica_groups=mesh['z'=16,'yl'=2,'yh'=2,'x'=4,'c'=2] {'yl','yh','x'}, dimensions={0} | all-to-all | bytes 1179648 | tf_op jit(solution)/shard_map/all_to_all | solution.py:477
  49.1 0.1 middle_sum.1
  49.2 24.3 %all_to_all.11.come_ref = bf16[16,16,128]{2,1,0:T(8,128)(2,1)S(1)} all-to-all(bf16[16,16,128]{2,1,0:T(8,128)(2,1)S(1)} %middle_sum.1), channel_id=1, replica_groups=mesh['z'=16,'yl'=2,'yh'=2,'x'=4,'c'=2] {'z'}, dimensions={0} | all-to-all | bytes 131072 | tf_op jit(solution)/shard_map/all_to_all | solution.py:478
  73.5 0.8 %last_sum.1 = (bf16[8,96]{1,0:T(8,128)(2,1)}, bf16[12,32]{1,0:T(8,128)(2,1)}) custom-call(bf16[16,16,128]{2,1,0:T(8,128)(2,1)S(1)} %all_to_all.11.come_ref), custom_call_target="tpu_custom_call" | custom-call | flops 100000 | bytes 70000 | tf_op jit(solution)/shard_map/last_sum/pallas_call | solution.py:434
  (2 shorter events, 0.1 us)
Async XLA Ops:
  0.6 0.7 copy-start.3
  1.3 12.5 %collective-permute-start = (bf16[80,2048]{1,0:T(8,128)(2,1)S(1)}, bf16[80,2048]{1,0:T(8,128)(2,1)S(1)}, u32[]{:S(2)}, u32[]{:S(2)}) collective-permute-start(bf16[80,2048]{1,0:T(8,128)(2,1)S(1)} %outer_parts.1), channel_id=1, source_target_pairs={{1,2},{3,4},{5,6},{7,8},{9,10},{11,12},{13,14},{15,0},{17,18},{19,... | collective-permute-start | bytes 983048 | tf_op jit(solution)/shard_map/ppermute | solution.py:446
  2.6 7.8 %copy-start.1 = (bf16[1,160,2048]{2,1,0:T(8,128)(2,1)S(1)}, bf16[1,160,2048]{2,1,0:T(8,128)(2,1)}, u32[]{:S(2)}) copy-start(bf16[1,160,2048]{2,1,0:T(8,128)(2,1)} %param.10) | copy-start | bytes 1966084
  2.6 7.8 %copy-start.2 = (bf16[1,160,2048]{2,1,0:T(8,128)(2,1)S(1)}, bf16[1,160,2048]{2,1,0:T(8,128)(2,1)}, u32[]{:S(2)}) copy-start(bf16[1,160,2048]{2,1,0:T(8,128)(2,1)} %param.11) | copy-start | bytes 1966084
  2.6 7.8 %copy-start.4 = (bf16[1,160,2048]{2,1,0:T(8,128)(2,1)S(1)}, bf16[1,160,2048]{2,1,0:T(8,128)(2,1)}, u32[]{:S(2)}) copy-start(bf16[1,160,2048]{2,1,0:T(8,128)(2,1)} %param.9) | copy-start | bytes 1966084
  2.7 7.8 %copy-start.5 = (bf16[1,160,2048]{2,1,0:T(8,128)(2,1)S(1)}, bf16[1,160,2048]{2,1,0:T(8,128)(2,1)}, u32[]{:S(2)}) copy-start(bf16[1,160,2048]{2,1,0:T(8,128)(2,1)} %param.12) | copy-start | bytes 1966084
  2.7 7.8 %copy-start.6 = (bf16[32,6144]{1,0:T(8,128)(2,1)S(1)}, bf16[32,6144]{1,0:T(8,128)(2,1)}, u32[]{:S(2)}) copy-start(bf16[32,6144]{1,0:T(8,128)(2,1)} %refs_6_.3) | copy-start | bytes 1179652
  5.2 11.7 %collective-permute-start.1 = (bf16[80,2176]{1,0:T(8,128)(2,1)S(1)}, bf16[80,2176]{1,0:T(8,128)(2,1)S(1)}, u32[]{:S(2)}, u32[]{:S(2)}) collective-permute-start(bf16[80,2176]{1,0:T(8,128)(2,1)S(1)} %get-tuple-element.23), channel_id=1, source_target_pairs={{0,1},{2,3},{4,5},{6,7},{8,9},{10,11},{12,13},{14,15},{16,17},{18,... | collective-permute-start | bytes 1044488 | tf_op jit(solution)/shard_map/ppermute | solution.py:448
  9.1 9.2 %collective-permute-start.4 = (bf16[80,128]{1,0:T(8,128)(2,1)S(1)}, bf16[80,128]{1,0:T(8,128)(2,1)S(1)}, u32[]{:S(2)}, u32[]{:S(2)}) collective-permute-start(bf16[80,128]{1,0:T(8,128)(2,1)S(1)} %get-tuple-element.29), channel_id=1, source_target_pairs={{1,2},{3,4},{5,6},{7,8},{9,10},{11,12},{13,14},{15,0},{17,18},{19,... | collective-permute-start | bytes 61448 | tf_op jit(solution)/shard_map/ppermute | solution.py:449
  15.6 4.4 %collective-permute-start.2 = (f32[80,128]{1,0:T(8,128)S(1)}, f32[80,128]{1,0:T(8,128)S(1)}, u32[]{:S(2)}, u32[]{:S(2)}) collective-permute-start(f32[80,128]{1,0:T(8,128)S(1)} %get-tuple-element.24.refs_8_), channel_id=1, source_target_pairs={{0,15},{2,1},{4,3},{6,5},{8,7},{10,9},{12,11},{14,13},{16,31},{18,... | collective-permute-start | bytes 122888 | tf_op jit(solution)/shard_map/ppermute | solution.py:456
  17.0 3.6 %collective-permute-start.3 = (f32[80,128]{1,0:T(8,128)S(1)}, f32[80,128]{1,0:T(8,128)S(1)}, u32[]{:S(2)}, u32[]{:S(2)}) collective-permute-start(f32[80,128]{1,0:T(8,128)S(1)} %get-tuple-element.26), channel_id=1, source_target_pairs={{1,0},{3,2},{5,4},{7,6},{9,8},{11,10},{13,12},{15,14},{17,16},{19,... | collective-permute-start | bytes 122888 | tf_op jit(solution)/shard_map/ppermute | solution.py:465
  18.3 2.3 %copy-start = (bf16[1,160,4096]{2,1,0:T(8,128)(2,1)S(1)}, bf16[1,160,4096]{2,1,0:T(8,128)(2,1)}, u32[]{:S(2)}) copy-start(bf16[1,160,4096]{2,1,0:T(8,128)(2,1)} %param.8) | copy-start | bytes 3932164
  21.4 4.7 %collective-permute-start.5 = (bf16[2304,128]{1,0:T(8,128)(2,1)S(1)}, bf16[2304,128]{1,0:T(8,128)(2,1)S(1)}, u32[]{:S(2)}, u32[]{:S(2)}) collective-permute-start(bf16[2304,128]{1,0:T(8,128)(2,1)S(1)} %get-tuple-element.35), channel_id=1, source_target_pairs={{0,1},{1,0},{2,3},{3,2},{4,5},{5,4},{6,7},{7,6},{8,9},{9,8},{10,11... | collective-permute-start | bytes 1769480 | tf_op jit(solution)/shard_map/ppermute | solution.py:475

commit v6 on v4

--- a/solution.py
+++ b/solution.py
@@ -55,7 +55,7 @@
     return lax.dot_general(left, right, (((0,), (0,)), ((), ())), preferred_element_type=F32)
 
 
-def attend(parts, allowed):
+def scores_of(parts, allowed):
     queries, keys, values, cotangents = zip(*parts)
     scores = [jnp.where(allowed, dot_last(key, query), -jnp.inf) for query, key in zip(queries, keys)]
     dprobs = [dot_last(value, cotangent) for value, cotangent in zip(values, cotangents)]
@@ -63,13 +63,19 @@
     powers = [jnp.exp((item - top) * SCALE) for item, top in zip(scores, tops)]
     probs = [item * (1.0 / jnp.sum(item, axis=0, keepdims=True)) for item in powers]
     weights = [item.astype(BF16) for item in probs]
-    dvalues = [dot(weight, cotangent).astype(BF16) for weight, cotangent in zip(weights, cotangents)]
     deltas = [
         jnp.sum(weight.astype(F32) * dprob, axis=0, keepdims=True) for weight, dprob in zip(weights, dprobs)
     ]
     dscores = [
         (prob * (dprob - delta)).astype(BF16) for prob, dprob, delta in zip(probs, dprobs, deltas)
     ]
+    return weights, dscores
+
+
+def attend(parts, allowed):
+    queries, keys, _, cotangents = zip(*parts)
+    weights, dscores = scores_of(parts, allowed)
+    dvalues = [dot(weight, cotangent).astype(BF16) for weight, cotangent in zip(weights, cotangents)]
     dkeys = [(dot(dscore, query) * SCALE).astype(BF16) for dscore, query in zip(dscores, queries)]
     dqueries = [(dot_first(dscore, key) * SCALE).astype(BF16) for dscore, key in zip(dscores, keys)]
     return list(zip(dqueries, dkeys, dvalues))
@@ -85,6 +91,11 @@
     return pl.ds(pl.multiple_of(order_ref[slot] * HEAD + block * WIDTH, HEAD), HEAD)
 
 
+def scalars(ref):
+    lane = lax.broadcasted_iota(jnp.int32, (1, HEADS), 1)
+    return [ref[0, slot] for slot in range(HEADS)]
+
+
 def narrow_lanes(slot, block=0):
     return slice(block * NARROW + slot * HEAD, block * NARROW + (slot + 1) * HEAD)
 
@@ -95,7 +106,31 @@
     return copy
 
 
+def start_low(normed_ref, down_ref, normed_own, down_own, wide_sems, rows):
+    copies = []
+    span = MODEL // WIDE
+    for part in range(WIDE):
+        lanes = slice(part * span, (part + 1) * span)
+        copies.append(fetch(normed_ref.at[rows, lanes], normed_own.at[rows, lanes], wide_sems.at[0, part]))
+        copies.append(fetch(down_ref.at[:, lanes], down_own.at[:, lanes], wide_sems.at[1, part]))
+    return copies
+
+
+def finish_low(copies, normed_own, down_own, rows):
+    low = None
+    span = MODEL // WIDE
+    for part in range(WIDE):
+        lanes = slice(part * span, (part + 1) * span)
+        for copy in copies[2 * part : 2 * part + 2]:
+            copy.wait()
+        term = dot_last(normed_own[rows, lanes], down_own[:, lanes])
+        low = term if low is None else low + term
+    low = low.astype(BF16)
+    return jnp.concatenate([low, jnp.zeros((low.shape[0], HEAD - 3 * RANK), BF16)], axis=1)
+
+
 def prepare(
+    rows,
     source_ref,
     key_ref,
     value_ref,
@@ -112,60 +147,53 @@
     order_sem,
 ):
     order_copy = fetch(source_ref, order_ref, order_sem)
-    pair_copies, wide_copies = [], []
-    for item, source in enumerate((key_ref, value_ref)):
-        copy = pltpu.make_async_copy(source.at[HALF:], pair_own.at[item], pair_sems.at[item])
-        copy.start()
-        pair_copies.append(copy)
-    span = MODEL // WIDE
-    for part in range(WIDE):
-        lanes = slice(part * span, (part + 1) * span)
-        for item, (source, target) in enumerate(((normed_ref, normed_own), (down_ref, down_own))):
-            copy = pltpu.make_async_copy(source.at[:, lanes], target.at[:, lanes], wide_sems.at[item, part])
-            copy.start()
-            wide_copies.append(copy)
+    pair_copies = [
+        fetch(source.at[HALF:], pair_own.at[item], pair_sems.at[item])
+        for item, source in enumerate((key_ref, value_ref))
+    ]
+    wide_copies = start_low(normed_ref, down_ref, normed_own, down_own, wide_sems, rows)
     order_copy.wait()
     for item in range(2):
         pair_copies[item].wait()
         for slot in range(SHIFTED):
             place = item * SHIFTED + slot
             send_ref[:, place * HEAD : (place + 1) * HEAD] = pair_own[item, :, lanes_of(order_ref, slot)]
-    low = jnp.zeros((ROWS, 3 * RANK), F32)
-    for part in range(WIDE):
-        lanes = slice(part * span, (part + 1) * span)
-        for copy in wide_copies[2 * part : 2 * part + 2]:
-            copy.wait()
-        low = low + dot_last(normed_own[:, lanes], down_own[:, lanes])
-    low = jnp.concatenate([low.astype(BF16), jnp.zeros((ROWS, HEAD - 3 * RANK), BF16)], axis=1)
+    low = finish_low(wide_copies, normed_own, down_own, rows)
     low_ref[...] = low
-    send_ref[:, 2 * SHIFTED * HEAD :] = low[HALF:]
+    send_ref[:, 2 * SHIFTED * HEAD :] = low[low.shape[0] - HALF :]
 
 
 def outer_kernel(*refs):
     @pl.when(lax.axis_index("c") == 1)
     def _():
-        prepare(*refs)
-
-
-def inner_kernel(have_ref, *refs):
+        prepare(slice(HALF, ROWS), *refs)
+
+
+def inner_kernel(tail_ref, *refs):
     core = lax.axis_index("c")
 
     @pl.when(core == 0)
     def _():
-        prepare(*refs)
+        prepare(slice(0, ROWS), *refs)
 
     @pl.when(core == 1)
     def _():
-        refs[6][...] = have_ref[...]
-
-
-def project(order_ref, grads_ref, up_ref, slots):
-    total = jnp.zeros((grads_ref.shape[0], HEAD), F32)
-    for block in range(3):
+        normed_ref, down_ref, low_ref = refs[3], refs[4], refs[6]
+        normed_own, down_own, wide_sems = refs[8], refs[9], refs[11]
+        rows = slice(0, HALF)
+        copies = start_low(normed_ref, down_ref, normed_own, down_own, wide_sems, rows)
+        low_ref[:HALF, :] = finish_low(copies, normed_own, down_own, rows)
+        low_ref[HALF:, :] = tail_ref[...]
+
+
+def project(order_ref, grads_ref, up_ref, slots, blocks=range(3), rows=slice(None)):
+    total = None
+    for block in blocks:
         up = jnp.concatenate([up_ref[:, lanes_of(order_ref, slot, block)] for slot in slots], axis=1)
         parts = [up if place == block else jnp.zeros_like(up) for place in range(4)]
         columns = slice(block * NARROW, (block + 1) * NARROW)
-        total = total + dot_last(grads_ref[:, columns], jnp.concatenate(parts, axis=0))
+        term = dot_last(grads_ref[rows, columns], jnp.concatenate(parts, axis=0))
+        total = term if total is None else total + term
     return total
 
 
@@ -187,12 +215,9 @@
     plain_proj_ref[...] = project(order_ref, plain_ref, up_ref, slots)
 
 
-def joint_work(
-    order_ref, refs, come_ref, up_ref, plain_proj_ref, half_proj_ref, late_ref, proj_ref, back_ref, far_ref
-):
+def joint_work(order_ref, refs, come_ref, up_ref, late_ref, back_ref, far_ref, dscore_ref):
     query_ref, key_ref, value_ref, cot_ref = refs
     far_ref[...] = come_ref[:, 2 * SHIFTED * HEAD :]
-    nothing = jnp.zeros((HALF, HEAD), BF16)
     slots = range(SHIFTED)
     parts = []
     for slot in slots:
@@ -202,22 +227,34 @@
             for place, ref in ((slot, key_ref), (SHIFTED + slot, value_ref))
         )
         parts.append([query_ref[:HALF, lanes], key, value, cot_ref[:HALF, lanes]])
-    for slot, (dquery, dkey, dvalue) in zip(slots, attend(parts, causal(ROWS, HALF, HALF))):
-        late_ref[:HALF, narrow_lanes(slot)] = dquery
-        late_ref[HALF:, narrow_lanes(slot)] = nothing
-        for block, grad in ((1, dkey), (2, dvalue)):
+    weights, dscores = scores_of(parts, causal(ROWS, HALF, HALF))
+    for slot, (query, _, _, cotangent) in zip(slots, parts):
+        dscore_ref[slot] = dscores[slot]
+        for block, grad in ((1, dot(dscores[slot], query) * SCALE), (2, dot(weights[slot], cotangent))):
+            grad = grad.astype(BF16)
             late_ref[:HALF, narrow_lanes(slot, block)] = grad[HALF:]
             late_ref[HALF:, narrow_lanes(slot, block)] = grad[:HALF]
-    total = project(order_ref, late_ref, up_ref, slots)
+    back_ref[...] = project(order_ref, late_ref, up_ref, slots, (1, 2), slice(HALF, ROWS))
+
+
+def rest_work(
+    order_ref, key_ref, come_ref, up_ref, late_ref, dscore_ref, plain_proj_ref, half_proj_ref, dquery_ref, proj_ref
+):
+    slots = range(SHIFTED)
+    for slot in slots:
+        far_key = come_ref[:, slot * HEAD : (slot + 1) * HEAD]
+        key = jnp.concatenate([far_key, key_ref[:HALF, lanes_of(order_ref, slot)]], axis=0)
+        dquery_ref[:, narrow_lanes(slot)] = (dot_first(dscore_ref[slot], key) * SCALE).astype(BF16)
+    total = project(order_ref, late_ref, up_ref, slots, (1, 2), slice(0, HALF))
+    total = total + project(order_ref, dquery_ref, up_ref, slots, (0,))
     plain = plain_proj_ref[...]
-    proj_ref[...] = jnp.concatenate([plain[:HALF] + total[:HALF], plain[HALF:] + half_proj_ref[...]], axis=0)
-    back_ref[...] = total[HALF:]
+    proj_ref[...] = jnp.concatenate([plain[:HALF] + total, plain[HALF:] + half_proj_ref[...]], axis=0)
 
 
 def own_kernel(*refs):
     source_ref, inputs, up_ref = refs[0], refs[1:5], refs[5]
-    half_refs, plain_refs, (order_ref, order_sem) = refs[6:8], refs[8:10], refs[10:]
-    fetch(source_ref, order_ref, order_sem).wait()
+    half_refs, plain_refs = refs[6:8], refs[8:10]
+    order_ref = scalars(source_ref)
 
     @pl.when(lax.axis_index("c") == 0)
     def _():
@@ -227,50 +264,68 @@
 
 
 def joint_kernel(*refs):
-    source_ref, inputs, rest, (order_ref, order_sem) = refs[0], refs[1:5], refs[5:-2], refs[-2:]
+    source_ref, inputs, rest = refs[0], refs[1:5], refs[5:]
 
     @pl.when(lax.axis_index("c") == 0)
     def _():
-        fetch(source_ref, order_ref, order_sem).wait()
-        joint_work(order_ref, inputs, *rest)
+        joint_work(scalars(source_ref), inputs, *rest)
+
+
+def rest_kernel(source_ref, *refs):
+    @pl.when(lax.axis_index("c") == 0)
+    def _():
+        rest_work(scalars(source_ref), *refs)
 
 
 def later_kernel(*refs):
     source_ref, inputs, come_ref, up_ref, half_proj_ref = refs[0], refs[1:5], refs[5], refs[6], refs[7]
-    plain_ref, outs, (plain_proj_ref, order_ref, order_sem) = refs[9], refs[10:14], refs[14:]
+    plain_ref, late_ref, back_ref, far_ref, dquery_ref, proj_ref, plain_proj_ref, dscore_ref = refs[9:]
 
     @pl.when(lax.axis_index("c") == 1)
     def _():
-        fetch(source_ref, order_ref, order_sem).wait()
+        order_ref = scalars(source_ref)
         plain_work(order_ref, inputs, up_ref, plain_ref, plain_proj_ref)
-        joint_work(order_ref, inputs, come_ref, up_ref, plain_proj_ref, half_proj_ref, *outs)
-
-
-def accumulate(order_ref, order_copy, plain_ref, late_ref, far_ref, half_ref, low_ref, sums_ref):
+        joint_work(order_ref, inputs, come_ref, up_ref, late_ref, back_ref, far_ref, dscore_ref)
+        rest_work(
+            order_ref,
+            inputs[1],
+            come_ref,
+            up_ref,
+            late_ref,
+            dscore_ref,
+            plain_proj_ref,
+            half_proj_ref,
+            dquery_ref,
+            proj_ref,
+        )
+
+
+def accumulate(order_ref, plain_ref, late_ref, far_ref, dquery_ref, half_ref, low_ref, sums_ref):
     low = low_ref[...]
-    late_low = jnp.concatenate([low[:HALF], far_ref[...], low[HALF:]], axis=0)
+    late_low = jnp.concatenate([low, far_ref[...]], axis=0)
     rights = [
         [jnp.concatenate([item[:, block * RANK : (block + 1) * RANK]] * 4, axis=1) for block in range(3)]
         for item in (low, late_low)
     ]
-    order_copy.wait()
     for block in range(3):
         for slot in range(SHIFTED):
             lanes = narrow_lanes(slot, block)
             sums_ref[lanes_of(order_ref, SHIFTED + slot, block), :] = dot_first(plain_ref[:, lanes], rights[0][block])
-            left = jnp.concatenate([late_ref[:, lanes], half_ref[:, lanes]], axis=0)
-            sums_ref[lanes_of(order_ref, slot, block), :] = dot_first(left, rights[1][block])
+            first = late_ref[:HALF, lanes] if block else dquery_ref[:, lanes]
+            left = [first, half_ref[:, lanes]] + [late_ref[HALF:, lanes]] * (block > 0)
+            right = rights[1 if block else 0][block]
+            sums_ref[lanes_of(order_ref, slot, block), :] = dot_first(jnp.concatenate(left, axis=0), right)
 
 
 def up_kernel(*refs):
-    source_ref, parts, half_ref, low_ref = refs[0], (refs[1:4], refs[4:7]), refs[7], refs[8]
-    out_ref, sums_ref, order_ref, order_sem = refs[9:]
-    order_copy = fetch(source_ref, order_ref, order_sem)
+    source_ref, parts, half_ref, low_ref = refs[0], (refs[1:5], refs[5:9]), refs[9], refs[10]
+    out_ref, sums_ref = refs[11:]
+    order_ref = scalars(source_ref)
     for core in range(C):
 
         @pl.when(lax.axis_index("c") == core)
         def _():
-            accumulate(order_ref, order_copy, *parts[core], half_ref, low_ref, sums_ref)
+            accumulate(order_ref, *parts[core], half_ref, low_ref, sums_ref)
 
     place = lax.broadcasted_iota(jnp.int32, (8, HEAD), 1) // RANK
     upper = lax.broadcasted_iota(jnp.int32, (8, HEAD), 0) < 4
@@ -356,11 +411,11 @@
     return jax.ShapeDtypeStruct(dims, kind)
 
 
-def prepare_call(body, name, extra, order, keys, values, normed, down):
+def prepare_call(body, name, rows, extra, order, keys, values, normed, down):
     return call(
         body,
         name,
-        (shape((HALF, (2 * SHIFTED + 1) * HEAD)), shape((ROWS, HEAD))),
+        (shape((HALF, (2 * SHIFTED + 1) * HEAD)), shape((rows, HEAD))),
         [VMEM] * len(extra) + [ANY] + [HBM] * 4,
         130_000_000,
         3_000_000,
@@ -378,7 +433,9 @@
 
 PLAIN = (shape((ROWS, 3 * NARROW)), shape((ROWS, HEAD), F32))
 HALVES = (shape((HALF, 3 * NARROW)), shape((HALF, HEAD), F32))
-JOINT = (shape((ROWS, 3 * NARROW)), shape((ROWS, HEAD), F32), shape((HALF, HEAD), F32), shape((HALF, HEAD)))
+JOINT = (shape((ROWS, 3 * NARROW)), shape((HALF, HEAD), F32), shape((HALF, HEAD)))
+DSCORE = (SHIFTED, ROWS, HALF)
+REST = (shape((HALF, NARROW)), shape((ROWS, HEAD), F32))
 
 
 def work_call(body, name, out_shape, inputs, flops, scratch=()):
@@ -386,10 +443,10 @@
         body,
         name,
         out_shape,
-        [ANY] + [VMEM] * (len(inputs) - 1),
+        [VMEM] * len(inputs),
         flops,
         6_000_000,
-        scratch_shapes=[*scratch, *ORDER],
+        scratch_shapes=scratch,
     )(*inputs)
 
 
@@ -421,36 +478,40 @@
     ahead = [(item, (item + 1) % count) for item in range(count)]
     behind = [(item, (item - 1) % count) for item in range(count)]
     sources = (order, keys, values, normed, down.T)
+    order = order.reshape(1, HEADS)
     inputs = (order, queries, keys, values, cotangent)
-    send, low = prepare_call(outer_kernel, "outer_parts", (), *sources)
+    send, tail = prepare_call(outer_kernel, "outer_parts", HALF, (), *sources)
     outer = lax.ppermute(send, ring, ahead[1::2])
-    send, low = prepare_call(inner_kernel, "inner_parts", (low,), *sources)
+    send, low = prepare_call(inner_kernel, "inner_parts", ROWS, (tail,), *sources)
     inner = lax.ppermute(send, ring, ahead[::2])
     half, half_proj, plain, plain_proj = work_call(
         own_kernel, "own_attention", HALVES + PLAIN, (*inputs, up), 2_000_000_000
     )
-    late, proj, back, far = work_call(
-        joint_kernel, "joint_attention", JOINT, (*inputs, outer, up, plain_proj, half_proj), 1_000_000_000
+    late, back, far, dscore = work_call(
+        joint_kernel, "joint_attention", (*JOINT, shape(DSCORE)), (*inputs, outer, up), 1_000_000_000
     )
     outer_back = lax.ppermute(back, ring, behind[::2])
+    dquery, proj = work_call(
+        rest_kernel, "rest_attention", REST, (order, keys, outer, up, late, dscore, plain_proj, half_proj), 500_000_000
+    )
     later = work_call(
         later_kernel,
         "later_attention",
-        PLAIN[:1] + JOINT,
+        PLAIN[:1] + JOINT + REST,
         (*inputs, inner, up, half_proj, far),
         3_000_000_000,
-        [pltpu.VMEM(PLAIN[1].shape, F32)],
-    )
-    inner_back = lax.ppermute(later[3], ring, behind[1::2])
+        [pltpu.VMEM(PLAIN[1].shape, F32), pltpu.VMEM(DSCORE, BF16)],
+    )
+    inner_back = lax.ppermute(later[2], ring, behind[1::2])
     up_part = work_call(
         up_kernel,
         "up_gradient",
         shape((C, G, PART, HEAD)),
-        (order, plain, late, far, later[0], later[1], later[4], half, low),
+        (order, plain, late, far, dquery, later[0], later[1], later[3], later[4], half, low),
         1_000_000_000,
         [pltpu.VMEM((3 * WIDTH, HEAD), F32)],
     )
-    mine, other = down_call(normed, proj, later[2], outer_back, inner_back, up_part)
+    mine, other = down_call(normed, proj, later[5], outer_back, inner_back, up_part)
     other = lax.ppermute(other, "c", [(0, 1), (1, 0)])
     chip = (mine.astype(F32) + other.astype(F32)).astype(BF16)
     plane = lax.all_to_all(chip.reshape(G, PART, HEAD), NEAR, 0, 0)

time: 71.8 us -> 70.7 us (0.985)
  starting transfers between devices: 8.86 us -> 10.1 us
  blocking collectives: 48.2 us -> 47 us
  Pallas kernels: 11.1 us -> 10 us
    ppermute x1, starting transfers between devices: 1.95 us -> 3.64 us  [per_device(): inner = lax.ppermute(send, ring, ahead[::2])]
    pallas_call x6 -> x7, Pallas kernels: 9.43 us -> 8.35 us  [the longest x5 5.86 us: work_call(): call(body, name, out_shape, [VMEM] * len(inputs), flops, 6000000, scratch...]
    all_to_all x1, blocking collectives: 24.6 us -> 23.7 us  [per_device(): plane = lax.all_to_all(chip.reshape(G, PART, HEAD), NEAR, 0, 0)]
  transfers between devices with their start and end apart: 5 -> 5, of which waited for: 1 -> 1; matrix products, arithmetic and copies ran while one was open for 0% -> 0% of each run, Pallas kernels for 13% -> 12%
where the time goes in v6:
time: 70.7 us; the launch traced here: 70.4 us
  blocking collectives  47 us (66%)
  starting transfers between devices  10.1 us (14%)
  Pallas kernels  10 us (14%)
  waiting for transfers between devices  1.62 us (2%)
  between operations  0.87 us (1%)
    all_to_all x1, blocking collectives, per_device(): plane = lax.all_to_all(chip.reshape(G, PART, HEAD), NEAR, 0, 0)  23.7 us
    all_to_all x1, blocking collectives, per_device(): line = lax.all_to_all(middle_call(plane), FAR, 0, 0)  23.2 us
    pallas_call x5, Pallas kernels, work_call(): call(body, name, out_shape, [VMEM] * len(inputs), flops, 6000000, scratch...  5.86 us
    ppermute x1, starting transfers between devices, per_device(): inner = lax.ppermute(send, ring, ahead[::2])  3.64 us
    ppermute x1, starting transfers between devices, per_device(): other = lax.ppermute(other, 'c', [(0, 1), (1, 0)])  2.55 us
    pallas_call x2, Pallas kernels, prepare_call(): call(body, name, (shape((HALF, (2 * SHIFTED + 1) * HEAD)), shape((rows, H...  2.49 us
    ppermute x1, waiting for transfers between devices, per_device(): other = lax.ppermute(other, 'c', [(0, 1), (1, 0)])  1.61 us
  transfers between devices with their start and end apart: 5, of which 1 were waited for; matrix products, arithmetic and copies ran while one was open for 0% of the time, Pallas kernels for 12%

profile of v6, /device:TPU:2, one launch (start us, length us, event | category | flops | bytes accessed | tf_op | source)
XLA Modules:
  0.0 70.4 jit_solution(5989719651622180506)
XLA Ops:
  0.6 0.0 copy-start.4
  0.6 0.6 copy-done.4
  1.3 0.1 outer_parts.1
  1.4 1.3 %collective-permute-start = (bf16[80,2176]{1,0:T(8,128)(2,1)S(1)}, bf16[80,2176]{1,0:T(8,128)(2,1)S(1)}, u32[]{:S(2)}, u32[]{:S(2)}) collective-permute-start(bf16[80,2176]{1,0:T(8,128)(2,1)S(1)} %get-tuple-element.26), channel_id=1, source_target_pairs={{1,2},{3,4},{5,6},{7,8},{9,10},{11,12},{13,14},{15,0},{17,18},{19,... | collective-permute-start | bytes 1044488 | tf_op jit(solution)/shard_map/ppermute | solution.py:484
  2.7 0.0 copy-start.1
  2.7 0.0 copy-start.2
  2.7 0.0 copy-start.3
  2.7 0.0 copy-start.5
  2.7 0.0 copy-start.6
  2.7 2.4 %inner_parts.1 = (bf16[80,2176]{1,0:T(8,128)(2,1)S(1)}, bf16[160,128]{1,0:T(8,128)(2,1)S(1)}) custom-call(bf16[80,128]{1,0:T(8,128)(2,1)S(1)} %get-tuple-element.32.tail_ref, s32[16]{0:T(128)S(1)} %copy-done.4, bf16[160,2048]{1,0:T(8,128)(2,1)} %bitcast.13, bf16[160,2048]{1,0:T(8,128)(2,1)} %bitcast.19, bf16[160,4096]{1,0:T(8,128)(2,1)} %bitcast.10, ...), custom_call_target="tpu_custom_call" | custom-call | flops 130000000 | bytes 3000000 | tf_op jit(solution)/shard_map/inner_parts/pallas_call | solution.py:415
  5.1 3.6 %collective-permute-start.1 = (bf16[80,2176]{1,0:T(8,128)(2,1)S(1)}, bf16[80,2176]{1,0:T(8,128)(2,1)S(1)}, u32[]{:S(2)}, u32[]{:S(2)}) collective-permute-start(bf16[80,2176]{1,0:T(8,128)(2,1)S(1)} %get-tuple-element.33), channel_id=1, source_target_pairs={{0,1},{2,3},{4,5},{6,7},{8,9},{10,11},{12,13},{14,15},{16,17},{18,... | collective-permute-start | bytes 1044488 | tf_op jit(solution)/shard_map/ppermute | solution.py:486
  8.8 0.0 copy-done.1
  8.8 0.0 copy-done.2
  8.8 0.0 copy-done.3
  8.8 0.0 copy-done.5
  8.8 0.0 copy-done.6
  8.8 2.9 %own_attention.1 = (bf16[80,3072]{1,0:T(8,128)(2,1)S(1)}, f32[80,128]{1,0:T(8,128)S(1)}, bf16[160,3072]{1,0:T(8,128)(2,1)S(1)}, f32[160,128]{1,0:T(8,128)S(1)}) custom-call(s32[1,16]{1,0:T(1,128)S(1)} %bitcast.23, bf16[160,2048]{1,0:T(8,128)(2,1)S(1)} %bitcast.28, bf16[160,2048]{1,0:T(8,128)(2,1)S(1)} %bitcast.14, bf16[160,2048]{1,0:T(8,128)(2,1)S(1)} %bitcast.20, ...), custom_call_target="tpu_custom_call" | custom-call | flops 2000000000 | bytes 6000000 | tf_op jit(solution)/shard_map/own_attention/pallas_call | solution.py:442
  11.7 0.0 collective-permute-done.refs_5_.refs_1_
  11.8 1.0 %joint_attention.1 = (bf16[160,3072]{1,0:T(8,128)(2,1)S(1)}, f32[80,128]{1,0:T(8,128)S(1)}, bf16[80,128]{1,0:T(8,128)(2,1)S(1)}, bf16[8,160,80]{2,1,0:T(8,128)(2,1)S(1)}) custom-call(s32[1,16]{1,0:T(1,128)S(1)} %bitcast.24, bf16[160,2048]{1,0:T(8,128)(2,1)S(1)} %bitcast.29, bf16[160,2048]{1,0:T(8,128)(2,1)S(1)} %bitcast.15, bf16[160,2048]{1,0:T(8,128)(2,1)S(1)} %bitcast.21, ...), custom_call_target="tpu_custom_call" | custom-call | flops 1000000000 | bytes 6000000 | tf_op jit(solution)/shard_map/joint_attention/pallas_call | solution.py:442
  12.8 1.3 %collective-permute-start.2 = (f32[80,128]{1,0:T(8,128)S(1)}, f32[80,128]{1,0:T(8,128)S(1)}, u32[]{:S(2)}, u32[]{:S(2)}) collective-permute-start(f32[80,128]{1,0:T(8,128)S(1)} %get-tuple-element.36), channel_id=1, source_target_pairs={{0,15},{2,1},{4,3},{6,5},{8,7},{10,9},{12,11},{14,13},{16,31},{18,... | collective-permute-start | bytes 122888 | tf_op jit(solution)/shard_map/ppermute | solution.py:493
  14.1 0.0 collective-permute-done.1.refs_5_
  14.2 1.3 %collective-permute-start.3 = (f32[80,128]{1,0:T(8,128)S(1)}, f32[80,128]{1,0:T(8,128)S(1)}, u32[]{:S(2)}, u32[]{:S(2)}) collective-permute-start(f32[80,128]{1,0:T(8,128)S(1)} %get-tuple-element.37), channel_id=1, source_target_pairs={{1,0},{3,2},{5,4},{7,6},{9,8},{11,10},{13,12},{15,14},{17,16},{19,... | collective-permute-start | bytes 122888 | tf_op jit(solution)/shard_map/ppermute | solution.py:505
  15.5 0.5 rest_attention.1
  16.0 0.0 copy-start
  16.0 1.4 %up_gradient.1.up_ref = bf16[2,16,144,128]{3,2,1,0:T(8,128)(2,1)S(1)} custom-call(s32[1,16]{1,0:T(1,128)S(1)} %bitcast.27, bf16[160,3072]{1,0:T(8,128)(2,1)S(1)} %get-tuple-element.38.refs_1_, bf16[160,3072]{1,0:T(8,128)(2,1)S(1)} %get-tuple-element.27.refs_3_.refs_2_, bf16[80,128]{1,0:T(8,128)(2,1)S(1)} %get-tuple-element.34.refs_8_.refs_3_, ...), custom_call_target="tpu_custom_call" | custom-call | flops 1000000000 | bytes 6000000 | tf_op jit(solution)/shard_map/up_gradient/pallas_call | solution.py:442
  17.4 0.0 collective-permute-done.2.outer_ref
  17.4 0.0 collective-permute-done.3.inner_ref
  17.4 0.0 copy-done
  17.4 0.8 %down_gradient.1 = (bf16[2304,128]{1,0:T(8,128)(2,1)S(1)}, bf16[2304,128]{1,0:T(8,128)(2,1)S(1)}) custom-call(bf16[160,4096]{1,0:T(8,128)(2,1)S(1)} %bitcast.11, f32[160,128]{1,0:T(8,128)S(1)} %get-tuple-element.31.first_ref, f32[160,128]{1,0:T(8,128)S(1)} %get-tuple-element.35.later_ref, f32[80,128]{1,0:T(8,128)S(1)} %collective-permute-done.2.outer_ref, ...), custom_call_target="tpu_custom_call" | custom-call | flops 500000000 | bytes 4000000 | tf_op jit(solution)/shard_map/down_gradient/pallas_call | solution.py:454
  18.2 2.6 %collective-permute-start.4 = (bf16[2304,128]{1,0:T(8,128)(2,1)S(1)}, bf16[2304,128]{1,0:T(8,128)(2,1)S(1)}, u32[]{:S(2)}, u32[]{:S(2)}) collective-permute-start(bf16[2304,128]{1,0:T(8,128)(2,1)S(1)} %get-tuple-element.47), channel_id=1, source_target_pairs={{0,1},{1,0},{2,3},{3,2},{4,5},{5,4},{6,7},{7,6},{8,9},{9,8},{10,11... | collective-permute-start | bytes 1769480 | tf_op jit(solution)/shard_map/ppermute | solution.py:515
  20.8 1.6 %collective-permute-done.4 = bf16[2304,128]{1,0:T(8,128)(2,1)S(1)} collective-permute-done((bf16[2304,128]{1,0:T(8,128)(2,1)S(1)}, bf16[2304,128]{1,0:T(8,128)(2,1)S(1)}, u32[]{:S(2)}, u32[]{:S(2)}) %collective-permute-start.4) | collective-permute-done | bytes 589856 | tf_op jit(solution)/shard_map/ppermute | solution.py:515
  22.4 0.2 add_convert_fusion
  22.6 23.7 %all_to_all.10.come_ref = bf16[16,144,128]{2,1,0:T(8,128)(2,1)S(1)} all-to-all(bf16[16,144,128]{2,1,0:T(8,128)(2,1)S(1)} %bitcast.36), channel_id=1, replica_groups=mesh['z'=16,'yl'=2,'yh'=2,'x'=4,'c'=2] {'yl','yh','x'}, dimensions={0} | all-to-all | bytes 1179648 | tf_op jit(solution)/shard_map/all_to_all | solution.py:517
  46.3 0.1 middle_sum.1
  46.4 23.2 %all_to_all.11.come_ref = bf16[16,16,128]{2,1,0:T(8,128)(2,1)S(1)} all-to-all(bf16[16,16,128]{2,1,0:T(8,128)(2,1)S(1)} %middle_sum.1), channel_id=1, replica_groups=mesh['z'=16,'yl'=2,'yh'=2,'x'=4,'c'=2] {'z'}, dimensions={0} | all-to-all | bytes 131072 | tf_op jit(solution)/shard_map/all_to_all | solution.py:518
  69.6 0.8 %last_sum.1 = (bf16[8,96]{1,0:T(8,128)(2,1)}, bf16[12,32]{1,0:T(8,128)(2,1)}) custom-call(bf16[16,16,128]{2,1,0:T(8,128)(2,1)S(1)} %all_to_all.11.come_ref), custom_call_target="tpu_custom_call" | custom-call | flops 100000 | bytes 70000 | tf_op jit(solution)/shard_map/last_sum/pallas_call | solution.py:469
  (1 shorter events, 0.0 us)
Async XLA Ops:
  0.6 0.7 copy-start.4
  1.4 10.4 %collective-permute-start = (bf16[80,2176]{1,0:T(8,128)(2,1)S(1)}, bf16[80,2176]{1,0:T(8,128)(2,1)S(1)}, u32[]{:S(2)}, u32[]{:S(2)}) collective-permute-start(bf16[80,2176]{1,0:T(8,128)(2,1)S(1)} %get-tuple-element.26), channel_id=1, source_target_pairs={{1,2},{3,4},{5,6},{7,8},{9,10},{11,12},{13,14},{15,0},{17,18},{19,... | collective-permute-start | bytes 1044488 | tf_op jit(solution)/shard_map/ppermute | solution.py:484
  2.7 6.1 %copy-start.1 = (bf16[1,160,2048]{2,1,0:T(8,128)(2,1)S(1)}, bf16[1,160,2048]{2,1,0:T(8,128)(2,1)}, u32[]{:S(2)}) copy-start(bf16[1,160,2048]{2,1,0:T(8,128)(2,1)} %param.10) | copy-start | bytes 1966084
  2.7 6.1 %copy-start.2 = (bf16[1,160,2048]{2,1,0:T(8,128)(2,1)S(1)}, bf16[1,160,2048]{2,1,0:T(8,128)(2,1)}, u32[]{:S(2)}) copy-start(bf16[1,160,2048]{2,1,0:T(8,128)(2,1)} %param.11) | copy-start | bytes 1966084
  2.7 6.1 %copy-start.3 = (bf16[32,6144]{1,0:T(8,128)(2,1)S(1)}, bf16[32,6144]{1,0:T(8,128)(2,1)}, u32[]{:S(2)}) copy-start(bf16[32,6144]{1,0:T(8,128)(2,1)} %refs_6_.3) | copy-start | bytes 1179652
  2.7 6.1 %copy-start.5 = (bf16[1,160,2048]{2,1,0:T(8,128)(2,1)S(1)}, bf16[1,160,2048]{2,1,0:T(8,128)(2,1)}, u32[]{:S(2)}) copy-start(bf16[1,160,2048]{2,1,0:T(8,128)(2,1)} %param.9) | copy-start | bytes 1966084
  2.7 6.1 %copy-start.6 = (bf16[1,160,2048]{2,1,0:T(8,128)(2,1)S(1)}, bf16[1,160,2048]{2,1,0:T(8,128)(2,1)}, u32[]{:S(2)}) copy-start(bf16[1,160,2048]{2,1,0:T(8,128)(2,1)} %param.12) | copy-start | bytes 1966084
  5.1 9.0 %collective-permute-start.1 = (bf16[80,2176]{1,0:T(8,128)(2,1)S(1)}, bf16[80,2176]{1,0:T(8,128)(2,1)S(1)}, u32[]{:S(2)}, u32[]{:S(2)}) collective-permute-start(bf16[80,2176]{1,0:T(8,128)(2,1)S(1)} %get-tuple-element.33), channel_id=1, source_target_pairs={{0,1},{2,3},{4,5},{6,7},{8,9},{10,11},{12,13},{14,15},{16,17},{18,... | collective-permute-start | bytes 1044488 | tf_op jit(solution)/shard_map/ppermute | solution.py:486
  12.8 4.6 %collective-permute-start.2 = (f32[80,128]{1,0:T(8,128)S(1)}, f32[80,128]{1,0:T(8,128)S(1)}, u32[]{:S(2)}, u32[]{:S(2)}) collective-permute-start(f32[80,128]{1,0:T(8,128)S(1)} %get-tuple-element.36), channel_id=1, source_target_pairs={{0,15},{2,1},{4,3},{6,5},{8,7},{10,9},{12,11},{14,13},{16,31},{18,... | collective-permute-start | bytes 122888 | tf_op jit(solution)/shard_map/ppermute | solution.py:493
  14.2 3.2 %collective-permute-start.3 = (f32[80,128]{1,0:T(8,128)S(1)}, f32[80,128]{1,0:T(8,128)S(1)}, u32[]{:S(2)}, u32[]{:S(2)}) collective-permute-start(f32[80,128]{1,0:T(8,128)S(1)} %get-tuple-element.37), channel_id=1, source_target_pairs={{1,0},{3,2},{5,4},{7,6},{9,8},{11,10},{13,12},{15,14},{17,16},{19,... | collective-permute-start | bytes 122888 | tf_op jit(solution)/shard_map/ppermute | solution.py:505
  16.0 1.4 %copy-start = (bf16[1,160,4096]{2,1,0:T(8,128)(2,1)S(1)}, bf16[1,160,4096]{2,1,0:T(8,128)(2,1)}, u32[]{:S(2)}) copy-start(bf16[1,160,4096]{2,1,0:T(8,128)(2,1)} %param.8) | copy-start | bytes 3932164
  18.2 4.2 %collective-permute-start.4 = (bf16[2304,128]{1,0:T(8,128)(2,1)S(1)}, bf16[2304,128]{1,0:T(8,128)(2,1)S(1)}, u32[]{:S(2)}, u32[]{:S(2)}) collective-permute-start(bf16[2304,128]{1,0:T(8,128)(2,1)S(1)} %get-tuple-element.47), channel_id=1, source_target_pairs={{0,1},{1,0},{2,3},{3,2},{4,5},{5,4},{6,7},{7,6},{8,9},{9,8},{10,11... | collective-permute-start | bytes 1769480 | tf_op jit(solution)/shard_map/ppermute | solution.py:515

commit v7 on v6

--- a/solution.py
+++ b/solution.py
@@ -356,29 +356,57 @@
             out_ref[c, g, Z * 8 :, :] = jnp.concatenate(rows, axis=0).astype(BF16)
 
 
-def down_kernel(normed_ref, first_ref, later_ref, outer_ref, inner_ref, up_ref, mine_ref, other_ref):
-    own = lax.axis_index("c")
-    total = jnp.where(own == 0, first_ref[...], later_ref[...])
-    back = jnp.where(own == 0, inner_ref[...], outer_ref[...])
-    total = jnp.concatenate([total[:HALF], total[HALF:] + back], axis=0).astype(BF16)
+def down_work(own, normed_ref, proj_ref, back_ref, up_ref, mine_ref, other_ref):
+    total = proj_ref[...]
+    total = jnp.concatenate([total[:HALF], total[HALF:] + back_ref[...]], axis=0).astype(BF16)
     lane = lax.broadcasted_iota(jnp.int32, (16, HEAD), 1)
+    outs = (mine_ref, other_ref) if own == 0 else (other_ref, mine_ref)
     for z in range(0, Z, 2):
         part = dot_first(normed_ref[:, z * G * 16 : (z + 2) * G * 16], total)
         part = part.reshape(2, G, C, 8, HEAD)
         for g in range(G):
-            pieces = []
+            start = g * PART + z * 8
             for c in range(C):
                 down = jnp.concatenate([part[0, g, c], part[1, g, c]], axis=0)
                 up = up_ref[c, g, z * 8 : z * 8 + 16, :]
-                pieces.append(jnp.where(lane < 3 * RANK, down, up.astype(F32)).astype(BF16))
-            start = g * PART + z * 8
-            mine_ref[start : start + 16, :] = jnp.where(own == 0, pieces[0], pieces[1])
-            other_ref[start : start + 16, :] = jnp.where(own == 0, pieces[1], pieces[0])
+                outs[c][start : start + 16, :] = jnp.where(lane < 3 * RANK, down, up.astype(F32)).astype(BF16)
     for g in range(G):
-        span = slice(g * PART + Z * 8, (g + 1) * PART)
-        pieces = [up_ref[c, g, Z * 8 :, :] for c in range(C)]
-        mine_ref[span, :] = jnp.where(own == 0, pieces[0], pieces[1])
-        other_ref[span, :] = jnp.where(own == 0, pieces[1], pieces[0])
+        for c in range(C):
+            outs[c][g * PART + Z * 8 : (g + 1) * PART, :] = up_ref[c, g, Z * 8 :, :]
+
+
+def early_down_kernel(normed_ref, proj_ref, back_ref, up_ref, mine_ref, other_ref, ready_ref):
+    ready_ref[...] = jnp.zeros_like(ready_ref)
+
+    @pl.when(lax.axis_index("c") == 0)
+    def _():
+        down_work(0, normed_ref, proj_ref, back_ref, up_ref, mine_ref, other_ref)
+
+
+def late_down_kernel(ready_ref, normed_ref, proj_ref, back_ref, up_ref, mine_ref, other_ref):
+    del ready_ref
+
+    @pl.when(lax.axis_index("c") == 1)
+    def _():
+        down_work(1, normed_ref, proj_ref, back_ref, up_ref, mine_ref, other_ref)
+
+
+def second_kernel(second_ref, second_come_ref, out_ref):
+    @pl.when(lax.axis_index("c") == 1)
+    def _():
+        out_ref[...] = (second_ref[...].astype(F32) + second_come_ref[...].astype(F32)).astype(BF16)
+
+
+def chip_kernel(first_ref, first_come_ref, second_ref, out_ref):
+    core = lax.axis_index("c")
+
+    @pl.when(core == 0)
+    def _():
+        out_ref[...] = (first_ref[...].astype(F32) + first_come_ref[...].astype(F32)).astype(BF16)
+
+    @pl.when(core == 1)
+    def _():
+        out_ref[...] = second_ref[...]
 
 
 def middle_kernel(come_ref, out_ref):
@@ -450,15 +478,7 @@
     )(*inputs)
 
 
-def down_call(*inputs):
-    return call(
-        down_kernel,
-        "down_gradient",
-        (shape((G * PART, HEAD)), shape((G * PART, HEAD))),
-        [VMEM] * 6,
-        500_000_000,
-        4_000_000,
-    )(*inputs)
+PILE = shape((G * PART, HEAD))
 
 
 def middle_call(come):
@@ -511,9 +531,24 @@
         1_000_000_000,
         [pltpu.VMEM((3 * WIDTH, HEAD), F32)],
     )
-    mine, other = down_call(normed, proj, later[5], outer_back, inner_back, up_part)
-    other = lax.ppermute(other, "c", [(0, 1), (1, 0)])
-    chip = (mine.astype(F32) + other.astype(F32)).astype(BF16)
+    first, first_other, ready = work_call(
+        early_down_kernel,
+        "early_down_gradient",
+        (PILE, PILE, shape((8, HEAD), F32)),
+        (normed, proj, inner_back, up_part),
+        500_000_000,
+    )
+    second_come = lax.ppermute(first_other, "c", [(0, 1)])
+    second, second_other = work_call(
+        late_down_kernel,
+        "late_down_gradient",
+        (PILE, PILE),
+        (ready, normed, later[5], outer_back, up_part),
+        500_000_000,
+    )
+    first_come = lax.ppermute(second_other, "c", [(1, 0)])
+    second = work_call(second_kernel, "second_sum", PILE, (second, second_come), 1_000_000)
+    chip = work_call(chip_kernel, "chip_sum", PILE, (first, first_come, second), 1_000_000)
     plane = lax.all_to_all(chip.reshape(G, PART, HEAD), NEAR, 0, 0)
     line = lax.all_to_all(middle_call(plane), FAR, 0, 0)
     down_grad, up_grad = last_call(line)

time: 70.7 us -> 71.1 us (level)
  blocking collectives: 47 us -> 45.9 us
  waiting for transfers between devices: 1.62 us -> 2.61 us
    all_to_all x1, blocking collectives: 23.7 us -> 22.3 us  [per_device(): plane = lax.all_to_all(chip.reshape(G, PART, HEAD), NEAR, 0, 0)]
    ppermute x1 -> x2, waiting for transfers between devices: 1.61 us -> 2.6 us  [the longest x1 2.35 us: per_device(): first_come = lax.ppermute(second_other, 'c', [(1, 0)])]
    pallas_call x5 -> x9, Pallas kernels: 5.86 us -> 6.8 us  [work_call(): call(body, name, out_shape, [VMEM] * len(inputs), flops, 6000000, scratch...]
    pallas_call x1 -> x0, Pallas kernels: 0.82 us -> none  [down_call(): call(down_kernel, 'down_gradient', (shape((G * PART, HEAD)), shape((G * P...]
    ppermute x1 -> x2, starting transfers between devices: 2.55 us -> 3.09 us  [the longest x1 1.8 us: per_device(): second_come = lax.ppermute(first_other, 'c', [(0, 1)])]
  transfers between devices with their start and end apart: 5 -> 6, of which waited for: 1 -> 2; matrix products, arithmetic and copies ran while one was open for 0% -> 0% of each run, Pallas kernels for 12% -> 13%
where the time goes in v7:
time: 71.1 us; the launch traced here: 70.8 us
  blocking collectives  45.9 us (65%)
  starting transfers between devices  10.6 us (15%)
  Pallas kernels  10.1 us (14%)
  waiting for transfers between devices  2.61 us (4%)
  between operations  0.89 us (1%)
    all_to_all x1, blocking collectives, per_device(): line = lax.all_to_all(middle_call(plane), FAR, 0, 0)  23.6 us
    all_to_all x1, blocking collectives, per_device(): plane = lax.all_to_all(chip.reshape(G, PART, HEAD), NEAR, 0, 0)  22.3 us
    pallas_call x9, Pallas kernels, work_call(): call(body, name, out_shape, [VMEM] * len(inputs), flops, 6000000, scratch...  6.8 us
    ppermute x1, starting transfers between devices, per_device(): inner = lax.ppermute(send, ring, ahead[::2])  3.64 us
    pallas_call x2, Pallas kernels, prepare_call(): call(body, name, (shape((HALF, (2 * SHIFTED + 1) * HEAD)), shape((rows, H...  2.49 us
    ppermute x1, waiting for transfers between devices, per_device(): first_come = lax.ppermute(second_other, 'c', [(1, 0)])  2.35 us
    ppermute x1, starting transfers between devices, per_device(): second_come = lax.ppermute(first_other, 'c', [(0, 1)])  1.8 us
  transfers between devices with their start and end apart: 6, of which 2 were waited for; matrix products, arithmetic and copies ran while one was open for 0% of the time, Pallas kernels for 13%

profile of v7, /device:TPU:2, one launch (start us, length us, event | category | flops | bytes accessed | tf_op | source)
XLA Modules:
  0.0 70.8 jit_solution(14120118599116989168)
XLA Ops:
  0.6 0.0 copy-start.4
  0.6 0.6 copy-done.4
  1.3 0.1 outer_parts.1
  1.4 1.3 %collective-permute-start = (bf16[80,2176]{1,0:T(8,128)(2,1)S(1)}, bf16[80,2176]{1,0:T(8,128)(2,1)S(1)}, u32[]{:S(2)}, u32[]{:S(2)}) collective-permute-start(bf16[80,2176]{1,0:T(8,128)(2,1)S(1)} %get-tuple-element.29), channel_id=1, source_target_pairs={{1,2},{3,4},{5,6},{7,8},{9,10},{11,12},{13,14},{15,0},{17,18},{19,... | collective-permute-start | bytes 1044488 | tf_op jit(solution)/shard_map/ppermute | solution.py:504
  2.7 0.0 copy-start.1
  2.7 0.0 copy-start.2
  2.7 0.0 copy-start.3
  2.7 0.0 copy-start.5
  2.7 0.0 copy-start.6
  2.7 2.4 %inner_parts.1 = (bf16[80,2176]{1,0:T(8,128)(2,1)S(1)}, bf16[160,128]{1,0:T(8,128)(2,1)S(1)}) custom-call(bf16[80,128]{1,0:T(8,128)(2,1)S(1)} %get-tuple-element.35.tail_ref, s32[16]{0:T(128)S(1)} %copy-done.4, bf16[160,2048]{1,0:T(8,128)(2,1)} %bitcast.14, bf16[160,2048]{1,0:T(8,128)(2,1)} %bitcast.20, bf16[160,4096]{1,0:T(8,128)(2,1)} %bitcast.10, ...), custom_call_target="tpu_custom_call" | custom-call | flops 130000000 | bytes 3000000 | tf_op jit(solution)/shard_map/inner_parts/pallas_call | solution.py:443
  5.1 3.6 %collective-permute-start.1 = (bf16[80,2176]{1,0:T(8,128)(2,1)S(1)}, bf16[80,2176]{1,0:T(8,128)(2,1)S(1)}, u32[]{:S(2)}, u32[]{:S(2)}) collective-permute-start(bf16[80,2176]{1,0:T(8,128)(2,1)S(1)} %get-tuple-element.36), channel_id=1, source_target_pairs={{0,1},{2,3},{4,5},{6,7},{8,9},{10,11},{12,13},{14,15},{16,17},{18,... | collective-permute-start | bytes 1044488 | tf_op jit(solution)/shard_map/ppermute | solution.py:506
  8.8 0.0 copy-done.1
  8.8 0.0 copy-done.2
  8.8 0.0 copy-done.3
  8.8 0.0 copy-done.5
  8.8 0.0 copy-done.6
  8.8 2.9 %own_attention.1 = (bf16[80,3072]{1,0:T(8,128)(2,1)S(1)}, f32[80,128]{1,0:T(8,128)S(1)}, bf16[160,3072]{1,0:T(8,128)(2,1)S(1)}, f32[160,128]{1,0:T(8,128)S(1)}) custom-call(s32[1,16]{1,0:T(1,128)S(1)} %bitcast.25, bf16[160,2048]{1,0:T(8,128)(2,1)S(1)} %bitcast.30, bf16[160,2048]{1,0:T(8,128)(2,1)S(1)} %bitcast.15, bf16[160,2048]{1,0:T(8,128)(2,1)S(1)} %bitcast.21, ...), custom_call_target="tpu_custom_call" | custom-call | flops 2000000000 | bytes 6000000 | tf_op jit(solution)/shard_map/own_attention/pallas_call | solution.py:470
  11.7 0.0 collective-permute-done.refs_5_.refs_1_
  11.8 1.0 %joint_attention.1 = (bf16[160,3072]{1,0:T(8,128)(2,1)S(1)}, f32[80,128]{1,0:T(8,128)S(1)}, bf16[80,128]{1,0:T(8,128)(2,1)S(1)}, bf16[8,160,80]{2,1,0:T(8,128)(2,1)S(1)}) custom-call(s32[1,16]{1,0:T(1,128)S(1)} %bitcast.26, bf16[160,2048]{1,0:T(8,128)(2,1)S(1)} %bitcast.31, bf16[160,2048]{1,0:T(8,128)(2,1)S(1)} %bitcast.16, bf16[160,2048]{1,0:T(8,128)(2,1)S(1)} %bitcast.22, ...), custom_call_target="tpu_custom_call" | custom-call | flops 1000000000 | bytes 6000000 | tf_op jit(solution)/shard_map/joint_attention/pallas_call | solution.py:470
  12.8 1.3 %collective-permute-start.3 = (f32[80,128]{1,0:T(8,128)S(1)}, f32[80,128]{1,0:T(8,128)S(1)}, u32[]{:S(2)}, u32[]{:S(2)}) collective-permute-start(f32[80,128]{1,0:T(8,128)S(1)} %get-tuple-element.50), channel_id=1, source_target_pairs={{0,15},{2,1},{4,3},{6,5},{8,7},{10,9},{12,11},{14,13},{16,31},{18,... | collective-permute-start | bytes 122888 | tf_op jit(solution)/shard_map/ppermute | solution.py:513
  14.1 0.0 collective-permute-done.1.refs_5_
  14.1 1.3 %collective-permute-start.2 = (f32[80,128]{1,0:T(8,128)S(1)}, f32[80,128]{1,0:T(8,128)S(1)}, u32[]{:S(2)}, u32[]{:S(2)}) collective-permute-start(f32[80,128]{1,0:T(8,128)S(1)} %get-tuple-element.38), channel_id=1, source_target_pairs={{1,0},{3,2},{5,4},{7,6},{9,8},{11,10},{13,12},{15,14},{17,16},{19,... | collective-permute-start | bytes 122888 | tf_op jit(solution)/shard_map/ppermute | solution.py:525
  15.4 0.5 rest_attention.1
  15.9 0.0 copy-start
  16.0 1.4 %up_gradient.1.up_ref = bf16[2,16,144,128]{3,2,1,0:T(8,128)(2,1)S(1)} custom-call(s32[1,16]{1,0:T(1,128)S(1)} %bitcast.29, bf16[160,3072]{1,0:T(8,128)(2,1)S(1)} %get-tuple-element.39.refs_1_, bf16[160,3072]{1,0:T(8,128)(2,1)S(1)} %get-tuple-element.30.refs_3_.refs_2_, bf16[80,128]{1,0:T(8,128)(2,1)S(1)} %get-tuple-element.37.refs_8_.refs_3_, ...), custom_call_target="tpu_custom_call" | custom-call | flops 1000000000 | bytes 6000000 | tf_op jit(solution)/shard_map/up_gradient/pallas_call | solution.py:470
  17.4 0.0 collective-permute-done.2.back_ref
  17.4 0.0 copy-done
  17.4 0.8 %early_down_gradient.1 = (bf16[2304,128]{1,0:T(8,128)(2,1)S(1)}, bf16[2304,128]{1,0:T(8,128)(2,1)S(1)}, f32[8,128]{1,0:T(8,128)S(1)}) custom-call(bf16[160,4096]{1,0:T(8,128)(2,1)S(1)} %bitcast.11, f32[160,128]{1,0:T(8,128)S(1)} %get-tuple-element.34.proj_ref, f32[80,128]{1,0:T(8,128)S(1)} %collective-permute-done.2.back_ref, ...), custom_call_target="tpu_custom_call" | custom-call | flops 500000000 | bytes 6000000 | tf_op jit(solution)/shard_map/early_down_gradient/pallas_call | solution.py:470
  18.2 1.8 %collective-permute-start.5 = (bf16[2304,128]{1,0:T(8,128)(2,1)S(1)}, bf16[2304,128]{1,0:T(8,128)(2,1)S(1)}, u32[]{:S(2)}, u32[]{:S(2)}) collective-permute-start(bf16[2304,128]{1,0:T(8,128)(2,1)S(1)} %get-tuple-element.53), channel_id=1, source_target_pairs={{0,1},{2,3},{4,5},{6,7},{8,9},{10,11},{12,13},{14,15},{16,17},{18,... | collective-permute-start | bytes 1769480 | tf_op jit(solution)/shard_map/ppermute | solution.py:541
  20.0 0.0 collective-permute-done.3.back_ref
  20.0 1.3 %collective-permute-start.4 = (bf16[2304,128]{1,0:T(8,128)(2,1)S(1)}, bf16[2304,128]{1,0:T(8,128)(2,1)S(1)}, u32[]{:S(2)}, u32[]{:S(2)}) collective-permute-start(bf16[2304,128]{1,0:T(8,128)(2,1)S(1)} %get-tuple-element.51), channel_id=1, source_target_pairs={{1,0},{3,2},{5,4},{7,6},{9,8},{11,10},{13,12},{15,14},{17,16},{19,... | collective-permute-start | bytes 1769480 | tf_op jit(solution)/shard_map/ppermute | solution.py:549
  21.3 0.2 collective-permute-done.5.second_come_ref
  21.6 2.4 %collective-permute-done.4.first_come_ref = bf16[2304,128]{1,0:T(8,128)(2,1)S(1)} collective-permute-done((bf16[2304,128]{1,0:T(8,128)(2,1)S(1)}, bf16[2304,128]{1,0:T(8,128)(2,1)S(1)}, u32[]{:S(2)}, u32[]{:S(2)}) %collective-permute-start.4) | collective-permute-done | bytes 589856 | tf_op jit(solution)/shard_map/ppermute | solution.py:549
  23.9 0.1 chip_sum.1
  24.1 22.3 %all_to_all.10.come_ref = bf16[16,144,128]{2,1,0:T(8,128)(2,1)S(1)} all-to-all(bf16[16,144,128]{2,1,0:T(8,128)(2,1)S(1)} %bitcast.24), channel_id=1, replica_groups=mesh['z'=16,'yl'=2,'yh'=2,'x'=4,'c'=2] {'yl','yh','x'}, dimensions={0} | all-to-all | bytes 1179648 | tf_op jit(solution)/shard_map/all_to_all | solution.py:552
  46.3 0.1 middle_sum.1
  46.4 23.6 %all_to_all.11.come_ref = bf16[16,16,128]{2,1,0:T(8,128)(2,1)S(1)} all-to-all(bf16[16,16,128]{2,1,0:T(8,128)(2,1)S(1)} %middle_sum.1), channel_id=1, replica_groups=mesh['z'=16,'yl'=2,'yh'=2,'x'=4,'c'=2] {'z'}, dimensions={0} | all-to-all | bytes 131072 | tf_op jit(solution)/shard_map/all_to_all | solution.py:553
  70.1 0.8 %last_sum.1 = (bf16[8,96]{1,0:T(8,128)(2,1)}, bf16[12,32]{1,0:T(8,128)(2,1)}) custom-call(bf16[16,16,128]{2,1,0:T(8,128)(2,1)S(1)} %all_to_all.11.come_ref), custom_call_target="tpu_custom_call" | custom-call | flops 100000 | bytes 70000 | tf_op jit(solution)/shard_map/last_sum/pallas_call | solution.py:489
  (3 shorter events, 0.0 us)
Async XLA Ops:
  0.6 0.7 copy-start.4
  1.4 10.4 %collective-permute-start = (bf16[80,2176]{1,0:T(8,128)(2,1)S(1)}, bf16[80,2176]{1,0:T(8,128)(2,1)S(1)}, u32[]{:S(2)}, u32[]{:S(2)}) collective-permute-start(bf16[80,2176]{1,0:T(8,128)(2,1)S(1)} %get-tuple-element.29), channel_id=1, source_target_pairs={{1,2},{3,4},{5,6},{7,8},{9,10},{11,12},{13,14},{15,0},{17,18},{19,... | collective-permute-start | bytes 1044488 | tf_op jit(solution)/shard_map/ppermute | solution.py:504
  2.7 6.1 %copy-start.1 = (bf16[1,160,2048]{2,1,0:T(8,128)(2,1)S(1)}, bf16[1,160,2048]{2,1,0:T(8,128)(2,1)}, u32[]{:S(2)}) copy-start(bf16[1,160,2048]{2,1,0:T(8,128)(2,1)} %param.10) | copy-start | bytes 1966084
  2.7 6.1 %copy-start.2 = (bf16[1,160,2048]{2,1,0:T(8,128)(2,1)S(1)}, bf16[1,160,2048]{2,1,0:T(8,128)(2,1)}, u32[]{:S(2)}) copy-start(bf16[1,160,2048]{2,1,0:T(8,128)(2,1)} %param.11) | copy-start | bytes 1966084
  2.7 6.1 %copy-start.3 = (bf16[32,6144]{1,0:T(8,128)(2,1)S(1)}, bf16[32,6144]{1,0:T(8,128)(2,1)}, u32[]{:S(2)}) copy-start(bf16[32,6144]{1,0:T(8,128)(2,1)} %refs_6_.3) | copy-start | bytes 1179652
  2.7 6.1 %copy-start.5 = (bf16[1,160,2048]{2,1,0:T(8,128)(2,1)S(1)}, bf16[1,160,2048]{2,1,0:T(8,128)(2,1)}, u32[]{:S(2)}) copy-start(bf16[1,160,2048]{2,1,0:T(8,128)(2,1)} %param.9) | copy-start | bytes 1966084
  2.7 6.1 %copy-start.6 = (bf16[1,160,2048]{2,1,0:T(8,128)(2,1)S(1)}, bf16[1,160,2048]{2,1,0:T(8,128)(2,1)}, u32[]{:S(2)}) copy-start(bf16[1,160,2048]{2,1,0:T(8,128)(2,1)} %param.12) | copy-start | bytes 1966084
  5.1 9.0 %collective-permute-start.1 = (bf16[80,2176]{1,0:T(8,128)(2,1)S(1)}, bf16[80,2176]{1,0:T(8,128)(2,1)S(1)}, u32[]{:S(2)}, u32[]{:S(2)}) collective-permute-start(bf16[80,2176]{1,0:T(8,128)(2,1)S(1)} %get-tuple-element.36), channel_id=1, source_target_pairs={{0,1},{2,3},{4,5},{6,7},{8,9},{10,11},{12,13},{14,15},{16,17},{18,... | collective-permute-start | bytes 1044488 | tf_op jit(solution)/shard_map/ppermute | solution.py:506
  12.8 7.2 %collective-permute-start.3 = (f32[80,128]{1,0:T(8,128)S(1)}, f32[80,128]{1,0:T(8,128)S(1)}, u32[]{:S(2)}, u32[]{:S(2)}) collective-permute-start(f32[80,128]{1,0:T(8,128)S(1)} %get-tuple-element.50), channel_id=1, source_target_pairs={{0,15},{2,1},{4,3},{6,5},{8,7},{10,9},{12,11},{14,13},{16,31},{18,... | collective-permute-start | bytes 122888 | tf_op jit(solution)/shard_map/ppermute | solution.py:513
  14.1 3.2 %collective-permute-start.2 = (f32[80,128]{1,0:T(8,128)S(1)}, f32[80,128]{1,0:T(8,128)S(1)}, u32[]{:S(2)}, u32[]{:S(2)}) collective-permute-start(f32[80,128]{1,0:T(8,128)S(1)} %get-tuple-element.38), channel_id=1, source_target_pairs={{1,0},{3,2},{5,4},{7,6},{9,8},{11,10},{13,12},{15,14},{17,16},{19,... | collective-permute-start | bytes 122888 | tf_op jit(solution)/shard_map/ppermute | solution.py:525
  15.9 1.4 %copy-start = (bf16[1,160,4096]{2,1,0:T(8,128)(2,1)S(1)}, bf16[1,160,4096]{2,1,0:T(8,128)(2,1)}, u32[]{:S(2)}) copy-start(bf16[1,160,4096]{2,1,0:T(8,128)(2,1)} %param.8) | copy-start | bytes 3932164
  18.2 3.4 %collective-permute-start.5 = (bf16[2304,128]{1,0:T(8,128)(2,1)S(1)}, bf16[2304,128]{1,0:T(8,128)(2,1)S(1)}, u32[]{:S(2)}, u32[]{:S(2)}) collective-permute-start(bf16[2304,128]{1,0:T(8,128)(2,1)S(1)} %get-tuple-element.53), channel_id=1, source_target_pairs={{0,1},{2,3},{4,5},{6,7},{8,9},{10,11},{12,13},{14,15},{16,17},{18,... | collective-permute-start | bytes 1769480 | tf_op jit(solution)/shard_map/ppermute | solution.py:541
  20.0 3.9 %collective-permute-start.4 = (bf16[2304,128]{1,0:T(8,128)(2,1)S(1)}, bf16[2304,128]{1,0:T(8,128)(2,1)S(1)}, u32[]{:S(2)}, u32[]{:S(2)}) collective-permute-start(bf16[2304,128]{1,0:T(8,128)(2,1)S(1)} %get-tuple-element.51), channel_id=1, source_target_pairs={{1,0},{3,2},{5,4},{7,6},{9,8},{11,10},{13,12},{15,14},{17,16},{19,... | collective-permute-start | bytes 1769480 | tf_op jit(solution)/shard_map/ppermute | solution.py:549

commit v8 on v7

--- a/solution.py
+++ b/solution.py
@@ -317,16 +317,7 @@
             sums_ref[lanes_of(order_ref, slot, block), :] = dot_first(jnp.concatenate(left, axis=0), right)
 
 
-def up_kernel(*refs):
-    source_ref, parts, half_ref, low_ref = refs[0], (refs[1:5], refs[5:9]), refs[9], refs[10]
-    out_ref, sums_ref = refs[11:]
-    order_ref = scalars(source_ref)
-    for core in range(C):
-
-        @pl.when(lax.axis_index("c") == core)
-        def _():
-            accumulate(order_ref, *parts[core], half_ref, low_ref, sums_ref)
-
+def pack(sums_ref, out_ref):
     place = lax.broadcasted_iota(jnp.int32, (8, HEAD), 1) // RANK
     upper = lax.broadcasted_iota(jnp.int32, (8, HEAD), 0) < 4
 
@@ -356,6 +347,25 @@
             out_ref[c, g, Z * 8 :, :] = jnp.concatenate(rows, axis=0).astype(BF16)
 
 
+def first_up_kernel(source_ref, *refs):
+    out_ref, sums_ref = refs[6:]
+
+    @pl.when(lax.axis_index("c") == 0)
+    def _():
+        accumulate(scalars(source_ref), *refs[:6], sums_ref)
+        pack(sums_ref, out_ref)
+
+
+def second_up_kernel(source_ref, back_ref, *refs):
+    out_ref, back_out_ref, sums_ref = refs[6:]
+
+    @pl.when(lax.axis_index("c") == 1)
+    def _():
+        accumulate(scalars(source_ref), *refs[:6], sums_ref)
+        pack(sums_ref, out_ref)
+        back_out_ref[...] = back_ref[...]
+
+
 def down_work(own, normed_ref, proj_ref, back_ref, up_ref, mine_ref, other_ref):
     total = proj_ref[...]
     total = jnp.concatenate([total[:HALF], total[HALF:] + back_ref[...]], axis=0).astype(BF16)
@@ -522,20 +532,30 @@
         3_000_000_000,
         [pltpu.VMEM(PLAIN[1].shape, F32), pltpu.VMEM(DSCORE, BF16)],
     )
-    inner_back = lax.ppermute(later[2], ring, behind[1::2])
-    up_part = work_call(
-        up_kernel,
-        "up_gradient",
-        shape((C, G, PART, HEAD)),
-        (order, plain, late, far, dquery, later[0], later[1], later[3], later[4], half, low),
+    sums = [pltpu.VMEM((3 * WIDTH, HEAD), F32)]
+    up_shape = shape((C, G, PART, HEAD))
+    second_up, inner_back = work_call(
+        second_up_kernel,
+        "second_up_gradient",
+        (up_shape, JOINT[1]),
+        (order, later[2], later[0], later[1], later[3], later[4], half, low),
         1_000_000_000,
-        [pltpu.VMEM((3 * WIDTH, HEAD), F32)],
+        sums,
+    )
+    inner_back = lax.ppermute(inner_back, ring, behind[1::2])
+    first_up = work_call(
+        first_up_kernel,
+        "first_up_gradient",
+        up_shape,
+        (order, plain, late, far, dquery, half, low),
+        1_000_000_000,
+        sums,
     )
     first, first_other, ready = work_call(
         early_down_kernel,
         "early_down_gradient",
         (PILE, PILE, shape((8, HEAD), F32)),
-        (normed, proj, inner_back, up_part),
+        (normed, proj, inner_back, first_up),
         500_000_000,
     )
     second_come = lax.ppermute(first_other, "c", [(0, 1)])
@@ -543,7 +563,7 @@
         late_down_kernel,
         "late_down_gradient",
         (PILE, PILE),
-        (ready, normed, later[5], outer_back, up_part),
+        (ready, normed, later[5], outer_back, second_up),
         500_000_000,
     )
     first_come = lax.ppermute(second_other, "c", [(1, 0)])

time: 71.1 us -> 71 us (level)
    pallas_call x9 -> x10, Pallas kernels: 6.8 us -> 6.86 us  [work_call(): call(body, name, out_shape, [VMEM] * len(inputs), flops, 6000000, scratch...]
where the time goes in v8:
time: 71 us; the launch traced here: 70.7 us
  blocking collectives  45.9 us (65%)
  starting transfers between devices  10.4 us (15%)
  Pallas kernels  10.2 us (14%)
  waiting for transfers between devices  2.61 us (4%)
  between operations  0.9 us (1%)
    all_to_all x1, blocking collectives, per_device(): line = lax.all_to_all(middle_call(plane), FAR, 0, 0)  23.6 us
    all_to_all x1, blocking collectives, per_device(): plane = lax.all_to_all(chip.reshape(G, PART, HEAD), NEAR, 0, 0)  22.3 us
    pallas_call x10, Pallas kernels, work_call(): call(body, name, out_shape, [VMEM] * len(inputs), flops, 6000000, scratch...  6.86 us
    ppermute x1, starting transfers between devices, per_device(): inner = lax.ppermute(send, ring, ahead[::2])  3.64 us
    pallas_call x2, Pallas kernels, prepare_call(): call(body, name, (shape((HALF, (2 * SHIFTED + 1) * HEAD)), shape((rows, H...  2.49 us
    ppermute x1, waiting for transfers between devices, per_device(): first_come = lax.ppermute(second_other, 'c', [(1, 0)])  2.35 us
    ppermute x1, starting transfers between devices, per_device(): second_come = lax.ppermute(first_other, 'c', [(0, 1)])  1.61 us
  transfers between devices with their start and end apart: 6, of which 2 were waited for; matrix products, arithmetic and copies ran while one was open for 0% of the time, Pallas kernels for 13%

profile of v8, /device:TPU:2, one launch (start us, length us, event | category | flops | bytes accessed | tf_op | source)
XLA Modules:
  0.0 70.7 jit_solution(3729247477227870863)
XLA Ops:
  0.6 0.0 copy-start.4
  0.6 0.6 copy-done.4
  1.3 0.1 outer_parts.1
  1.4 1.3 %collective-permute-start = (bf16[80,2176]{1,0:T(8,128)(2,1)S(1)}, bf16[80,2176]{1,0:T(8,128)(2,1)S(1)}, u32[]{:S(2)}, u32[]{:S(2)}) collective-permute-start(bf16[80,2176]{1,0:T(8,128)(2,1)S(1)} %get-tuple-element.31), channel_id=1, source_target_pairs={{1,2},{3,4},{5,6},{7,8},{9,10},{11,12},{13,14},{15,0},{17,18},{19,... | collective-permute-start | bytes 1044488 | tf_op jit(solution)/shard_map/ppermute | solution.py:514
  2.7 0.0 copy-start.1
  2.7 0.0 copy-start.2
  2.7 0.0 copy-start.3
  2.7 0.0 copy-start.5
  2.7 0.0 copy-start.6
  2.7 2.4 %inner_parts.1 = (bf16[80,2176]{1,0:T(8,128)(2,1)S(1)}, bf16[160,128]{1,0:T(8,128)(2,1)S(1)}) custom-call(bf16[80,128]{1,0:T(8,128)(2,1)S(1)} %get-tuple-element.37.tail_ref, s32[16]{0:T(128)S(1)} %copy-done.4, bf16[160,2048]{1,0:T(8,128)(2,1)} %bitcast.14, bf16[160,2048]{1,0:T(8,128)(2,1)} %bitcast.20, bf16[160,4096]{1,0:T(8,128)(2,1)} %bitcast.10, ...), custom_call_target="tpu_custom_call" | custom-call | flops 130000000 | bytes 3000000 | tf_op jit(solution)/shard_map/inner_parts/pallas_call | solution.py:453
  5.1 3.6 %collective-permute-start.1 = (bf16[80,2176]{1,0:T(8,128)(2,1)S(1)}, bf16[80,2176]{1,0:T(8,128)(2,1)S(1)}, u32[]{:S(2)}, u32[]{:S(2)}) collective-permute-start(bf16[80,2176]{1,0:T(8,128)(2,1)S(1)} %get-tuple-element.38), channel_id=1, source_target_pairs={{0,1},{2,3},{4,5},{6,7},{8,9},{10,11},{12,13},{14,15},{16,17},{18,... | collective-permute-start | bytes 1044488 | tf_op jit(solution)/shard_map/ppermute | solution.py:516
  8.8 0.0 copy-done.1
  8.8 0.0 copy-done.2
  8.8 0.0 copy-done.3
  8.8 0.0 copy-done.5
  8.8 0.0 copy-done.6
  8.8 2.9 %own_attention.1 = (bf16[80,3072]{1,0:T(8,128)(2,1)S(1)}, f32[80,128]{1,0:T(8,128)S(1)}, bf16[160,3072]{1,0:T(8,128)(2,1)S(1)}, f32[160,128]{1,0:T(8,128)S(1)}) custom-call(s32[1,16]{1,0:T(1,128)S(1)} %bitcast.25, bf16[160,2048]{1,0:T(8,128)(2,1)S(1)} %bitcast.31, bf16[160,2048]{1,0:T(8,128)(2,1)S(1)} %bitcast.15, bf16[160,2048]{1,0:T(8,128)(2,1)S(1)} %bitcast.21, ...), custom_call_target="tpu_custom_call" | custom-call | flops 2000000000 | bytes 6000000 | tf_op jit(solution)/shard_map/own_attention/pallas_call | solution.py:480
  11.8 0.0 collective-permute-done.refs_5_.refs_1_
  11.8 1.0 %joint_attention.1 = (bf16[160,3072]{1,0:T(8,128)(2,1)S(1)}, f32[80,128]{1,0:T(8,128)S(1)}, bf16[80,128]{1,0:T(8,128)(2,1)S(1)}, bf16[8,160,80]{2,1,0:T(8,128)(2,1)S(1)}) custom-call(s32[1,16]{1,0:T(1,128)S(1)} %bitcast.26, bf16[160,2048]{1,0:T(8,128)(2,1)S(1)} %bitcast.32, bf16[160,2048]{1,0:T(8,128)(2,1)S(1)} %bitcast.16, bf16[160,2048]{1,0:T(8,128)(2,1)S(1)} %bitcast.22, ...), custom_call_target="tpu_custom_call" | custom-call | flops 1000000000 | bytes 6000000 | tf_op jit(solution)/shard_map/joint_attention/pallas_call | solution.py:480
  12.8 1.3 %collective-permute-start.3 = (f32[80,128]{1,0:T(8,128)S(1)}, f32[80,128]{1,0:T(8,128)S(1)}, u32[]{:S(2)}, u32[]{:S(2)}) collective-permute-start(f32[80,128]{1,0:T(8,128)S(1)} %get-tuple-element.53), channel_id=1, source_target_pairs={{0,15},{2,1},{4,3},{6,5},{8,7},{10,9},{12,11},{14,13},{16,31},{18,... | collective-permute-start | bytes 122888 | tf_op jit(solution)/shard_map/ppermute | solution.py:523
  14.1 0.0 collective-permute-done.1.refs_5_
  14.2 1.3 %collective-permute-start.2 = (f32[80,128]{1,0:T(8,128)S(1)}, f32[80,128]{1,0:T(8,128)S(1)}, u32[]{:S(2)}, u32[]{:S(2)}) collective-permute-start(f32[80,128]{1,0:T(8,128)S(1)} %get-tuple-element.47), channel_id=1, source_target_pairs={{1,0},{3,2},{5,4},{7,6},{9,8},{11,10},{13,12},{15,14},{17,16},{19,... | collective-permute-start | bytes 122888 | tf_op jit(solution)/shard_map/ppermute | solution.py:545
  15.5 0.5 rest_attention.1
  16.0 0.0 copy-start
  16.0 1.4 %first_up_gradient.1.up_ref = bf16[2,16,144,128]{3,2,1,0:T(8,128)(2,1)S(1)} custom-call(s32[1,16]{1,0:T(1,128)S(1)} %bitcast.30, bf16[160,3072]{1,0:T(8,128)(2,1)S(1)} %get-tuple-element.48.refs_0_, bf16[160,3072]{1,0:T(8,128)(2,1)S(1)} %get-tuple-element.32.refs_3_.refs_1_, bf16[80,128]{1,0:T(8,128)(2,1)S(1)} %get-tuple-element.39.refs_8_.refs_2_, ...), custom_call_target="tpu_custom_call" | custom-call | flops 1000000000 | bytes 6000000 | tf_op jit(solution)/shard_map/first_up_gradient/pallas_call | solution.py:480
  17.4 0.0 collective-permute-done.2.back_ref
  17.5 0.0 copy-done
  17.5 0.8 %early_down_gradient.1 = (bf16[2304,128]{1,0:T(8,128)(2,1)S(1)}, bf16[2304,128]{1,0:T(8,128)(2,1)S(1)}, f32[8,128]{1,0:T(8,128)S(1)}) custom-call(bf16[160,4096]{1,0:T(8,128)(2,1)S(1)} %bitcast.11, f32[160,128]{1,0:T(8,128)S(1)} %get-tuple-element.36.proj_ref, f32[80,128]{1,0:T(8,128)S(1)} %collective-permute-done.2.back_ref, ...), custom_call_target="tpu_custom_call" | custom-call | flops 500000000 | bytes 6000000 | tf_op jit(solution)/shard_map/early_down_gradient/pallas_call | solution.py:480
  18.3 1.6 %collective-permute-start.5 = (bf16[2304,128]{1,0:T(8,128)(2,1)S(1)}, bf16[2304,128]{1,0:T(8,128)(2,1)S(1)}, u32[]{:S(2)}, u32[]{:S(2)}) collective-permute-start(bf16[2304,128]{1,0:T(8,128)(2,1)S(1)} %get-tuple-element.57), channel_id=1, source_target_pairs={{0,1},{2,3},{4,5},{6,7},{8,9},{10,11},{12,13},{14,15},{16,17},{18,... | collective-permute-start | bytes 1769480 | tf_op jit(solution)/shard_map/ppermute | solution.py:561
  19.9 0.0 collective-permute-done.3.back_ref
  19.9 1.3 %collective-permute-start.4 = (bf16[2304,128]{1,0:T(8,128)(2,1)S(1)}, bf16[2304,128]{1,0:T(8,128)(2,1)S(1)}, u32[]{:S(2)}, u32[]{:S(2)}) collective-permute-start(bf16[2304,128]{1,0:T(8,128)(2,1)S(1)} %get-tuple-element.55), channel_id=1, source_target_pairs={{1,0},{3,2},{5,4},{7,6},{9,8},{11,10},{13,12},{15,14},{17,16},{19,... | collective-permute-start | bytes 1769480 | tf_op jit(solution)/shard_map/ppermute | solution.py:569
  21.2 0.2 collective-permute-done.5.second_come_ref
  21.5 2.4 %collective-permute-done.4.first_come_ref = bf16[2304,128]{1,0:T(8,128)(2,1)S(1)} collective-permute-done((bf16[2304,128]{1,0:T(8,128)(2,1)S(1)}, bf16[2304,128]{1,0:T(8,128)(2,1)S(1)}, u32[]{:S(2)}, u32[]{:S(2)}) %collective-permute-start.4) | collective-permute-done | bytes 589856 | tf_op jit(solution)/shard_map/ppermute | solution.py:569
  23.8 0.1 chip_sum.1
  24.0 22.3 %all_to_all.10.come_ref = bf16[16,144,128]{2,1,0:T(8,128)(2,1)S(1)} all-to-all(bf16[16,144,128]{2,1,0:T(8,128)(2,1)S(1)} %bitcast.24), channel_id=1, replica_groups=mesh['z'=16,'yl'=2,'yh'=2,'x'=4,'c'=2] {'yl','yh','x'}, dimensions={0} | all-to-all | bytes 1179648 | tf_op jit(solution)/shard_map/all_to_all | solution.py:572
  46.2 0.1 middle_sum.1
  46.3 23.6 %all_to_all.11.come_ref = bf16[16,16,128]{2,1,0:T(8,128)(2,1)S(1)} all-to-all(bf16[16,16,128]{2,1,0:T(8,128)(2,1)S(1)} %middle_sum.1), channel_id=1, replica_groups=mesh['z'=16,'yl'=2,'yh'=2,'x'=4,'c'=2] {'z'}, dimensions={0} | all-to-all | bytes 131072 | tf_op jit(solution)/shard_map/all_to_all | solution.py:573
  69.9 0.8 %last_sum.1 = (bf16[8,96]{1,0:T(8,128)(2,1)}, bf16[12,32]{1,0:T(8,128)(2,1)}) custom-call(bf16[16,16,128]{2,1,0:T(8,128)(2,1)S(1)} %all_to_all.11.come_ref), custom_call_target="tpu_custom_call" | custom-call | flops 100000 | bytes 70000 | tf_op jit(solution)/shard_map/last_sum/pallas_call | solution.py:499
  (4 shorter events, 0.0 us)
Async XLA Ops:
  0.6 0.7 copy-start.4
  1.4 10.4 %collective-permute-start = (bf16[80,2176]{1,0:T(8,128)(2,1)S(1)}, bf16[80,2176]{1,0:T(8,128)(2,1)S(1)}, u32[]{:S(2)}, u32[]{:S(2)}) collective-permute-start(bf16[80,2176]{1,0:T(8,128)(2,1)S(1)} %get-tuple-element.31), channel_id=1, source_target_pairs={{1,2},{3,4},{5,6},{7,8},{9,10},{11,12},{13,14},{15,0},{17,18},{19,... | collective-permute-start | bytes 1044488 | tf_op jit(solution)/shard_map/ppermute | solution.py:514
  2.7 6.1 %copy-start.1 = (bf16[1,160,2048]{2,1,0:T(8,128)(2,1)S(1)}, bf16[1,160,2048]{2,1,0:T(8,128)(2,1)}, u32[]{:S(2)}) copy-start(bf16[1,160,2048]{2,1,0:T(8,128)(2,1)} %param.10) | copy-start | bytes 1966084
  2.7 6.1 %copy-start.2 = (bf16[1,160,2048]{2,1,0:T(8,128)(2,1)S(1)}, bf16[1,160,2048]{2,1,0:T(8,128)(2,1)}, u32[]{:S(2)}) copy-start(bf16[1,160,2048]{2,1,0:T(8,128)(2,1)} %param.11) | copy-start | bytes 1966084
  2.7 6.1 %copy-start.3 = (bf16[32,6144]{1,0:T(8,128)(2,1)S(1)}, bf16[32,6144]{1,0:T(8,128)(2,1)}, u32[]{:S(2)}) copy-start(bf16[32,6144]{1,0:T(8,128)(2,1)} %refs_6_.3) | copy-start | bytes 1179652
  2.7 6.1 %copy-start.5 = (bf16[1,160,2048]{2,1,0:T(8,128)(2,1)S(1)}, bf16[1,160,2048]{2,1,0:T(8,128)(2,1)}, u32[]{:S(2)}) copy-start(bf16[1,160,2048]{2,1,0:T(8,128)(2,1)} %param.9) | copy-start | bytes 1966084
  2.7 6.1 %copy-start.6 = (bf16[1,160,2048]{2,1,0:T(8,128)(2,1)S(1)}, bf16[1,160,2048]{2,1,0:T(8,128)(2,1)}, u32[]{:S(2)}) copy-start(bf16[1,160,2048]{2,1,0:T(8,128)(2,1)} %param.12) | copy-start | bytes 1966084
  5.1 9.0 %collective-permute-start.1 = (bf16[80,2176]{1,0:T(8,128)(2,1)S(1)}, bf16[80,2176]{1,0:T(8,128)(2,1)S(1)}, u32[]{:S(2)}, u32[]{:S(2)}) collective-permute-start(bf16[80,2176]{1,0:T(8,128)(2,1)S(1)} %get-tuple-element.38), channel_id=1, source_target_pairs={{0,1},{2,3},{4,5},{6,7},{8,9},{10,11},{12,13},{14,15},{16,17},{18,... | collective-permute-start | bytes 1044488 | tf_op jit(solution)/shard_map/ppermute | solution.py:516
  12.8 7.1 %collective-permute-start.3 = (f32[80,128]{1,0:T(8,128)S(1)}, f32[80,128]{1,0:T(8,128)S(1)}, u32[]{:S(2)}, u32[]{:S(2)}) collective-permute-start(f32[80,128]{1,0:T(8,128)S(1)} %get-tuple-element.53), channel_id=1, source_target_pairs={{0,15},{2,1},{4,3},{6,5},{8,7},{10,9},{12,11},{14,13},{16,31},{18,... | collective-permute-start | bytes 122888 | tf_op jit(solution)/shard_map/ppermute | solution.py:523
  14.2 3.3 %collective-permute-start.2 = (f32[80,128]{1,0:T(8,128)S(1)}, f32[80,128]{1,0:T(8,128)S(1)}, u32[]{:S(2)}, u32[]{:S(2)}) collective-permute-start(f32[80,128]{1,0:T(8,128)S(1)} %get-tuple-element.47), channel_id=1, source_target_pairs={{1,0},{3,2},{5,4},{7,6},{9,8},{11,10},{13,12},{15,14},{17,16},{19,... | collective-permute-start | bytes 122888 | tf_op jit(solution)/shard_map/ppermute | solution.py:545
  16.0 1.5 %copy-start = (bf16[1,160,4096]{2,1,0:T(8,128)(2,1)S(1)}, bf16[1,160,4096]{2,1,0:T(8,128)(2,1)}, u32[]{:S(2)}) copy-start(bf16[1,160,4096]{2,1,0:T(8,128)(2,1)} %param.8) | copy-start | bytes 3932164
  18.3 3.2 %collective-permute-start.5 = (bf16[2304,128]{1,0:T(8,128)(2,1)S(1)}, bf16[2304,128]{1,0:T(8,128)(2,1)S(1)}, u32[]{:S(2)}, u32[]{:S(2)}) collective-permute-start(bf16[2304,128]{1,0:T(8,128)(2,1)S(1)} %get-tuple-element.57), channel_id=1, source_target_pairs={{0,1},{2,3},{4,5},{6,7},{8,9},{10,11},{12,13},{14,15},{16,17},{18,... | collective-permute-start | bytes 1769480 | tf_op jit(solution)/shard_map/ppermute | solution.py:561
  19.9 3.9 %collective-permute-start.4 = (bf16[2304,128]{1,0:T(8,128)(2,1)S(1)}, bf16[2304,128]{1,0:T(8,128)(2,1)S(1)}, u32[]{:S(2)}, u32[]{:S(2)}) collective-permute-start(bf16[2304,128]{1,0:T(8,128)(2,1)S(1)} %get-tuple-element.55), channel_id=1, source_target_pairs={{1,0},{3,2},{5,4},{7,6},{9,8},{11,10},{13,12},{15,14},{17,16},{19,... | collective-permute-start | bytes 1769480 | tf_op jit(solution)/shard_map/ppermute | solution.py:569

commit v9 on v6

--- a/solution.py
+++ b/solution.py
@@ -19,7 +19,7 @@
 NEAR, FAR = ("yl", "yh", "x"), ("z",)
 Z, G, C = 16, 16, 2
 BAND = Z // 4
-WIDE = 2
+WIDE = 1
 NARROW = SHIFTED * HEAD
 PART = Z * 8 + BAND * 4
 

time: 70.7 us -> 70.7 us (level)
  no operation moved by 1% of the time
where the time goes in v9:
time: 70.7 us; the launch traced here: 70.4 us
  blocking collectives  47 us (66%)
  starting transfers between devices  10.1 us (14%)
  Pallas kernels  10 us (14%)
  waiting for transfers between devices  1.62 us (2%)
  between operations  0.87 us (1%)
    all_to_all x1, blocking collectives, per_device(): plane = lax.all_to_all(chip.reshape(G, PART, HEAD), NEAR, 0, 0)  23.7 us
    all_to_all x1, blocking collectives, per_device(): line = lax.all_to_all(middle_call(plane), FAR, 0, 0)  23.3 us
    pallas_call x5, Pallas kernels, work_call(): call(body, name, out_shape, [VMEM] * len(inputs), flops, 6000000, scratch...  5.87 us
    ppermute x1, starting transfers between devices, per_device(): inner = lax.ppermute(send, ring, ahead[::2])  3.64 us
    ppermute x1, starting transfers between devices, per_device(): other = lax.ppermute(other, 'c', [(0, 1), (1, 0)])  2.56 us
    pallas_call x2, Pallas kernels, prepare_call(): call(body, name, (shape((HALF, (2 * SHIFTED + 1) * HEAD)), shape((rows, H...  2.47 us
    ppermute x1, waiting for transfers between devices, per_device(): other = lax.ppermute(other, 'c', [(0, 1), (1, 0)])  1.61 us
  transfers between devices with their start and end apart: 5, of which 1 were waited for; matrix products, arithmetic and copies ran while one was open for 0% of the time, Pallas kernels for 12%

profile of v9, /device:TPU:2, one launch (start us, length us, event | category | flops | bytes accessed | tf_op | source)
XLA Modules:
  0.0 70.4 jit_solution(12621470577974706668)
XLA Ops:
  0.6 0.0 copy-start.4
  0.6 0.6 copy-done.4
  1.3 1.3 %collective-permute-start = (bf16[80,2176]{1,0:T(8,128)(2,1)S(1)}, bf16[80,2176]{1,0:T(8,128)(2,1)S(1)}, u32[]{:S(2)}, u32[]{:S(2)}) collective-permute-start(bf16[80,2176]{1,0:T(8,128)(2,1)S(1)} %get-tuple-element.26), channel_id=1, source_target_pairs={{1,2},{3,4},{5,6},{7,8},{9,10},{11,12},{13,14},{15,0},{17,18},{19,... | collective-permute-start | bytes 1044488 | tf_op jit(solution)/shard_map/ppermute | solution.py:484
  2.6 0.0 copy-start.1
  2.7 0.0 copy-start.2
  2.7 0.0 copy-start.3
  2.7 0.0 copy-start.5
  2.7 0.0 copy-start.6
  2.7 2.4 %inner_parts.1 = (bf16[80,2176]{1,0:T(8,128)(2,1)S(1)}, bf16[160,128]{1,0:T(8,128)(2,1)S(1)}) custom-call(bf16[80,128]{1,0:T(8,128)(2,1)S(1)} %get-tuple-element.32.tail_ref, s32[16]{0:T(128)S(1)} %copy-done.4, bf16[160,2048]{1,0:T(8,128)(2,1)} %bitcast.13, bf16[160,2048]{1,0:T(8,128)(2,1)} %bitcast.19, bf16[160,4096]{1,0:T(8,128)(2,1)} %bitcast.10, ...), custom_call_target="tpu_custom_call" | custom-call | flops 130000000 | bytes 3000000 | tf_op jit(solution)/shard_map/inner_parts/pallas_call | solution.py:415
  5.1 3.6 %collective-permute-start.1 = (bf16[80,2176]{1,0:T(8,128)(2,1)S(1)}, bf16[80,2176]{1,0:T(8,128)(2,1)S(1)}, u32[]{:S(2)}, u32[]{:S(2)}) collective-permute-start(bf16[80,2176]{1,0:T(8,128)(2,1)S(1)} %get-tuple-element.33), channel_id=1, source_target_pairs={{0,1},{2,3},{4,5},{6,7},{8,9},{10,11},{12,13},{14,15},{16,17},{18,... | collective-permute-start | bytes 1044488 | tf_op jit(solution)/shard_map/ppermute | solution.py:486
  8.8 0.0 copy-done.1
  8.8 0.0 copy-done.2
  8.8 0.0 copy-done.3
  8.8 0.0 copy-done.5
  8.8 0.0 copy-done.6
  8.8 2.9 %own_attention.1 = (bf16[80,3072]{1,0:T(8,128)(2,1)S(1)}, f32[80,128]{1,0:T(8,128)S(1)}, bf16[160,3072]{1,0:T(8,128)(2,1)S(1)}, f32[160,128]{1,0:T(8,128)S(1)}) custom-call(s32[1,16]{1,0:T(1,128)S(1)} %bitcast.23, bf16[160,2048]{1,0:T(8,128)(2,1)S(1)} %bitcast.28, bf16[160,2048]{1,0:T(8,128)(2,1)S(1)} %bitcast.14, bf16[160,2048]{1,0:T(8,128)(2,1)S(1)} %bitcast.20, ...), custom_call_target="tpu_custom_call" | custom-call | flops 2000000000 | bytes 6000000 | tf_op jit(solution)/shard_map/own_attention/pallas_call | solution.py:442
  11.7 0.0 collective-permute-done.refs_5_.refs_1_
  11.7 1.0 %joint_attention.1 = (bf16[160,3072]{1,0:T(8,128)(2,1)S(1)}, f32[80,128]{1,0:T(8,128)S(1)}, bf16[80,128]{1,0:T(8,128)(2,1)S(1)}, bf16[8,160,80]{2,1,0:T(8,128)(2,1)S(1)}) custom-call(s32[1,16]{1,0:T(1,128)S(1)} %bitcast.24, bf16[160,2048]{1,0:T(8,128)(2,1)S(1)} %bitcast.29, bf16[160,2048]{1,0:T(8,128)(2,1)S(1)} %bitcast.15, bf16[160,2048]{1,0:T(8,128)(2,1)S(1)} %bitcast.21, ...), custom_call_target="tpu_custom_call" | custom-call | flops 1000000000 | bytes 6000000 | tf_op jit(solution)/shard_map/joint_attention/pallas_call | solution.py:442
  12.8 1.3 %collective-permute-start.2 = (f32[80,128]{1,0:T(8,128)S(1)}, f32[80,128]{1,0:T(8,128)S(1)}, u32[]{:S(2)}, u32[]{:S(2)}) collective-permute-start(f32[80,128]{1,0:T(8,128)S(1)} %get-tuple-element.36), channel_id=1, source_target_pairs={{0,15},{2,1},{4,3},{6,5},{8,7},{10,9},{12,11},{14,13},{16,31},{18,... | collective-permute-start | bytes 122888 | tf_op jit(solution)/shard_map/ppermute | solution.py:493
  14.1 0.0 collective-permute-done.1.refs_5_
  14.1 1.3 %collective-permute-start.3 = (f32[80,128]{1,0:T(8,128)S(1)}, f32[80,128]{1,0:T(8,128)S(1)}, u32[]{:S(2)}, u32[]{:S(2)}) collective-permute-start(f32[80,128]{1,0:T(8,128)S(1)} %get-tuple-element.37), channel_id=1, source_target_pairs={{1,0},{3,2},{5,4},{7,6},{9,8},{11,10},{13,12},{15,14},{17,16},{19,... | collective-permute-start | bytes 122888 | tf_op jit(solution)/shard_map/ppermute | solution.py:505
  15.4 0.5 rest_attention.1
  15.9 0.0 copy-start
  16.0 1.4 %up_gradient.1.up_ref = bf16[2,16,144,128]{3,2,1,0:T(8,128)(2,1)S(1)} custom-call(s32[1,16]{1,0:T(1,128)S(1)} %bitcast.27, bf16[160,3072]{1,0:T(8,128)(2,1)S(1)} %get-tuple-element.38.refs_1_, bf16[160,3072]{1,0:T(8,128)(2,1)S(1)} %get-tuple-element.27.refs_3_.refs_2_, bf16[80,128]{1,0:T(8,128)(2,1)S(1)} %get-tuple-element.34.refs_8_.refs_3_, ...), custom_call_target="tpu_custom_call" | custom-call | flops 1000000000 | bytes 6000000 | tf_op jit(solution)/shard_map/up_gradient/pallas_call | solution.py:442
  17.4 0.0 collective-permute-done.2.outer_ref
  17.4 0.0 collective-permute-done.3.inner_ref
  17.4 0.0 copy-done
  17.4 0.8 %down_gradient.1 = (bf16[2304,128]{1,0:T(8,128)(2,1)S(1)}, bf16[2304,128]{1,0:T(8,128)(2,1)S(1)}) custom-call(bf16[160,4096]{1,0:T(8,128)(2,1)S(1)} %bitcast.11, f32[160,128]{1,0:T(8,128)S(1)} %get-tuple-element.31.first_ref, f32[160,128]{1,0:T(8,128)S(1)} %get-tuple-element.35.later_ref, f32[80,128]{1,0:T(8,128)S(1)} %collective-permute-done.2.outer_ref, ...), custom_call_target="tpu_custom_call" | custom-call | flops 500000000 | bytes 4000000 | tf_op jit(solution)/shard_map/down_gradient/pallas_call | solution.py:454
  18.2 2.6 %collective-permute-start.4 = (bf16[2304,128]{1,0:T(8,128)(2,1)S(1)}, bf16[2304,128]{1,0:T(8,128)(2,1)S(1)}, u32[]{:S(2)}, u32[]{:S(2)}) collective-permute-start(bf16[2304,128]{1,0:T(8,128)(2,1)S(1)} %get-tuple-element.47), channel_id=1, source_target_pairs={{0,1},{1,0},{2,3},{3,2},{4,5},{5,4},{6,7},{7,6},{8,9},{9,8},{10,11... | collective-permute-start | bytes 1769480 | tf_op jit(solution)/shard_map/ppermute | solution.py:515
  20.8 1.6 %collective-permute-done.4 = bf16[2304,128]{1,0:T(8,128)(2,1)S(1)} collective-permute-done((bf16[2304,128]{1,0:T(8,128)(2,1)S(1)}, bf16[2304,128]{1,0:T(8,128)(2,1)S(1)}, u32[]{:S(2)}, u32[]{:S(2)}) %collective-permute-start.4) | collective-permute-done | bytes 589856 | tf_op jit(solution)/shard_map/ppermute | solution.py:515
  22.4 0.2 add_convert_fusion
  22.6 23.7 %all_to_all.10.come_ref = bf16[16,144,128]{2,1,0:T(8,128)(2,1)S(1)} all-to-all(bf16[16,144,128]{2,1,0:T(8,128)(2,1)S(1)} %bitcast.36), channel_id=1, replica_groups=mesh['z'=16,'yl'=2,'yh'=2,'x'=4,'c'=2] {'yl','yh','x'}, dimensions={0} | all-to-all | bytes 1179648 | tf_op jit(solution)/shard_map/all_to_all | solution.py:517
  46.3 0.1 middle_sum.1
  46.4 23.3 %all_to_all.11.come_ref = bf16[16,16,128]{2,1,0:T(8,128)(2,1)S(1)} all-to-all(bf16[16,16,128]{2,1,0:T(8,128)(2,1)S(1)} %middle_sum.1), channel_id=1, replica_groups=mesh['z'=16,'yl'=2,'yh'=2,'x'=4,'c'=2] {'z'}, dimensions={0} | all-to-all | bytes 131072 | tf_op jit(solution)/shard_map/all_to_all | solution.py:518
  69.6 0.8 %last_sum.1 = (bf16[8,96]{1,0:T(8,128)(2,1)}, bf16[12,32]{1,0:T(8,128)(2,1)}) custom-call(bf16[16,16,128]{2,1,0:T(8,128)(2,1)S(1)} %all_to_all.11.come_ref), custom_call_target="tpu_custom_call" | custom-call | flops 100000 | bytes 70000 | tf_op jit(solution)/shard_map/last_sum/pallas_call | solution.py:469
  (2 shorter events, 0.1 us)
Async XLA Ops:
  0.6 0.7 copy-start.4
  1.3 10.4 %collective-permute-start = (bf16[80,2176]{1,0:T(8,128)(2,1)S(1)}, bf16[80,2176]{1,0:T(8,128)(2,1)S(1)}, u32[]{:S(2)}, u32[]{:S(2)}) collective-permute-start(bf16[80,2176]{1,0:T(8,128)(2,1)S(1)} %get-tuple-element.26), channel_id=1, source_target_pairs={{1,2},{3,4},{5,6},{7,8},{9,10},{11,12},{13,14},{15,0},{17,18},{19,... | collective-permute-start | bytes 1044488 | tf_op jit(solution)/shard_map/ppermute | solution.py:484
  2.6 6.1 %copy-start.1 = (bf16[1,160,2048]{2,1,0:T(8,128)(2,1)S(1)}, bf16[1,160,2048]{2,1,0:T(8,128)(2,1)}, u32[]{:S(2)}) copy-start(bf16[1,160,2048]{2,1,0:T(8,128)(2,1)} %param.10) | copy-start | bytes 1966084
  2.7 6.1 %copy-start.2 = (bf16[1,160,2048]{2,1,0:T(8,128)(2,1)S(1)}, bf16[1,160,2048]{2,1,0:T(8,128)(2,1)}, u32[]{:S(2)}) copy-start(bf16[1,160,2048]{2,1,0:T(8,128)(2,1)} %param.11) | copy-start | bytes 1966084
  2.7 6.1 %copy-start.3 = (bf16[32,6144]{1,0:T(8,128)(2,1)S(1)}, bf16[32,6144]{1,0:T(8,128)(2,1)}, u32[]{:S(2)}) copy-start(bf16[32,6144]{1,0:T(8,128)(2,1)} %refs_6_.3) | copy-start | bytes 1179652
  2.7 6.1 %copy-start.5 = (bf16[1,160,2048]{2,1,0:T(8,128)(2,1)S(1)}, bf16[1,160,2048]{2,1,0:T(8,128)(2,1)}, u32[]{:S(2)}) copy-start(bf16[1,160,2048]{2,1,0:T(8,128)(2,1)} %param.9) | copy-start | bytes 1966084
  2.7 6.1 %copy-start.6 = (bf16[1,160,2048]{2,1,0:T(8,128)(2,1)S(1)}, bf16[1,160,2048]{2,1,0:T(8,128)(2,1)}, u32[]{:S(2)}) copy-start(bf16[1,160,2048]{2,1,0:T(8,128)(2,1)} %param.12) | copy-start | bytes 1966084
  5.1 9.0 %collective-permute-start.1 = (bf16[80,2176]{1,0:T(8,128)(2,1)S(1)}, bf16[80,2176]{1,0:T(8,128)(2,1)S(1)}, u32[]{:S(2)}, u32[]{:S(2)}) collective-permute-start(bf16[80,2176]{1,0:T(8,128)(2,1)S(1)} %get-tuple-element.33), channel_id=1, source_target_pairs={{0,1},{2,3},{4,5},{6,7},{8,9},{10,11},{12,13},{14,15},{16,17},{18,... | collective-permute-start | bytes 1044488 | tf_op jit(solution)/shard_map/ppermute | solution.py:486
  12.8 4.6 %collective-permute-start.2 = (f32[80,128]{1,0:T(8,128)S(1)}, f32[80,128]{1,0:T(8,128)S(1)}, u32[]{:S(2)}, u32[]{:S(2)}) collective-permute-start(f32[80,128]{1,0:T(8,128)S(1)} %get-tuple-element.36), channel_id=1, source_target_pairs={{0,15},{2,1},{4,3},{6,5},{8,7},{10,9},{12,11},{14,13},{16,31},{18,... | collective-permute-start | bytes 122888 | tf_op jit(solution)/shard_map/ppermute | solution.py:493
  14.1 3.2 %collective-permute-start.3 = (f32[80,128]{1,0:T(8,128)S(1)}, f32[80,128]{1,0:T(8,128)S(1)}, u32[]{:S(2)}, u32[]{:S(2)}) collective-permute-start(f32[80,128]{1,0:T(8,128)S(1)} %get-tuple-element.37), channel_id=1, source_target_pairs={{1,0},{3,2},{5,4},{7,6},{9,8},{11,10},{13,12},{15,14},{17,16},{19,... | collective-permute-start | bytes 122888 | tf_op jit(solution)/shard_map/ppermute | solution.py:505
  15.9 1.4 %copy-start = (bf16[1,160,4096]{2,1,0:T(8,128)(2,1)S(1)}, bf16[1,160,4096]{2,1,0:T(8,128)(2,1)}, u32[]{:S(2)}) copy-start(bf16[1,160,4096]{2,1,0:T(8,128)(2,1)} %param.8) | copy-start | bytes 3932164
  18.2 4.2 %collective-permute-start.4 = (bf16[2304,128]{1,0:T(8,128)(2,1)S(1)}, bf16[2304,128]{1,0:T(8,128)(2,1)S(1)}, u32[]{:S(2)}, u32[]{:S(2)}) collective-permute-start(bf16[2304,128]{1,0:T(8,128)(2,1)S(1)} %get-tuple-element.47), channel_id=1, source_target_pairs={{0,1},{1,0},{2,3},{3,2},{4,5},{5,4},{6,7},{7,6},{8,9},{9,8},{10,11... | collective-permute-start | bytes 1769480 | tf_op jit(solution)/shard_map/ppermute | solution.py:515
